TPU v7x, 512 devices: a whole 4x8x8 slice. The times are simulated.
512 devices in a mesh: grp: 8 (over y_lo, core), night: 64 (over x, y_hi, z).
Axes of the slice: x: 4, y: 8 (y_hi: 2, y_lo: 4; y = y_hi * 4 + y_lo), z: 8, core: 2. Of those that a mesh axis runs over, the one named last changes fastest.
Arguments:
- sensor_reading_array: float32 [512, 16, 65536], P('night', None, 'grp'), may hold values from -16 to 16
- starting_evening_loadings: float32 [64, 512], P(None, 'night'), may hold values from -6 to 6
- starting_span_loadings: float32 [64, 16], replicated, may hold values from -6 to 6
Outputs:
- updated_sensor_loadings: float32 [64, 65536], P(None, ('grp', 'night'))
- updated_evening_loadings: float32 [64, 512], P(None, 'night')
- updated_span_loadings: float32 [64, 16], replicated
All inputs are finite; a program needn't handle non-finite values.
Results may differ from a plain program's by a relative error of at most 0.000075.
Values sent between devices are 32-bit elements; how exact they have to be, the bound alone decides.
No kernel may reach another device: no remote copies, remote signals or barrier semaphores. Data moves between devices by JAX's collectives and lax.ppermute only.
A program may use at most 64 MiB of HBM per device.

v0:
```python
import jax
import jax.numpy as jnp
from jax import lax
from jax.sharding import PartitionSpec as P

FULL_ACCURACY = lax.Precision.HIGHEST
EPSILON_SHIFT = 1e-06


def normal_equation_answer(gram_matrix, right_side):
    factor = jnp.linalg.cholesky(gram_matrix)
    return jax.scipy.linalg.cho_solve((factor, True), right_side)


def on_device(sensor_reading_array, starting_evening_loadings, starting_span_loadings):
    rank_rows = starting_evening_loadings.shape[0]
    local_evenings, span_places, sensor_batch_lines = sensor_reading_array.shape
    unfolded_readings = sensor_reading_array.reshape(
        local_evenings * span_places, sensor_batch_lines
    )
    evening_number = lax.axis_size("night")
    local_share_part = sensor_batch_lines // evening_number
    sensor_total_lines = sensor_batch_lines * lax.axis_size("grp")
    span_inner_matrix = jnp.dot(
        starting_span_loadings, starting_span_loadings.T, precision=FULL_ACCURACY
    )
    evening_cross_matrix = lax.psum(
        jnp.dot(starting_evening_loadings, starting_evening_loadings.T, precision=FULL_ACCURACY),
        "night",
    )
    columnwise_kron = (
        starting_evening_loadings[:, :, None] * starting_span_loadings[:, None, :]
    ).reshape(rank_rows, local_evenings * span_places)
    partial_value = jnp.dot(columnwise_kron, unfolded_readings, precision=FULL_ACCURACY)
    reduced_total = lax.psum(partial_value, "night")
    unnormed_sensor_loadings = normal_equation_answer(
        evening_cross_matrix * span_inner_matrix, reduced_total
    )
    own_raw = lax.dynamic_slice_in_dim(
        unnormed_sensor_loadings, lax.axis_index("night") * local_share_part, local_share_part, 1
    )
    component_norm_sq = lax.psum(jnp.sum(own_raw * own_raw, axis=1), ("grp", "night"))
    component_norms = jnp.sqrt(component_norm_sq / sensor_total_lines + EPSILON_SHIFT)
    own_cols = own_raw / component_norms[:, None]
    sensor_inner_matrix = lax.psum(
        jnp.dot(own_cols, own_cols.T, precision=FULL_ACCURACY), ("grp", "night")
    )
    sensor_tile_lines = unnormed_sensor_loadings / component_norms[:, None]
    mode_reduced_matrix = jnp.dot(
        unfolded_readings, sensor_tile_lines.T, precision=FULL_ACCURACY
    ).reshape(local_evenings, span_places, rank_rows)
    night_part = jnp.einsum(
        "jkr,rk->rj", mode_reduced_matrix, starting_span_loadings, precision=FULL_ACCURACY
    )
    evening_mode_matrix = lax.psum(night_part, "grp")
    unnormed_evening_loadings = normal_equation_answer(
        sensor_inner_matrix * span_inner_matrix, evening_mode_matrix
    )
    night_total_rows = local_evenings * evening_number
    night_squares = lax.psum(
        jnp.sum(unnormed_evening_loadings * unnormed_evening_loadings, axis=1), "night"
    )
    night_scale = jnp.sqrt(night_squares / night_total_rows + EPSILON_SHIFT)
    updated_evening_loadings = unnormed_evening_loadings / night_scale[:, None]
    evening_inner_matrix = lax.psum(
        jnp.dot(updated_evening_loadings, updated_evening_loadings.T, precision=FULL_ACCURACY),
        "night",
    )
    interval_part = jnp.einsum(
        "jkr,rj->rk", mode_reduced_matrix, updated_evening_loadings, precision=FULL_ACCURACY
    )
    span_mode_matrix = lax.psum(interval_part, ("grp", "night"))
    unnormed_span_loadings = normal_equation_answer(
        sensor_inner_matrix * evening_inner_matrix, span_mode_matrix
    )
    interval_scale = jnp.sqrt(
        jnp.mean(unnormed_span_loadings * unnormed_span_loadings, axis=1) + EPSILON_SHIFT
    )
    updated_span_loadings = unnormed_span_loadings / interval_scale[:, None]
    return (own_cols, updated_evening_loadings, updated_span_loadings)


def solution(mesh):
    in_specs = (P("night", None, "grp"), P(None, "night"), P())
    out_specs = (P(None, ("grp", "night")), P(None, "night"), P())
    return jax.shard_map(
        on_device, mesh=mesh, in_specs=in_specs, out_specs=out_specs, check_vma=False
    )
```

profile of v0, /device:TPU:8, one launch (start us, length us, event | category | flops | bytes accessed | tf_op | source)
XLA Modules:
  0.0 1878.3 jit_solution(9424208015665163540)
XLA Ops:
  7.2 0.0 all-reduce.2.cloned.1.call-start
  7.2 0.8 copy.20
  8.0 0.8 copy.19
  8.8 0.1 broadcast_multiply_fusion
  8.9 8.9 convolution_bitcast_fusion
  17.8 0.0 all-reduce.2.cloned.1.call-update
  17.8 0.7 copy-done.3
  18.5 0.2 fusion.26
  18.7 444.1 %psum.56 = f32[64,64]{0,1:T(8,128)S(1)} all-reduce(f32[64,64]{0,1:T(8,128)S(1)} %fusion.26), channel_id=1, replica_groups=mesh['grp'=8,'night'=64] {'night'}, use_global_device_ids=true, to_apply=%region_0.0 | all-reduce | flops 4096 | bytes 32768 | tf_op jit(solution)/shard_map/psum | solution.py:27
  462.8 0.2 fusion.25
  463.1 0.1 copy.18
  463.2 5.8 cholesky.59
  469.1 0.6 compare_reduce_fusion.2
  469.7 0.7 fusion.7
  470.4 4.9 custom-call.23
  475.3 394.0 %all-reduce.2.cloned.1.call-done = f32[64,8192]{1,0:T(8,128)} async-done(((f32[64,8192]{1,0:T(8,128)}), f32[64,8192]{1,0:T(8,128)}) %all-reduce.2.cloned.1.call-update) | async-done | bytes 2097168 | tf_op jit(solution)/shard_map/psum | solution.py:35
  869.2 3.5 fusion.22
  872.7 1.9 fusion.20
  874.7 0.1 multiply_reduce_fusion.2
  874.8 96.1 %psum.58 = f32[64]{0:T(128)S(1)} all-reduce(f32[64]{0:T(128)S(1)} %multiply_reduce_fusion.2), channel_id=1, replica_groups=mesh['grp'=8,'night'=64] {'grp','night'}, use_global_device_ids=true, to_apply=%region_5.7 | all-reduce | flops 64 | bytes 512 | tf_op jit(solution)/shard_map/psum | solution.py:42
  970.9 0.1 dynamic-slice_divide_fusion
  971.0 0.0 copy-start
  971.0 6.3 fusion.2
  977.3 0.1 copy.44
  977.4 0.1 copy.36
  977.5 25.0 %psum.60 = f32[64,8]{1,0:T(8,128)S(1)} all-reduce(f32[64,8]{1,0:T(8,128)S(1)} %copy.36), channel_id=1, replica_groups=mesh['grp'=8,'night'=64] {'grp'}, use_global_device_ids=true, to_apply=%region_7.9 | all-reduce | flops 512 | bytes 4096 | tf_op jit(solution)/shard_map/psum | solution.py:55
  1002.5 0.2 fusion.27
  1002.7 96.1 %psum.59 = f32[64,64]{0,1:T(8,128)S(1)} all-reduce(f32[64,64]{0,1:T(8,128)S(1)} %fusion.27), channel_id=1, replica_groups=mesh['grp'=8,'night'=64] {'grp','night'}, use_global_device_ids=true, to_apply=%region_6.8 | all-reduce | flops 4096 | bytes 32768 | tf_op jit(solution)/shard_map/psum | solution.py:45
  1098.8 0.1 copy.23
  1098.9 5.8 cholesky.70
  1104.8 0.6 compare_reduce_fusion.1
  1105.4 0.7 fusion.8
  1106.1 4.9 custom-call.24
  1111.0 0.3 fusion.17
  1111.2 0.2 multiply_reduce_fusion.4
  1111.5 219.6 %psum.61 = f32[64]{0:T(128)S(1)} all-reduce(f32[64]{0:T(128)S(1)} %get-tuple-element.6), channel_id=1, replica_groups=mesh['grp'=8,'night'=64] {'night'}, use_global_device_ids=true, to_apply=%region_9.11 | all-reduce | flops 64 | bytes 512 | tf_op jit(solution)/shard_map/psum | solution.py:60
  1331.1 0.2 fusion.28
  1331.4 0.1 copy.43
  1331.4 94.5 %psum.63 = f32[64,16]{1,0:T(8,128)S(1)} all-reduce(f32[64,16]{1,0:T(8,128)S(1)} %copy.43), channel_id=1, replica_groups=mesh['grp'=8,'night'=64] {'grp','night'}, use_global_device_ids=true, to_apply=%region_11.13 | all-reduce | flops 1024 | bytes 8192 | tf_op jit(solution)/shard_map/psum | solution.py:72
  1426.0 432.2 %psum.62 = f32[64,64]{0,1:T(8,128)S(1)} all-reduce(f32[64,64]{0,1:T(8,128)S(1)} %fusion.28), channel_id=1, replica_groups=mesh['grp'=8,'night'=64] {'night'}, use_global_device_ids=true, to_apply=%region_10.12 | all-reduce | flops 4096 | bytes 32768 | tf_op jit(solution)/shard_map/psum | solution.py:65
  1858.2 0.1 copy.26
  1858.3 5.8 cholesky.81
  1864.2 0.6 compare_reduce_fusion
  1864.8 0.7 fusion.9
  1865.5 4.9 custom-call.25
  1870.4 0.3 fusion.12
  1870.6 0.2 multiply_reduce_fusion.3
  1870.9 0.6 broadcast_divide_fusion
  (20 shorter events, 0.2 us)
Async XLA Ops:
  7.2 862.1 %all-reduce.2.cloned.1.call-start = ((), (), s32[]{:S(2)}) async-start(), calls=%async_computation | async-start | bytes 4194304 | tf_op jit(solution)/shard_map/psum | solution.py:35
  17.8 0.7 copy-start.3
  17.8 445.1 %copy-start.1 = (f32[64,16]{0,1:T(8,128)S(1)}, f32[64,16]{0,1:T(8,128)}, u32[]{:S(2)}) copy-start(f32[64,16]{0,1:T(8,128)} %param.6) | copy-start | bytes 12292
  971.0 31.5 %copy-start = (f32[64,128]{1,0:T(8,128)}, f32[64,128]{1,0:T(8,128)S(1)}, u32[]{:S(2)}) copy-start(f32[64,128]{1,0:T(8,128)S(1)} %dynamic-slice_divide_fusion) | copy-start | bytes 98308
  1331.1 540.4 %copy-start.2 = (f32[64,8]{0,1:T(8,128)}, f32[64,8]{0,1:T(8,128)S(1)}, u32[]{:S(2)}) copy-start(f32[64,8]{0,1:T(8,128)S(1)} %broadcast_divide_fusion.1) | copy-start | bytes 6148
Sparse Core Ops, SparseCore 0:
  17.9 851.2 all-reduce.1
where the time goes:
time: 1880 us
  blocking collectives  1410 us (75%)
  waiting for transfers between devices  394 us (21%)
  other arithmetic  37.3 us (2%)
  matrix products  22.4 us (1%)
    psum x1, blocking collectives, on_device(): lax.psum(jnp.dot(starting_evening_loadings, starting_evening_loadings.T,...  444 us
    psum x1, blocking collectives, on_device(): lax.psum(jnp.dot(updated_evening_loadings, updated_evening_loadings.T, pr...  432 us
    psum x1, waiting for transfers between devices, on_device(): reduced_total = lax.psum(partial_value, 'night')  394 us
    psum x1, blocking collectives, on_device(): lax.psum(jnp.sum(unnormed_evening_loadings * unnormed_evening_loadings, a...  220 us
    psum x1, blocking collectives, on_device(): lax.psum(jnp.sum(own_raw * own_raw, axis=1), ('grp', 'night'))  96.1 us
    psum x1, blocking collectives, on_device(): lax.psum(jnp.dot(own_cols, own_cols.T, precision=FULL_ACCURACY), ('grp',...  96.1 us
    psum x1, blocking collectives, on_device(): span_mode_matrix = lax.psum(interval_part, ('grp', 'night'))  94.5 us
  transfers between devices with their start and end apart: 1, of which 1 were waited for; matrix products, arithmetic and copies ran while one was open for 1% of the time, Pallas kernels for 0%

commit v1 on v0

v1 whole, which is shorter than its diff:
```python
import jax
import jax.numpy as jnp
import numpy as np
from jax import lax
from jax.sharding import Mesh, PartitionSpec as P

FULL = lax.Precision.HIGHEST
EPS = 1e-06
GRP = ("ylo", "core")
NIGHT = ("x", "yhi", "z")
SPLIT = {"ylo": 4, "core": 2, "x": 4, "yhi": 2, "z": 8}


def spd_inverse(gram):
    factor = jnp.linalg.cholesky(gram)
    low = jax.scipy.linalg.solve_triangular(
        factor, jnp.eye(gram.shape[0], dtype=gram.dtype), lower=True
    )
    return jnp.dot(low.T, low, precision=FULL)


def exchange(blocks, axis):
    return lax.all_to_all(blocks, axis, 0, 0, tiled=True)


def exchange_sum(blocks, axis):
    return jnp.sum(exchange(blocks, axis), axis=0)


def spread(block, axis):
    size = lax.axis_size(axis)
    return exchange(jnp.broadcast_to(block, (size,) + block.shape), axis)


def on_device(readings, evenings, spans):
    rank, own_nights = evenings.shape
    nights, intervals, meters = readings.shape
    nx, nyhi, nz = (lax.axis_size(a) for a in NIGHT)
    night_devices = nx * nyhi * nz
    share = meters // night_devices
    meter_total = meters * lax.axis_size(GRP)
    night_total = nights * night_devices
    x2 = readings.reshape(nights * intervals, meters)

    gram_c = jnp.dot(spans, spans.T, precision=FULL)
    all_evenings = spread(evenings, NIGHT)
    gram_b = jnp.einsum("nrj,nsj->rs", all_evenings, all_evenings, precision=FULL)
    inverse_a = spd_inverse(gram_b * gram_c)

    kron = (evenings[:, :, None] * spans[:, None, :]).reshape(rank, nights * intervals)
    partial = jnp.dot(kron, x2, precision=FULL)
    blocks = partial.reshape(rank, nx, nyhi, nz, share).transpose(1, 3, 2, 0, 4)
    blocks = exchange_sum(blocks, "x")
    blocks = exchange_sum(blocks, "z")
    own = exchange_sum(blocks, "yhi")

    own_raw = jnp.dot(inverse_a, own, precision=FULL)
    full = spread(spread(spread(own_raw, "yhi"), "z"), "x")
    full = full.transpose(3, 0, 2, 1, 4).reshape(rank, meters)

    contracted = jnp.dot(x2, full.T, precision=FULL)
    gram_raw = jnp.dot(full, full.T, precision=FULL)
    summed = jnp.sum(spread(jnp.concatenate([contracted, gram_raw], axis=0), GRP), axis=0)
    gram_raw = summed[nights * intervals :]
    scale_a = jnp.sqrt(jnp.diagonal(gram_raw) / meter_total + EPS)
    own_cols = own_raw / scale_a[:, None]
    gram_a = gram_raw / scale_a[:, None] / scale_a[None, :]
    contracted = (summed[: nights * intervals] / scale_a[None, :]).reshape(
        nights, intervals, rank
    )

    night_products = jnp.einsum("jkr,rk->rj", contracted, spans, precision=FULL)
    night_raw = jnp.dot(spd_inverse(gram_a * gram_c), night_products, precision=FULL)
    interval_part = jnp.einsum("jkr,rj->rk", contracted, night_raw, precision=FULL)
    gathered = spread(jnp.concatenate([night_raw, interval_part], axis=1), NIGHT)
    all_nights = gathered[:, :, :nights]
    gram_raw = jnp.einsum("nrj,nsj->rs", all_nights, all_nights, precision=FULL)
    scale_b = jnp.sqrt(jnp.diagonal(gram_raw) / night_total + EPS)
    evenings_out = night_raw / scale_b[:, None]
    gram_n = gram_raw / scale_b[:, None] / scale_b[None, :]
    interval_products = jnp.sum(gathered[:, :, nights:], axis=0) / scale_b[:, None]
    spans_raw = jnp.dot(spd_inverse(gram_a * gram_n), interval_products, precision=FULL)
    scale_c = jnp.sqrt(jnp.mean(spans_raw * spans_raw, axis=1) + EPS)
    return own_cols, evenings_out, spans_raw / scale_c[:, None]


def solution(mesh):
    fine = Mesh(
        np.asarray(mesh.devices).reshape(tuple(SPLIT.values())), tuple(SPLIT)
    )
    in_specs = (P(NIGHT, None, GRP), P(None, NIGHT), P())
    out_specs = (P(None, GRP + NIGHT), P(None, NIGHT), P())
    return jax.shard_map(
        on_device, mesh=fine, in_specs=in_specs, out_specs=out_specs, check_vma=False
    )
```

time: 1880 us -> 241 us (0.13)
  the two profiles are of different devices: /device:TPU:8 before, /device:TPU:1 now
where the time goes in v1:
time: 241 us; the launch traced here: 240 us
  waiting for transfers between devices  61.4 us (25%)
  starting transfers between devices  52.6 us (22%)
  blocking collectives  47.9 us (20%)
  other arithmetic  41.6 us (17%)
  local copies, waits for them, and re-layouts  18.8 us (8%)
  matrix products  16.3 us (7%)
    all_to_all x6, waiting for transfers between devices, exchange(): return lax.all_to_all(blocks, axis, 0, 0, tiled=True)  61.4 us
    all_to_all x6, starting transfers between devices, exchange(): return lax.all_to_all(blocks, axis, 0, 0, tiled=True)  52.6 us
    all_to_all x3, blocking collectives, exchange(): return lax.all_to_all(blocks, axis, 0, 0, tiled=True)  47.9 us
    another operation x9, other arithmetic, spd_inverse(): factor = jnp.linalg.cholesky(gram)  19.6 us
    another operation x6, other arithmetic, spd_inverse(): jax.scipy.linalg.solve_triangular(factor, jnp.eye(gram.shape[0], dtype=gr...  16.6 us
    dot_general x1, matrix products, on_device(): partial = jnp.dot(kron, x2, precision=FULL)  6.32 us
    dot_general x1, local copies, waits for them, and re-layouts, on_device(): partial = jnp.dot(kron, x2, precision=FULL)  5.58 us
    dot_general x1, matrix products, on_device(): contracted = jnp.dot(x2, full.T, precision=FULL)  4.83 us
  transfers between devices with their start and end apart: 6, of which 5 were waited for; matrix products, arithmetic and copies ran while one was open for 13% of the time, Pallas kernels for 0%

profile of v1, /device:TPU:1, one launch (start us, length us, event | category | flops | bytes accessed | tf_op | source)
XLA Modules:
  0.0 239.7 jit_solution(11756241716886914141)
XLA Ops:
  0.6 0.7 broadcast_bitcast_fusion.1
  1.3 0.8 reshape.88
  2.2 19.6 %all-to-all-start = ((f32[64,1,512]{2,1,0:T(1,128)}), f32[64,1,512]{2,1,0:T(1,128)S(1)}, u32[]{:S(2)}, u32[]{:S(2)}) async-start(f32[64,1,512]{2,1,0:T(1,128)} %reshape.88), calls=%async_computation | async-start | bytes 262144 | tf_op jit(solution)/shard_map/all_to_all | solution.py:23
  21.8 5.6 %copy.91 = f32[8192,128]{1,0:T(8,128)} copy(f32[8192,128]{0,1:T(8,128)} %bitcast.91) | data formatting | bytes 8388608 | tf_op jit(solution)/shard_map/dot_general | solution.py:51
  27.4 6.3 %convolution_bitcast_fusion = f32[4,8,2,64,128]{4,3,1,2,0:T(8,128)S(1)} fusion(f32[64,128,1,1,1]{0,1,4,3,2:T(8,128)S(1)} %bitcast.99, f32[4,2,8,128,128]{4,3,2,1,0:T(8,128)} %bitcast.93), kind=kOutput, calls=%fused_computation.5 | convolution fusion | flops 805306368 | bytes 6324224 | tf_op jit(solution)/shard_map/dot_general | solution.py:51
  33.7 2.6 %copy.93 = f32[4,8,2,64,128]{4,1,2,3,0:T(8,128)} copy(f32[4,8,2,64,128]{4,3,1,2,0:T(8,128)S(1)} %convolution_bitcast_fusion) | data formatting | bytes 4194304 | tf_op jit(solution)/shard_map/transpose | solution.py:52
  36.3 3.9 %all-to-all-start.1 = ((f32[4,8,2,64,128]{4,1,2,3,0:T(8,128)}), f32[4,8,2,64,128]{4,1,2,3,0:T(8,128)S(1)}, u32[]{:S(2)}, u32[]{:S(2)}) async-start(f32[4,8,2,64,128]{4,1,2,3,0:T(8,128)} %copy.93), calls=%async_computation.1 | async-start | bytes 4194304 | tf_op jit(solution)/shard_map/all_to_all | solution.py:23
  40.9 0.9 reduce.8
  42.0 23.0 %all-to-all-done.1 = f32[4,8,2,64,128]{4,1,2,3,0:T(8,128)S(1)} async-done(((f32[4,8,2,64,128]{4,1,2,3,0:T(8,128)}), f32[4,8,2,64,128]{4,1,2,3,0:T(8,128)S(1)}, u32[]{:S(2)}, u32[]{:S(2)}) %all-to-all-start.1) | async-done | bytes 2097184 | tf_op jit(solution)/shard_map/all_to_all | solution.py:23
  65.2 1.1 copy.94
  66.3 6.4 %all-to-all-start.2 = ((f32[8,2,64,128]{3,1,2,0:T(2,128)}), f32[8,2,64,128]{3,1,2,0:T(2,128)S(1)}, u32[]{:S(2)}, u32[]{:S(2)}) async-start(f32[8,2,64,128]{3,1,2,0:T(2,128)} %copy.94), calls=%async_computation.2 | async-start | bytes 1048576 | tf_op jit(solution)/shard_map/all_to_all | solution.py:23
  72.6 0.6 fusion.6
  73.3 5.8 %cholesky.59 = f32[64,64]{1,0:T(8,128)S(1)} custom-call(f32[64,64]{1,0:T(8,128)S(1)} %fusion.23), custom_call_target="Cholesky" | custom-call | tf_op jit(solution)/shard_map/jit(cholesky)/cholesky | solution.py:15
  79.2 0.6 compare_reduce_fusion.2
  79.9 0.7 fusion.15
  80.5 4.9 %custom-call.11 = f32[1,64,64]{1,2,0:T(8,128)S(1)} custom-call(f32[1,64,64]{2,1,0:T(8,128)S(1)} %fusion.15), custom_call_target="InvertDiagBlocksLowerTriangular" | custom-call | tf_op jit(solution)/shard_map/jit(_solve_triangular)/triangular_solve | solution.py:16
  85.7 1.6 all-to-all-done.2
  87.5 0.6 copy.96
  88.1 6.4 %all-to-all-start.3 = ((f32[2,64,128]{2,1,0:T(8,128)}), f32[2,64,128]{2,1,0:T(8,128)S(1)}, u32[]{:S(2)}, u32[]{:S(2)}) async-start(f32[2,64,128]{2,1,0:T(8,128)} %copy.96), calls=%async_computation.3 | async-start | bytes 131072 | tf_op jit(solution)/shard_map/all_to_all | solution.py:23
  94.8 6.6 %all-to-all-done.3 = f32[2,64,128]{2,1,0:T(8,128)S(1)} async-done(((f32[2,64,128]{2,1,0:T(8,128)}), f32[2,64,128]{2,1,0:T(8,128)S(1)}, u32[]{:S(2)}, u32[]{:S(2)}) %all-to-all-start.3) | async-done | bytes 65568 | tf_op jit(solution)/shard_map/all_to_all | solution.py:23
  101.6 9.3 %all_to_all.45 = f32[2,64,128]{2,1,0:T(8,128)S(1)} all-to-all(f32[2,64,128]{2,1,0:T(8,128)S(1)} %broadcast_in_dim.20), channel_id=1, replica_groups=mesh['ylo'=4,'core'=2,'x'=4,'yhi'=2,'z'=8] {'yhi'}, dimensions={0} | all-to-all | bytes 131072 | tf_op jit(solution)/shard_map/all_to_all | solution.py:23
  110.9 17.1 %all_to_all.46 = f32[8,2,64,128]{3,2,1,0:T(8,128)S(1)} all-to-all(f32[8,2,64,128]{3,2,1,0:T(8,128)S(1)} %broadcast_in_dim.21), channel_id=1, replica_groups=mesh['ylo'=4,'core'=2,'x'=4,'yhi'=2,'z'=8] {'z'}, dimensions={0} | all-to-all | bytes 1048576 | tf_op jit(solution)/shard_map/all_to_all | solution.py:23
  128.3 21.6 %all_to_all.47 = f32[4,8,2,64,128]{4,3,1,2,0:T(8,128)S(1)} all-to-all(f32[4,8,2,64,128]{4,3,1,2,0:T(8,128)S(1)} %broadcast_in_dim.22), channel_id=1, replica_groups=mesh['ylo'=4,'core'=2,'x'=4,'yhi'=2,'z'=8] {'x'}, dimensions={0} | all-to-all | bytes 4194304 | tf_op jit(solution)/shard_map/all_to_all | solution.py:23
  149.9 1.2 copy.98
  151.1 1.0 copy-done
  152.1 4.8 %fusion.3 = f32[128,64]{0,1:T(8,128)S(1)} fusion(f32[128,8192]{1,0:T(8,128)S(1)} %bitcast.92, f32[8,8,64,128]{3,2,1,0:T(8,128)S(1)} %bitcast.94), kind=kOutput, calls=%fused_computation.7 | convolution fusion | flops 805306368 | bytes 6324224 | tf_op jit(solution)/shard_map/dot_general | solution.py:61
  156.9 1.8 convolution_bitcast_fusion.1
  158.7 0.8 broadcast_in_dim.40
  159.6 11.5 %all-to-all-start.7 = ((f32[8,192,64]{1,2,0:T(8,128)}), f32[8,192,64]{1,2,0:T(8,128)S(1)}, u32[]{:S(2)}, u32[]{:S(2)}) async-start(f32[8,192,64]{1,2,0:T(8,128)} %broadcast_in_dim.40), calls=%async_computation.7 | async-start | bytes 1048576 | tf_op jit(solution)/shard_map/all_to_all | solution.py:23
  171.1 14.5 %all-to-all-done.7 = f32[8,192,64]{1,2,0:T(8,128)S(1)} async-done(((f32[8,192,64]{1,2,0:T(8,128)}), f32[8,192,64]{1,2,0:T(8,128)S(1)}, u32[]{:S(2)}, u32[]{:S(2)}) %all-to-all-start.7) | async-done | bytes 393248 | tf_op jit(solution)/shard_map/all_to_all | solution.py:23
  185.7 0.8 gather_fusion
  186.8 5.8 %cholesky.70 = f32[64,64]{1,0:T(8,128)S(1)} custom-call(f32[64,64]{1,0:T(8,128)S(1)} %fusion.21), custom_call_target="Cholesky" | custom-call | tf_op jit(solution)/shard_map/jit(cholesky)/cholesky | solution.py:15
  192.6 0.6 compare_reduce_fusion.1
  193.3 0.7 fusion.16
  193.9 4.9 %custom-call.12 = f32[1,64,64]{1,2,0:T(8,128)S(1)} custom-call(f32[1,64,64]{2,1,0:T(8,128)S(1)} %fusion.16), custom_call_target="InvertDiagBlocksLowerTriangular" | custom-call | tf_op jit(solution)/shard_map/jit(_solve_triangular)/triangular_solve | solution.py:16
  199.7 1.2 reshape.90
  201.0 4.8 %all-to-all-start.8 = ((f32[64,1,1536]{2,1,0:T(1,128)}), f32[64,1,1536]{2,1,0:T(1,128)S(1)}, u32[]{:S(2)}, u32[]{:S(2)}) async-start(f32[64,1,1536]{2,1,0:T(1,128)} %reshape.90), calls=%async_computation.8 | async-start | bytes 786432 | tf_op jit(solution)/shard_map/all_to_all | solution.py:23
  205.8 0.7 broadcast_divide_fusion
  206.5 15.6 %all-to-all-done.8 = f32[64,1,1536]{2,1,0:T(1,128)S(1)} async-done(((f32[64,1,1536]{2,1,0:T(1,128)}), f32[64,1,1536]{2,1,0:T(1,128)S(1)}, u32[]{:S(2)}, u32[]{:S(2)}) %all-to-all-start.8) | async-done | bytes 393248 | tf_op jit(solution)/shard_map/all_to_all | solution.py:23
  222.1 1.6 reduce.9
  223.9 0.6 convolution_bitcast_fusion.2
  224.6 0.8 gather_fusion.1
  225.5 0.6 broadcast_divide_fusion.2
  226.3 5.8 %cholesky.81 = f32[64,64]{1,0:T(8,128)S(1)} custom-call(f32[64,64]{1,0:T(8,128)S(1)} %fusion.19), custom_call_target="Cholesky" | custom-call | tf_op jit(solution)/shard_map/jit(cholesky)/cholesky | solution.py:15
  232.2 0.6 compare_reduce_fusion
  232.8 0.7 fusion.17
  233.5 4.9 %custom-call.13 = f32[1,64,64]{1,2,0:T(8,128)S(1)} custom-call(f32[1,64,64]{2,1,0:T(8,128)S(1)} %fusion.17), custom_call_target="InvertDiagBlocksLowerTriangular" | custom-call | tf_op jit(solution)/shard_map/jit(_solve_triangular)/triangular_solve | solution.py:16
  239.1 0.6 broadcast_divide_fusion.1
  (54 shorter events, 4.8 us)
Async XLA Ops:
  2.2 34.1 %all-to-all-start = ((f32[64,1,512]{2,1,0:T(1,128)}), f32[64,1,512]{2,1,0:T(1,128)S(1)}, u32[]{:S(2)}, u32[]{:S(2)}) async-start(f32[64,1,512]{2,1,0:T(1,128)} %reshape.88), calls=%async_computation | async-start | bytes 262144 | tf_op jit(solution)/shard_map/all_to_all | solution.py:23
  21.8 5.6 %copy-start.1 = (f32[64,16]{0,1:T(8,128)S(1)}, f32[64,16]{0,1:T(8,128)}, u32[]{:S(2)}) copy-start(f32[64,16]{0,1:T(8,128)} %param.8) | copy-start | bytes 12292
  21.8 5.6 %copy-start.2 = (f32[64,8]{0,1:T(8,128)S(1)}, f32[64,8]{0,1:T(8,128)}, u32[]{:S(2)}) copy-start(f32[64,8]{0,1:T(8,128)} %param.7) | copy-start | bytes 6148
  36.3 28.7 %all-to-all-start.1 = ((f32[4,8,2,64,128]{4,1,2,3,0:T(8,128)}), f32[4,8,2,64,128]{4,1,2,3,0:T(8,128)S(1)}, u32[]{:S(2)}, u32[]{:S(2)}) async-start(f32[4,8,2,64,128]{4,1,2,3,0:T(8,128)} %copy.93), calls=%async_computation.1 | async-start | bytes 4194304 | tf_op jit(solution)/shard_map/all_to_all | solution.py:23
  66.3 21.0 %all-to-all-start.2 = ((f32[8,2,64,128]{3,1,2,0:T(2,128)}), f32[8,2,64,128]{3,1,2,0:T(2,128)S(1)}, u32[]{:S(2)}, u32[]{:S(2)}) async-start(f32[8,2,64,128]{3,1,2,0:T(2,128)} %copy.94), calls=%async_computation.2 | async-start | bytes 1048576 | tf_op jit(solution)/shard_map/all_to_all | solution.py:23
  88.1 13.3 %all-to-all-start.3 = ((f32[2,64,128]{2,1,0:T(8,128)}), f32[2,64,128]{2,1,0:T(8,128)S(1)}, u32[]{:S(2)}, u32[]{:S(2)}) async-start(f32[2,64,128]{2,1,0:T(8,128)} %copy.96), calls=%async_computation.3 | async-start | bytes 131072 | tf_op jit(solution)/shard_map/all_to_all | solution.py:23
  149.9 2.2 copy-start
  159.6 26.0 %all-to-all-start.7 = ((f32[8,192,64]{1,2,0:T(8,128)}), f32[8,192,64]{1,2,0:T(8,128)S(1)}, u32[]{:S(2)}, u32[]{:S(2)}) async-start(f32[8,192,64]{1,2,0:T(8,128)} %broadcast_in_dim.40), calls=%async_computation.7 | async-start | bytes 1048576 | tf_op jit(solution)/shard_map/all_to_all | solution.py:23
  201.0 21.2 %all-to-all-start.8 = ((f32[64,1,1536]{2,1,0:T(1,128)}), f32[64,1,1536]{2,1,0:T(1,128)S(1)}, u32[]{:S(2)}, u32[]{:S(2)}) async-start(f32[64,1,1536]{2,1,0:T(1,128)} %reshape.90), calls=%async_computation.8 | async-start | bytes 786432 | tf_op jit(solution)/shard_map/all_to_all | solution.py:23

commit v2 on v1

v2 whole, which is shorter than its diff:
```python
import functools

import jax
import jax.numpy as jnp
import numpy as np
from jax import lax
from jax.experimental import pallas as pl
from jax.experimental.pallas import tpu as pltpu
from jax.sharding import Mesh, PartitionSpec as P

FULL = lax.Precision.HIGHEST
EPS = 1e-06
GRP = ("ylo", "core")
NIGHT = ("x", "yhi", "z")
ZY = ("z", "yhi")
SPLIT = {"ylo": 4, "core": 2, "x": 4, "yhi": 2, "z": 8}
VMEM = pl.BlockSpec(memory_space=pltpu.VMEM)
PARAMS = pltpu.CompilerParams(vmem_limit_bytes=40 * 1024 * 1024)


def f32(*shape):
    return jax.ShapeDtypeStruct(shape, jnp.float32)


def call(body, outs, *operands):
    return pl.pallas_call(
        body,
        out_shape=outs,
        in_specs=[VMEM] * len(operands),
        out_specs=jax.tree.map(lambda _: VMEM, outs),
        compiler_params=PARAMS,
    )(*operands)


def block_order(nx, nyhi, nz):
    return [
        ((x * nyhi + y) * nz + z, (x * nz + z) * nyhi + y)
        for x in range(nx)
        for y in range(nyhi)
        for z in range(nz)
    ]


def partial_body(order, nz, kron_ref, x_ref, out_ref):
    share = out_ref.shape[-1]
    for first in range(0, len(order), nz):
        columns = pl.ds(first * share, nz * share)
        product = jnp.dot(
            kron_ref[...], x_ref[:, columns], precision=FULL,
            preferred_element_type=jnp.float32,
        )
        for i in range(nz):
            out_ref[order[first + i][1]] = product[:, i * share : (i + 1) * share]


def contract_body(order, nz, copies, x_ref, a_ref, out_ref):
    rank, share = a_ref.shape[1:]
    rows = x_ref.shape[0]
    total = jnp.zeros((rows + rank, rank), jnp.float32)
    for first in range(0, len(order), nz):
        loadings = jnp.concatenate(
            [a_ref[order[first + i][1]] for i in range(nz)], axis=1
        )
        left = jnp.concatenate(
            [x_ref[:, pl.ds(first * share, nz * share)], loadings], axis=0
        )
        total += lax.dot_general(
            left, loadings, (((1,), (1,)), ((), ())), precision=FULL,
            preferred_element_type=jnp.float32,
        )
    half, quarter = rows // 2, rank // 2
    packed = jnp.concatenate(
        [
            jnp.concatenate([total[:half], total[half:rows]], axis=1),
            jnp.concatenate([total[rows : rows + quarter], total[rows + quarter :]], axis=1),
        ],
        axis=0,
    )
    for i in range(copies):
        out_ref[i] = packed


def right_divide(gram, right):
    size = gram.shape[0]
    work = jnp.concatenate([gram, right], axis=0)
    lane = lax.broadcasted_iota(jnp.int32, (1, size), 1)
    for p in range(size):
        at = p % 8
        row = work[at : at + 1, :]
        here = lane == p
        factor = jnp.where(here, -1.0, row) / row[:, p : p + 1]
        work = jnp.where(here, 0.0, work) - work[:, p : p + 1] * factor
        if at == 7:
            work = work[8:]
    return work


def diagonals(gram):
    size = gram.shape[0]
    mask = lax.broadcasted_iota(jnp.int32, (size, size), 0) == lax.broadcasted_iota(
        jnp.int32, (size, size), 1
    )
    kept = jnp.where(mask, gram, 0.0)
    return jnp.sum(kept, axis=0, keepdims=True), jnp.sum(kept, axis=1, keepdims=True)


def night_body(meters, got_ref, gram_c_ref, spans_t_ref, send_ref, raw_ref, gram_ref, scale_ref):
    rank = gram_c_ref.shape[0]
    intervals = spans_t_ref.shape[0]
    got = got_ref[0]
    for i in range(1, got_ref.shape[0]):
        got += got_ref[i]
    half = got.shape[0] - rank // 2
    contracted = jnp.concatenate([got[:half, :rank], got[:half, rank:]], axis=0)
    gram = jnp.concatenate([got[half:, :rank], got[half:, rank:]], axis=0)
    along, down = diagonals(gram)
    along = jnp.sqrt(along / meters + EPS)
    down = jnp.sqrt(down / meters + EPS)
    gram = gram / down / along
    contracted = (contracted / along).reshape(-1, intervals, rank)
    products = jnp.sum(contracted * spans_t_ref[...][None], axis=1)
    raw = right_divide(gram * gram_c_ref[...], products)
    interval = contracted[0] * raw[0:1]
    for j in range(1, raw.shape[0]):
        interval += contracted[j] * raw[j : j + 1]
    packed = jnp.concatenate(
        [
            jnp.concatenate([raw, raw], axis=1),
            jnp.concatenate([interval[: intervals // 2], interval[intervals // 2 :]], axis=1),
        ],
        axis=0,
    )
    for i in range(send_ref.shape[0]):
        send_ref[i] = packed
    raw_ref[...] = raw
    gram_ref[...] = gram
    scale_ref[...] = down


def transposed(block):
    rows, columns = block.shape
    block = jnp.concatenate([block, jnp.zeros((128 - rows, columns), jnp.float32)], axis=0)
    block = jnp.concatenate([block, jnp.zeros((128, 128 - columns), jnp.float32)], axis=1)
    return block.T[:columns, :rows]


def span_body(night_total, got_ref, raw_ref, gram_ref, evenings_ref, spans_ref):
    rank = gram_ref.shape[0]
    nights = raw_ref.shape[0]
    everything = got_ref[:, :nights, :][:, :, :rank].reshape(-1, rank)
    gram = lax.dot_general(
        everything, everything, (((0,), (0,)), ((), ())), precision=FULL,
        preferred_element_type=jnp.float32,
    )
    interval = jnp.sum(got_ref[:, nights:, :], axis=0)
    along, down = diagonals(gram)
    along = jnp.sqrt(along / night_total + EPS)
    down = jnp.sqrt(down / night_total + EPS)
    gram = gram / down / along
    interval = jnp.concatenate([interval[:, :rank], interval[:, rank:]], axis=0) / along
    raw = right_divide(gram * gram_ref[...], interval)
    scale = jnp.sqrt(jnp.mean(raw * raw, axis=0, keepdims=True) + EPS)
    evenings_ref[...] = transposed(raw_ref[...] / along)
    spans_ref[...] = transposed(raw / scale)


def spd_inverse(gram):
    factor = jnp.linalg.cholesky(gram)
    low = jax.scipy.linalg.solve_triangular(
        factor, jnp.eye(gram.shape[0], dtype=gram.dtype), lower=True
    )
    return jnp.dot(low.T, low, precision=FULL)


def exchange(blocks, axis):
    return lax.all_to_all(blocks, axis, 0, 0, tiled=True)


def exchange_sum(blocks, axis):
    size = lax.axis_size(axis)
    got = exchange(blocks, axis)
    return jnp.sum(got.reshape((size, -1) + got.shape[1:]), axis=0)


def spread(block, axis):
    size = lax.axis_size(axis)
    return exchange(jnp.broadcast_to(block, (size,) + block.shape), axis)


def on_device(readings, evenings, spans):
    rank, nights = evenings.shape
    _, intervals, meters = readings.shape
    nx, nyhi, nz = (lax.axis_size(a) for a in NIGHT)
    night_devices = nx * nyhi * nz
    share = meters // night_devices
    copies = lax.axis_size(GRP)
    order = block_order(nx, nyhi, nz)
    x2 = readings.reshape(nights * intervals, meters)

    gram_c = jnp.dot(spans, spans.T, precision=FULL)
    all_evenings = spread(evenings, NIGHT)
    gram_b = jnp.einsum("nrj,nsj->rs", all_evenings, all_evenings, precision=FULL)
    inverse_a = spd_inverse(gram_b * gram_c)

    kron = (evenings[:, :, None] * spans[:, None, :]).reshape(rank, nights * intervals)
    blocks = call(
        functools.partial(partial_body, order, nz), f32(night_devices, rank, share), kron, x2
    )
    blocks = exchange_sum(blocks, "x")
    own = exchange_sum(blocks, ZY)[0]
    own_raw = jnp.dot(inverse_a, own, precision=FULL)
    full = spread(spread(own_raw, ZY), "x").reshape(night_devices, rank, share)

    packed = call(
        functools.partial(contract_body, order, nz, copies),
        f32(copies, (nights * intervals + rank) // 2, 2 * rank), x2, full,
    )
    send, raw, gram_a, scale = call(
        functools.partial(night_body, meters * copies),
        (
            f32(night_devices, nights + intervals // 2, 2 * rank),
            f32(nights, rank), f32(rank, rank), f32(rank, 1),
        ),
        exchange(packed, GRP), gram_c, spans.T,
    )
    evenings_out, spans_out = call(
        functools.partial(span_body, nights * night_devices),
        (f32(rank, nights), f32(rank, intervals)),
        exchange(send, NIGHT), raw, gram_a,
    )
    return own_raw / scale, evenings_out, spans_out


def solution(mesh):
    fine = Mesh(
        np.asarray(mesh.devices).reshape(tuple(SPLIT.values())), tuple(SPLIT)
    )
    in_specs = (P(NIGHT, None, GRP), P(None, NIGHT), P())
    out_specs = (P(None, GRP + NIGHT), P(None, NIGHT), P())
    return jax.shard_map(
        on_device, mesh=fine, in_specs=in_specs, out_specs=out_specs, check_vma=False
    )
```

time: 241 us -> 205 us (0.85)
  the two profiles are of different devices: /device:TPU:1 before, /device:TPU:8 now
where the time goes in v2:
time: 205 us; the launch traced here: 204 us
  blocking collectives  65.1 us (32%)
  waiting for transfers between devices  61.6 us (30%)
  starting transfers between devices  32.5 us (16%)
  Pallas kernels  20.8 us (10%)
  other arithmetic  15.6 us (8%)
  local copies, waits for them, and re-layouts  6.21 us (3%)
    all_to_all x3, blocking collectives, exchange(): return lax.all_to_all(blocks, axis, 0, 0, tiled=True)  65.1 us
    all_to_all x4, waiting for transfers between devices, exchange(): return lax.all_to_all(blocks, axis, 0, 0, tiled=True)  61.6 us
    all_to_all x4, starting transfers between devices, exchange(): return lax.all_to_all(blocks, axis, 0, 0, tiled=True)  32.5 us
    pallas_call x4, Pallas kernels, call(): pl.pallas_call(body, out_shape=outs, in_specs=[VMEM] * len(operands), out...  20.8 us
    another operation x3, other arithmetic, spd_inverse(): factor = jnp.linalg.cholesky(gram)  6.52 us
    another operation x2, other arithmetic, spd_inverse(): jax.scipy.linalg.solve_triangular(factor, jnp.eye(gram.shape[0], dtype=gr...  5.55 us
    unnamed x11, local copies, waits for them, and re-layouts  5.19 us
  transfers between devices with their start and end apart: 4, of which 4 were waited for; matrix products, arithmetic and copies ran while one was open for 8% of the time, Pallas kernels for 2%

profile of v2, /device:TPU:8, one launch (start us, length us, event | category | flops | bytes accessed | tf_op | source)
XLA Modules:
  0.0 204.0 jit_solution(5296919642222082765)
XLA Ops:
  0.6 0.7 broadcast_bitcast_fusion
  1.3 0.8 reshape.39
  2.2 18.1 %all-to-all-start = ((f32[64,1,512]{2,1,0:T(1,128)}), f32[64,1,512]{2,1,0:T(1,128)S(1)}, u32[]{:S(2)}, u32[]{:S(2)}) async-start(f32[64,1,512]{2,1,0:T(1,128)} %reshape.39), calls=%async_computation | async-start | bytes 262144 | tf_op jit(solution)/shard_map/all_to_all | solution.py:176
  20.3 0.7 broadcast_multiply_fusion
  21.0 0.1 copy.34.kron_ref
  21.1 0.0 copy-start
  21.1 2.2 %copy-done = f32[8,16,8192]{2,1,0:T(8,128)S(1)} copy-done((f32[8,16,8192]{2,1,0:T(8,128)S(1)}, f32[8,16,8192]{2,1,0:T(8,128)}, u32[]{:S(2)}) %copy-start) | copy-done | bytes 4194328
  23.3 3.2 %shard_map.58 = f32[64,64,128]{2,1,0:T(8,128)} custom-call(f32[64,128]{1,0:T(8,128)S(1)} %copy.34.kron_ref, f32[128,8192]{1,0:T(8,128)S(1)} %bitcast.27), custom_call_target="tpu_custom_call" | custom-call | tf_op jit(solution)/shard_map/pallas_call | solution.py:26
  26.6 0.0 copy-start.2
  26.6 9.1 %all-to-all-done = f32[64,1,512]{2,1,0:T(1,128)S(1)} async-done(((f32[64,1,512]{2,1,0:T(1,128)}), f32[64,1,512]{2,1,0:T(1,128)S(1)}, u32[]{:S(2)}, u32[]{:S(2)}) %all-to-all-start) | async-done | bytes 131104 | tf_op jit(solution)/shard_map/all_to_all | solution.py:176
  35.7 3.6 %all-to-all-start.1 = ((f32[64,64,128]{2,1,0:T(8,128)}), f32[64,64,128]{2,1,0:T(8,128)S(1)}, u32[]{:S(2)}, u32[]{:S(2)}) async-start(f32[64,64,128]{2,1,0:T(8,128)} %shard_map.58), calls=%async_computation.1 | async-start | bytes 4194304 | tf_op jit(solution)/shard_map/all_to_all | solution.py:176
  39.3 0.0 copy-done.2
  39.3 0.2 fusion.6.gram_c_ref
  39.5 0.1 copy.32
  39.6 0.5 broadcast.58
  40.1 1.0 reduce.9
  41.1 0.1 reshape.40
  41.2 0.6 fusion
  41.8 0.1 copy.33
  41.9 22.8 %all-to-all-done.1 = f32[64,64,128]{2,1,0:T(8,128)S(1)} async-done(((f32[64,64,128]{2,1,0:T(8,128)}), f32[64,64,128]{2,1,0:T(8,128)S(1)}, u32[]{:S(2)}, u32[]{:S(2)}) %all-to-all-start.1) | async-done | bytes 2097184 | tf_op jit(solution)/shard_map/all_to_all | solution.py:176
  64.7 1.0 reduce_sum.18
  65.7 3.9 %all-to-all-start.2 = ((f32[16,64,128]{2,1,0:T(8,128)}), f32[16,64,128]{2,1,0:T(8,128)S(1)}, u32[]{:S(2)}, u32[]{:S(2)}) async-start(f32[16,64,128]{2,1,0:T(8,128)} %reduce_sum.18), calls=%async_computation.2 | async-start | bytes 1048576 | tf_op jit(solution)/shard_map/all_to_all | solution.py:176
  69.6 5.8 %cholesky.17 = f32[64,64]{1,0:T(8,128)S(1)} custom-call(f32[64,64]{1,0:T(8,128)S(1)} %fusion.5), custom_call_target="Cholesky" | custom-call | tf_op jit(solution)/shard_map/jit(cholesky)/cholesky | solution.py:168
  75.4 0.6 compare_reduce_fusion
  76.1 0.7 fusion.2
  76.7 4.9 %custom-call.7 = f32[1,64,64]{1,2,0:T(8,128)S(1)} custom-call(f32[1,64,64]{2,1,0:T(8,128)S(1)} %fusion.2), custom_call_target="InvertDiagBlocksLowerTriangular" | custom-call | tf_op jit(solution)/shard_map/jit(_solve_triangular)/triangular_solve | solution.py:169
  81.6 0.2 fusion.3
  81.9 0.2 fusion.7
  82.1 7.3 %all-to-all-done.2 = f32[16,64,128]{2,1,0:T(8,128)S(1)} async-done(((f32[16,64,128]{2,1,0:T(8,128)}), f32[16,64,128]{2,1,0:T(8,128)S(1)}, u32[]{:S(2)}, u32[]{:S(2)}) %all-to-all-start.2) | async-done | bytes 524320 | tf_op jit(solution)/shard_map/all_to_all | solution.py:176
  89.5 0.2 fusion.8
  89.7 24.0 %all_to_all.35 = f32[16,64,128]{2,1,0:T(8,128)S(1)} all-to-all(f32[16,64,128]{2,1,0:T(8,128)S(1)} %broadcast_in_dim.14), channel_id=1, replica_groups=mesh['ylo'=4,'core'=2,'x'=4,'yhi'=2,'z'=8] {'z','yhi'}, dimensions={0} | all-to-all | bytes 1048576 | tf_op jit(solution)/shard_map/all_to_all | solution.py:176
  113.7 0.2 broadcast_in_dim.15
  113.9 0.0 copy-start.1
  113.9 27.2 %all_to_all.36 = f32[4,16,64,128]{3,2,1,0:T(8,128)S(1)} all-to-all(f32[4,16,64,128]{3,2,1,0:T(8,128)S(1)} %broadcast_in_dim.15), channel_id=1, replica_groups=mesh['ylo'=4,'core'=2,'x'=4,'yhi'=2,'z'=8] {'x'}, dimensions={0} | all-to-all | bytes 4194304 | tf_op jit(solution)/shard_map/all_to_all | solution.py:176
  141.2 0.0 copy-done.1
  141.2 5.2 %shard_map.59 = f32[8,96,128]{2,1,0:T(8,128)S(1)} custom-call(f32[128,8192]{1,0:T(8,128)S(1)} %bitcast.28, f32[64,64,128]{2,1,0:T(8,128)S(1)} %bitcast.29), custom_call_target="tpu_custom_call" | custom-call | tf_op jit(solution)/shard_map/pallas_call | solution.py:26
  146.4 13.8 %all_to_all.37.got_ref = f32[8,96,128]{2,1,0:T(8,128)S(1)} all-to-all(f32[8,96,128]{2,1,0:T(8,128)S(1)} %shard_map.59), channel_id=1, replica_groups=mesh['ylo'=4,'core'=2,'x'=4,'yhi'=2,'z'=8] {'ylo','core'}, dimensions={0} | all-to-all | bytes 786432 | tf_op jit(solution)/shard_map/all_to_all | solution.py:176
  160.2 6.4 %shard_map.60 = (f32[64,16,128]{2,1,0:T(8,128)}, f32[8,64]{1,0:T(8,128)S(1)}, f32[64,64]{1,0:T(8,128)S(1)}, f32[64,1]{1,0:T(8,128)S(1)}) custom-call(f32[8,96,128]{2,1,0:T(8,128)S(1)} %all_to_all.37.got_ref, f32[64,64]{1,0:T(8,128)S(1)} %fusion.6.gram_c_ref, f32[16,64]{1,0:T(8,128)S(1)} %bitcast.30), custom_call_target="tpu_custom_call" | custom-call | tf_op jit(solution)/shard_map/pallas_call | solution.py:26
  166.7 6.9 %all-to-all-start.6 = ((f32[64,16,128]{2,1,0:T(8,128)}), f32[64,16,128]{2,1,0:T(8,128)S(1)}, u32[]{:S(2)}, u32[]{:S(2)}) async-start(f32[64,16,128]{2,1,0:T(8,128)} %get-tuple-element.10), calls=%async_computation.6 | async-start | bytes 1048576 | tf_op jit(solution)/shard_map/all_to_all | solution.py:176
  173.6 0.1 reduce.8
  173.7 0.7 broadcast_divide_fusion
  174.4 22.3 %all-to-all-done.6.got_ref = f32[64,16,128]{2,1,0:T(8,128)S(1)} async-done(((f32[64,16,128]{2,1,0:T(8,128)}), f32[64,16,128]{2,1,0:T(8,128)S(1)}, u32[]{:S(2)}, u32[]{:S(2)}) %all-to-all-start.6) | async-done | bytes 524320 | tf_op jit(solution)/shard_map/all_to_all | solution.py:176
  196.7 5.9 %shard_map.61 = (f32[64,8]{1,0:T(8,128)S(1)}, f32[64,16]{1,0:T(8,128)S(1)}) custom-call(f32[64,16,128]{2,1,0:T(8,128)S(1)} %all-to-all-done.6.got_ref, f32[8,64]{1,0:T(8,128)S(1)} %get-tuple-element.11.raw_ref, f32[64,64]{1,0:T(8,128)S(1)} %get-tuple-element.12.gram_ref), custom_call_target="tpu_custom_call" | custom-call | tf_op jit(solution)/shard_map/pallas_call | solution.py:26
  202.6 0.7 copy.35
  203.3 0.7 copy.36
  (4 shorter events, 0.1 us)
Async XLA Ops:
  2.2 33.5 %all-to-all-start = ((f32[64,1,512]{2,1,0:T(1,128)}), f32[64,1,512]{2,1,0:T(1,128)S(1)}, u32[]{:S(2)}, u32[]{:S(2)}) async-start(f32[64,1,512]{2,1,0:T(1,128)} %reshape.39), calls=%async_computation | async-start | bytes 262144 | tf_op jit(solution)/shard_map/all_to_all | solution.py:176
  21.1 2.2 %copy-start = (f32[8,16,8192]{2,1,0:T(8,128)S(1)}, f32[8,16,8192]{2,1,0:T(8,128)}, u32[]{:S(2)}) copy-start(f32[8,16,8192]{2,1,0:T(8,128)} %param.3) | copy-start | bytes 12582916
  26.6 12.7 %copy-start.2 = (f32[64,16]{0,1:T(8,128)S(1)}, f32[64,16]{0,1:T(8,128)}, u32[]{:S(2)}) copy-start(f32[64,16]{0,1:T(8,128)} %param.5) | copy-start | bytes 12292
  35.7 29.0 %all-to-all-start.1 = ((f32[64,64,128]{2,1,0:T(8,128)}), f32[64,64,128]{2,1,0:T(8,128)S(1)}, u32[]{:S(2)}, u32[]{:S(2)}) async-start(f32[64,64,128]{2,1,0:T(8,128)} %shard_map.58), calls=%async_computation.1 | async-start | bytes 4194304 | tf_op jit(solution)/shard_map/all_to_all | solution.py:176
  65.7 23.7 %all-to-all-start.2 = ((f32[16,64,128]{2,1,0:T(8,128)}), f32[16,64,128]{2,1,0:T(8,128)S(1)}, u32[]{:S(2)}, u32[]{:S(2)}) async-start(f32[16,64,128]{2,1,0:T(8,128)} %reduce_sum.18), calls=%async_computation.2 | async-start | bytes 1048576 | tf_op jit(solution)/shard_map/all_to_all | solution.py:176
  113.9 27.2 %copy-start.1 = (f32[8,16,8192]{2,1,0:T(8,128)S(1)}, f32[8,16,8192]{2,1,0:T(8,128)}, u32[]{:S(2)}) copy-start(f32[8,16,8192]{2,1,0:T(8,128)} %param.3) | copy-start | bytes 12582916
  166.7 30.0 %all-to-all-start.6 = ((f32[64,16,128]{2,1,0:T(8,128)}), f32[64,16,128]{2,1,0:T(8,128)S(1)}, u32[]{:S(2)}, u32[]{:S(2)}) async-start(f32[64,16,128]{2,1,0:T(8,128)} %get-tuple-element.10), calls=%async_computation.6 | async-start | bytes 1048576 | tf_op jit(solution)/shard_map/all_to_all | solution.py:176

commit v3 on v2

--- a/solution.py
+++ b/solution.py
@@ -15,6 +15,7 @@
 ZY = ("z", "yhi")
 SPLIT = {"ylo": 4, "core": 2, "x": 4, "yhi": 2, "z": 8}
 VMEM = pl.BlockSpec(memory_space=pltpu.VMEM)
+STREAM = pltpu.CompilerParams(vmem_limit_bytes=60 * 1024 * 1024)
 PARAMS = pltpu.CompilerParams(vmem_limit_bytes=40 * 1024 * 1024)
 
 
@@ -32,52 +33,98 @@
     )(*operands)
 
 
-def block_order(nx, nyhi, nz):
-    return [
-        ((x * nyhi + y) * nz + z, (x * nz + z) * nyhi + y)
-        for x in range(nx)
-        for y in range(nyhi)
-        for z in range(nz)
-    ]
-
-
-def partial_body(order, nz, kron_ref, x_ref, out_ref):
-    share = out_ref.shape[-1]
-    for first in range(0, len(order), nz):
-        columns = pl.ds(first * share, nz * share)
+def partial_body(nyhi, nz, kron_ref, x_ref, out_ref):
+    rank, share = kron_ref.shape[0], x_ref.shape[1] // (nyhi * nz)
+    for y in range(nyhi):
         product = jnp.dot(
-            kron_ref[...], x_ref[:, columns], precision=FULL,
+            kron_ref[...], x_ref[:, y * nz * share : (y + 1) * nz * share], precision=FULL,
             preferred_element_type=jnp.float32,
         )
-        for i in range(nz):
-            out_ref[order[first + i][1]] = product[:, i * share : (i + 1) * share]
-
-
-def contract_body(order, nz, copies, x_ref, a_ref, out_ref):
+        for z in range(nz):
+            out_ref[0, z * nyhi + y] = product[:, z * share : (z + 1) * share]
+
+
+def inverse_body(gram_b_ref, gram_c_ref, out_ref):
+    gram = gram_b_ref[...] * gram_c_ref[...]
+    out_ref[...] = right_divide(gram, identity(gram.shape[0]))
+
+
+def join_body(got_ref, gram_ref, out_ref, gram_out_ref):
+    for n in range(out_ref.shape[0]):
+        block = got_ref[0, n]
+        for i in range(1, got_ref.shape[0]):
+            block += got_ref[i, n]
+        out_ref[n] = block
+    gram_out_ref[...] = gram_ref[...]
+
+
+def own_body(got_ref, gram_ref, own_ref, send_ref, gram_out_ref):
+    products = got_ref[0]
+    for i in range(1, got_ref.shape[0]):
+        products += got_ref[i]
+    own_ref[...] = products
+    for i in range(send_ref.shape[0]):
+        send_ref[i] = products
+    gram_out_ref[...] = gram_ref[...]
+
+
+def apply_body(inverse_ref, own_ref, got_ref, own_out_ref, send_ref):
+    dot = functools.partial(jnp.dot, precision=FULL, preferred_element_type=jnp.float32)
+    inverse = inverse_ref[...]
+    own_out_ref[...] = dot(inverse, own_ref[...])
+    step = min(8, got_ref.shape[0])
+    width = got_ref.shape[-1]
+    for first in range(0, got_ref.shape[0], step):
+        products = jnp.concatenate([got_ref[first + i] for i in range(step)], axis=1)
+        loadings = dot(inverse, products)
+        for i in range(step):
+            block = loadings[:, i * width : (i + 1) * width]
+            for k in range(send_ref.shape[0]):
+                send_ref[k, first + i] = block
+
+
+def identity(size):
+    return (
+        lax.broadcasted_iota(jnp.int32, (size, size), 0)
+        == lax.broadcasted_iota(jnp.int32, (size, size), 1)
+    ).astype(jnp.float32)
+
+
+def contract_body(nyhi, nz, x_ref, a_ref, out_ref, total_ref):
     rank, share = a_ref.shape[1:]
     rows = x_ref.shape[0]
-    total = jnp.zeros((rows + rank, rank), jnp.float32)
-    for first in range(0, len(order), nz):
-        loadings = jnp.concatenate(
-            [a_ref[order[first + i][1]] for i in range(nz)], axis=1
-        )
+    step = pl.program_id(0)
+
+    @pl.when(step == 0)
+    def _():
+        total_ref[...] = jnp.zeros_like(total_ref)
+
+    total = total_ref[...]
+    for y in range(nyhi):
+        loadings = jnp.concatenate([a_ref[z * nyhi + y] for z in range(nz)], axis=1)
         left = jnp.concatenate(
-            [x_ref[:, pl.ds(first * share, nz * share)], loadings], axis=0
+            [x_ref[:, y * nz * share : (y + 1) * nz * share], loadings], axis=0
         )
         total += lax.dot_general(
             left, loadings, (((1,), (1,)), ((), ())), precision=FULL,
             preferred_element_type=jnp.float32,
         )
-    half, quarter = rows // 2, rank // 2
-    packed = jnp.concatenate(
-        [
-            jnp.concatenate([total[:half], total[half:rows]], axis=1),
-            jnp.concatenate([total[rows : rows + quarter], total[rows + quarter :]], axis=1),
-        ],
-        axis=0,
-    )
-    for i in range(copies):
-        out_ref[i] = packed
+    total_ref[...] = total
+
+    @pl.when(step == pl.num_programs(0) - 1)
+    def _():
+        half, quarter = rows // 2, rank // 2
+        packed = jnp.concatenate(
+            [
+                jnp.concatenate([total[:half], total[half:rows]], axis=1),
+                jnp.concatenate(
+                    [total[rows : rows + quarter], total[rows + quarter :]], axis=1
+                ),
+            ],
+            axis=0,
+        )
+        for i in range(out_ref.shape[0]):
+            out_ref[i] = packed
 
 
 def right_divide(gram, right):
@@ -137,13 +184,6 @@
     scale_ref[...] = down
 
 
-def transposed(block):
-    rows, columns = block.shape
-    block = jnp.concatenate([block, jnp.zeros((128 - rows, columns), jnp.float32)], axis=0)
-    block = jnp.concatenate([block, jnp.zeros((128, 128 - columns), jnp.float32)], axis=1)
-    return block.T[:columns, :rows]
-
-
 def span_body(night_total, got_ref, raw_ref, gram_ref, evenings_ref, spans_ref):
     rank = gram_ref.shape[0]
     nights = raw_ref.shape[0]
@@ -160,31 +200,24 @@
     interval = jnp.concatenate([interval[:, :rank], interval[:, rank:]], axis=0) / along
     raw = right_divide(gram * gram_ref[...], interval)
     scale = jnp.sqrt(jnp.mean(raw * raw, axis=0, keepdims=True) + EPS)
-    evenings_ref[...] = transposed(raw_ref[...] / along)
-    spans_ref[...] = transposed(raw / scale)
-
-
-def spd_inverse(gram):
-    factor = jnp.linalg.cholesky(gram)
-    low = jax.scipy.linalg.solve_triangular(
-        factor, jnp.eye(gram.shape[0], dtype=gram.dtype), lower=True
-    )
-    return jnp.dot(low.T, low, precision=FULL)
+    evenings_ref[...] = raw_ref[...] / along
+    spans_ref[...] = raw / scale
 
 
 def exchange(blocks, axis):
     return lax.all_to_all(blocks, axis, 0, 0, tiled=True)
 
 
-def exchange_sum(blocks, axis):
+def paired(total, axis, step):
     size = lax.axis_size(axis)
-    got = exchange(blocks, axis)
-    return jnp.sum(got.reshape((size, -1) + got.shape[1:]), axis=0)
-
-
-def spread(block, axis):
-    size = lax.axis_size(axis)
-    return exchange(jnp.broadcast_to(block, (size,) + block.shape), axis)
+    return total + lax.ppermute(total, axis, [(i, i ^ step) for i in range(size)])
+
+
+def butterfly(total, axis, step=1):
+    while step < lax.axis_size(axis):
+        total = paired(total, axis, step)
+        step *= 2
+    return total
 
 
 def on_device(readings, evenings, spans):
@@ -194,27 +227,55 @@
     night_devices = nx * nyhi * nz
     share = meters // night_devices
     copies = lax.axis_size(GRP)
-    order = block_order(nx, nyhi, nz)
     x2 = readings.reshape(nights * intervals, meters)
-
     gram_c = jnp.dot(spans, spans.T, precision=FULL)
-    all_evenings = spread(evenings, NIGHT)
-    gram_b = jnp.einsum("nrj,nsj->rs", all_evenings, all_evenings, precision=FULL)
-    inverse_a = spd_inverse(gram_b * gram_c)
-
     kron = (evenings[:, :, None] * spans[:, None, :]).reshape(rank, nights * intervals)
-    blocks = call(
-        functools.partial(partial_body, order, nz), f32(night_devices, rank, share), kron, x2
-    )
-    blocks = exchange_sum(blocks, "x")
-    own = exchange_sum(blocks, ZY)[0]
-    own_raw = jnp.dot(inverse_a, own, precision=FULL)
-    full = spread(spread(own_raw, ZY), "x").reshape(night_devices, rank, share)
-
-    packed = call(
-        functools.partial(contract_body, order, nz, copies),
-        f32(copies, (nights * intervals + rank) // 2, 2 * rank), x2, full,
-    )
+    places = nyhi * nz
+    blocks = pl.pallas_call(
+        functools.partial(partial_body, nyhi, nz),
+        out_shape=f32(nx, places, rank, share),
+        grid=(nx,),
+        in_specs=[
+            pl.BlockSpec((rank, nights * intervals), lambda i: (0, 0)),
+            pl.BlockSpec((nights * intervals, places * share), lambda i: (0, i)),
+        ],
+        out_specs=pl.BlockSpec((1, places, rank, share), lambda i: (i, 0, 0, 0)),
+        compiler_params=STREAM,
+    )(kron, x2)
+
+    square = f32(rank, rank)
+    gram_b = jnp.dot(evenings, evenings.T, precision=FULL)
+    gram_b = butterfly(gram_b, "z")
+    joined, gram_b = call(
+        join_body, (f32(places, rank, share), square), exchange(blocks, "x"), gram_b
+    )
+    gram_b = butterfly(gram_b, "yhi")
+    gram_b = paired(gram_b, "x", 1)
+    own, send, gram_b = call(
+        own_body, (f32(rank, share), f32(places, rank, share), square),
+        exchange(joined, ZY), gram_b,
+    )
+    gram_b = butterfly(gram_b, "x", 2)
+    inverse = call(inverse_body, square, gram_b, gram_c)
+    own_raw, send = call(
+        apply_body, (f32(rank, share), f32(nx, places, rank, share)),
+        inverse, own, exchange(send, ZY),
+    )
+    full = exchange(send, "x").reshape(night_devices, rank, share)
+
+    packed_shape = (copies, (nights * intervals + rank) // 2, 2 * rank)
+    packed = pl.pallas_call(
+        functools.partial(contract_body, nyhi, nz),
+        out_shape=f32(*packed_shape),
+        grid=(nx,),
+        in_specs=[
+            pl.BlockSpec((nights * intervals, places * share), lambda i: (0, i)),
+            pl.BlockSpec((places, rank, share), lambda i: (i, 0, 0)),
+        ],
+        out_specs=pl.BlockSpec(packed_shape, lambda i: (0, 0, 0)),
+        scratch_shapes=[pltpu.VMEM((nights * intervals + rank, rank), jnp.float32)],
+        compiler_params=STREAM,
+    )(x2, full)
     send, raw, gram_a, scale = call(
         functools.partial(night_body, meters * copies),
         (
@@ -225,10 +286,10 @@
     )
     evenings_out, spans_out = call(
         functools.partial(span_body, nights * night_devices),
-        (f32(rank, nights), f32(rank, intervals)),
+        (f32(nights, rank), f32(intervals, rank)),
         exchange(send, NIGHT), raw, gram_a,
     )
-    return own_raw / scale, evenings_out, spans_out
+    return own_raw / scale, evenings_out.T, spans_out.T
 
 
 def solution(mesh):

time: 205 us -> 200 us (0.976)
  starting transfers between devices: 32.5 us -> 71.8 us
  blocking collectives: 65.1 us -> 39.7 us
  other arithmetic: 15.6 us -> 1.56 us
  Pallas kernels: 20.8 us -> 33.9 us
  waiting for transfers between devices: 61.6 us -> 49.9 us
  local copies, waits for them, and re-layouts: 6.21 us -> 0.7 us
    all_to_all x4, waiting for transfers between devices: 61.6 us -> 26.7 us  [exchange(): return lax.all_to_all(blocks, axis, 0, 0, tiled=True)]
    ppermute x0 -> x6, starting transfers between devices: none -> 32.4 us  [paired(): lax.ppermute(total, axis, [(i, i ^ step) for i in range(size)])]
    all_to_all x3 -> x2, blocking collectives: 65.1 us -> 39.7 us  [exchange(): return lax.all_to_all(blocks, axis, 0, 0, tiled=True)]
    ppermute x0 -> x6, waiting for transfers between devices: none -> 23.2 us  [paired(): lax.ppermute(total, axis, [(i, i ^ step) for i in range(size)])]
    pallas_call x0 -> x2, Pallas kernels: none -> 13.2 us  [the longest x1 7.9 us: on_device(): pl.pallas_call(functools.partial(contract_body, nyhi, nz), out_shape=f32(...]
    another operation x5 -> x0, other arithmetic: 12.1 us -> none  [the longest x3 6.52 us: spd_inverse(): factor = jnp.linalg.cholesky(gram)]
    all_to_all x4, starting transfers between devices: 32.5 us -> 39.5 us  [exchange(): return lax.all_to_all(blocks, axis, 0, 0, tiled=True)]
    unnamed x11 -> x4, local copies, waits for them, and re-layouts: 5.19 us -> 0.01 us
  transfers between devices with their start and end apart: 4 -> 10, of which waited for: 4 -> 9; matrix products, arithmetic and copies ran while one was open for 8% -> 1% of each run, Pallas kernels for 2% -> 3%
where the time goes in v3:
time: 200 us; the launch traced here: 199 us
  starting transfers between devices  71.8 us (36%)
  waiting for transfers between devices  49.9 us (25%)
  blocking collectives  39.7 us (20%)
  Pallas kernels  33.9 us (17%)
    all_to_all x2, blocking collectives, exchange(): return lax.all_to_all(blocks, axis, 0, 0, tiled=True)  39.7 us
    all_to_all x4, starting transfers between devices, exchange(): return lax.all_to_all(blocks, axis, 0, 0, tiled=True)  39.5 us
    ppermute x6, starting transfers between devices, paired(): lax.ppermute(total, axis, [(i, i ^ step) for i in range(size)])  32.4 us
    all_to_all x4, waiting for transfers between devices, exchange(): return lax.all_to_all(blocks, axis, 0, 0, tiled=True)  26.7 us
    ppermute x6, waiting for transfers between devices, paired(): lax.ppermute(total, axis, [(i, i ^ step) for i in range(size)])  23.2 us
    pallas_call x6, Pallas kernels, call(): pl.pallas_call(body, out_shape=outs, in_specs=[VMEM] * len(operands), out...  20.6 us
    pallas_call x1, Pallas kernels, on_device(): pl.pallas_call(functools.partial(contract_body, nyhi, nz), out_shape=f32(...  7.9 us
    pallas_call x1, Pallas kernels, on_device(): pl.pallas_call(functools.partial(partial_body, nyhi, nz), out_shape=f32(n...  5.33 us
  transfers between devices with their start and end apart: 10, of which 9 were waited for; matrix products, arithmetic and copies ran while one was open for 1% of the time, Pallas kernels for 3%

profile of v3, /device:TPU:8, one launch (start us, length us, event | category | flops | bytes accessed | tf_op | source)
XLA Modules:
  0.0 198.8 jit_solution(1790621497936928207)
XLA Ops:
  0.6 0.7 broadcast_multiply_fusion
  1.3 0.7 copy.8.kron_ref
  2.0 5.3 %shard_map.58 = f32[4,16,64,128]{3,2,1,0:T(8,128)} custom-call(f32[64,128]{1,0:T(8,128)} %copy.8.kron_ref, f32[128,8192]{1,0:T(8,128)} %bitcast.11), custom_call_target="tpu_custom_call" | custom-call | tf_op jit(solution)/shard_map/pallas_call | solution.py:234
  7.4 0.0 copy-start.1
  7.4 4.4 %all-to-all-start = ((f32[4,16,64,128]{3,2,1,0:T(8,128)}), f32[4,16,64,128]{3,2,1,0:T(8,128)S(1)}, u32[]{:S(2)}, u32[]{:S(2)}) async-start(f32[4,16,64,128]{3,2,1,0:T(8,128)} %shard_map.58), calls=%async_computation | async-start | bytes 4194304 | tf_op jit(solution)/shard_map/all_to_all | solution.py:208
  11.8 0.0 copy-done.1
  11.8 0.2 fusion
  12.0 4.3 %collective-permute-start = (f32[64,64]{1,0:T(8,128)S(1)}, f32[64,64]{1,0:T(8,128)S(1)}, u32[]{:S(2)}, u32[]{:S(2)}) collective-permute-start(f32[64,64]{1,0:T(8,128)S(1)} %fusion), channel_id=1, source_target_pairs={{0,1},{1,0},{2,3},{3,2},{4,5},{5,4},{6,7},{7,6},{8,9},{9,8},{10,11... | collective-permute-start | bytes 49160 | tf_op jit(solution)/shard_map/ppermute | solution.py:213
  16.3 1.9 collective-permute-done
  18.2 6.1 %collective-permute-start.1 = (f32[64,64]{1,0:T(8,128)S(1)}, f32[64,64]{1,0:T(8,128)S(1)}, u32[]{:S(2)}, u32[]{:S(2)}) collective-permute-start(f32[64,64]{1,0:T(8,128)S(1)} %add.18), channel_id=1, source_target_pairs={{0,2},{1,3},{2,0},{3,1},{4,6},{5,7},{6,4},{7,5},{8,10},{9,11},{10,... | collective-permute-start | bytes 49160 | tf_op jit(solution)/shard_map/ppermute | solution.py:213
  24.3 1.9 collective-permute-done.1
  26.2 9.3 %collective-permute-start.2 = (f32[64,64]{1,0:T(8,128)S(1)}, f32[64,64]{1,0:T(8,128)S(1)}, u32[]{:S(2)}, u32[]{:S(2)}) collective-permute-start(f32[64,64]{1,0:T(8,128)S(1)} %add.19), channel_id=1, source_target_pairs={{0,4},{1,5},{2,6},{3,7},{4,0},{5,1},{6,2},{7,3},{8,12},{9,13},{10,... | collective-permute-start | bytes 49160 | tf_op jit(solution)/shard_map/ppermute | solution.py:213
  35.5 1.9 collective-permute-done.2
  37.4 0.0 copy-start
  37.4 0.7 all-to-all-done.got_ref
  38.1 0.9 shard_map.59
  39.0 14.8 %all-to-all-start.1 = ((f32[16,64,128]{2,1,0:T(8,128)}), f32[16,64,128]{2,1,0:T(8,128)S(1)}, u32[]{:S(2)}, u32[]{:S(2)}) async-start(f32[16,64,128]{2,1,0:T(8,128)} %get-tuple-element.16), calls=%async_computation.1 | async-start | bytes 1048576 | tf_op jit(solution)/shard_map/all_to_all | solution.py:208
  53.8 7.7 %collective-permute-start.3 = (f32[64,64]{1,0:T(8,128)S(1)}, f32[64,64]{1,0:T(8,128)S(1)}, u32[]{:S(2)}, u32[]{:S(2)}) collective-permute-start(f32[64,64]{1,0:T(8,128)S(1)} %get-tuple-element.17), channel_id=1, source_target_pairs={{0,8},{8,0},{1,9},{9,1},{2,10},{10,2},{3,11},{11,3},{4,12},{12,4},... | collective-permute-start | bytes 49160 | tf_op jit(solution)/shard_map/ppermute | solution.py:213
  61.6 9.7 %collective-permute-done.3 = f32[64,64]{1,0:T(8,128)S(1)} collective-permute-done((f32[64,64]{1,0:T(8,128)S(1)}, f32[64,64]{1,0:T(8,128)S(1)}, u32[]{:S(2)}, u32[]{:S(2)}) %collective-permute-start.3) | collective-permute-done | bytes 16416 | tf_op jit(solution)/shard_map/ppermute | solution.py:213
  71.2 2.5 %collective-permute-start.4 = (f32[64,64]{1,0:T(8,128)S(1)}, f32[64,64]{1,0:T(8,128)S(1)}, u32[]{:S(2)}, u32[]{:S(2)}) collective-permute-start(f32[64,64]{1,0:T(8,128)S(1)} %add.21), channel_id=1, source_target_pairs={{0,16},{16,0},{32,48},{48,32},{1,17},{17,1},{33,49},{49,33},{2,18}... | collective-permute-start | bytes 49160 | tf_op jit(solution)/shard_map/ppermute | solution.py:213
  73.7 3.3 %collective-permute-done.4 = f32[64,64]{1,0:T(8,128)S(1)} collective-permute-done((f32[64,64]{1,0:T(8,128)S(1)}, f32[64,64]{1,0:T(8,128)S(1)}, u32[]{:S(2)}, u32[]{:S(2)}) %collective-permute-start.4) | collective-permute-done | bytes 16416 | tf_op jit(solution)/shard_map/ppermute | solution.py:213
  77.0 0.0 all-to-all-done.1.got_ref
  77.0 0.9 shard_map.60
  77.9 8.1 %all-to-all-start.2 = ((f32[16,64,128]{2,1,0:T(8,128)}), f32[16,64,128]{2,1,0:T(8,128)S(1)}, u32[]{:S(2)}, u32[]{:S(2)}) async-start(f32[16,64,128]{2,1,0:T(8,128)} %get-tuple-element.20), calls=%async_computation.2 | async-start | bytes 1048576 | tf_op jit(solution)/shard_map/all_to_all | solution.py:208
  86.1 2.5 %collective-permute-start.5 = (f32[64,64]{1,0:T(8,128)S(1)}, f32[64,64]{1,0:T(8,128)S(1)}, u32[]{:S(2)}, u32[]{:S(2)}) collective-permute-start(f32[64,64]{1,0:T(8,128)S(1)} %get-tuple-element.18), channel_id=1, source_target_pairs={{0,32},{16,48},{32,0},{48,16},{1,33},{17,49},{33,1},{49,17},{2,34}... | collective-permute-start | bytes 49160 | tf_op jit(solution)/shard_map/ppermute | solution.py:213
  88.6 0.0 copy-done
  88.6 0.2 fusion.1.gram_c_ref
  88.8 4.5 %collective-permute-done.5 = f32[64,64]{1,0:T(8,128)S(1)} collective-permute-done((f32[64,64]{1,0:T(8,128)S(1)}, f32[64,64]{1,0:T(8,128)S(1)}, u32[]{:S(2)}, u32[]{:S(2)}) %collective-permute-start.5) | collective-permute-done | bytes 16416 | tf_op jit(solution)/shard_map/ppermute | solution.py:213
  93.4 5.4 %shard_map.61.inverse_ref = f32[64,64]{1,0:T(8,128)S(1)} custom-call(f32[64,64]{1,0:T(8,128)S(1)} %add.23.gram_b_ref, f32[64,64]{1,0:T(8,128)S(1)} %fusion.1.gram_c_ref), custom_call_target="tpu_custom_call" | custom-call | tf_op jit(solution)/shard_map/pallas_call | solution.py:27
  98.7 3.6 %all-to-all-done.2.got_ref = f32[16,64,128]{2,1,0:T(8,128)S(1)} async-done(((f32[16,64,128]{2,1,0:T(8,128)}), f32[16,64,128]{2,1,0:T(8,128)S(1)}, u32[]{:S(2)}, u32[]{:S(2)}) %all-to-all-start.2) | async-done | bytes 524320 | tf_op jit(solution)/shard_map/all_to_all | solution.py:208
  102.3 0.6 shard_map.62
  103.0 25.7 %all_to_all.30 = f32[4,16,64,128]{3,2,1,0:T(8,128)} all-to-all(f32[4,16,64,128]{3,2,1,0:T(8,128)S(1)} %get-tuple-element.22), channel_id=1, replica_groups=mesh['ylo'=4,'core'=2,'x'=4,'yhi'=2,'z'=8] {'x'}, dimensions={0} | all-to-all | bytes 4194304 | tf_op jit(solution)/shard_map/all_to_all | solution.py:208
  128.7 7.9 %shard_map.63 = f32[8,96,128]{2,1,0:T(8,128)} custom-call(f32[128,8192]{1,0:T(8,128)} %bitcast.12, f32[64,64,128]{2,1,0:T(8,128)} %bitcast.13), custom_call_target="tpu_custom_call" | custom-call | tf_op jit(solution)/shard_map/pallas_call | solution.py:267
  136.6 14.0 %all_to_all.31.got_ref = f32[8,96,128]{2,1,0:T(8,128)S(1)} all-to-all(f32[8,96,128]{2,1,0:T(8,128)} %shard_map.63), channel_id=1, replica_groups=mesh['ylo'=4,'core'=2,'x'=4,'yhi'=2,'z'=8] {'ylo','core'}, dimensions={0} | all-to-all | bytes 786432 | tf_op jit(solution)/shard_map/all_to_all | solution.py:208
  150.6 6.5 %shard_map.64 = (f32[64,16,128]{2,1,0:T(8,128)}, f32[8,64]{1,0:T(8,128)S(1)}, f32[64,64]{1,0:T(8,128)S(1)}, f32[64,1]{1,0:T(8,128)S(1)}) custom-call(f32[8,96,128]{2,1,0:T(8,128)S(1)} %all_to_all.31.got_ref, f32[64,64]{1,0:T(8,128)S(1)} %fusion.1.gram_c_ref, f32[16,64]{1,0:T(8,128)S(1)} %bitcast.10), custom_call_target="tpu_custom_call" | custom-call | tf_op jit(solution)/shard_map/pallas_call | solution.py:27
  157.1 12.2 %all-to-all-start.5 = ((f32[64,16,128]{2,1,0:T(8,128)}), f32[64,16,128]{2,1,0:T(8,128)S(1)}, u32[]{:S(2)}, u32[]{:S(2)}) async-start(f32[64,16,128]{2,1,0:T(8,128)} %get-tuple-element.24), calls=%async_computation.5 | async-start | bytes 1048576 | tf_op jit(solution)/shard_map/all_to_all | solution.py:208
  169.2 0.1 reduce
  169.3 0.7 broadcast_divide_fusion
  170.0 22.3 %all-to-all-done.5.got_ref = f32[64,16,128]{2,1,0:T(8,128)S(1)} async-done(((f32[64,16,128]{2,1,0:T(8,128)}), f32[64,16,128]{2,1,0:T(8,128)S(1)}, u32[]{:S(2)}, u32[]{:S(2)}) %all-to-all-start.5) | async-done | bytes 524320 | tf_op jit(solution)/shard_map/all_to_all | solution.py:208
  192.4 6.4 %shard_map.65 = (f32[8,64]{1,0:T(8,128)}, f32[16,64]{1,0:T(8,128)}) custom-call(f32[64,16,128]{2,1,0:T(8,128)S(1)} %all-to-all-done.5.got_ref, f32[8,64]{1,0:T(8,128)S(1)} %get-tuple-element.25.raw_ref, f32[64,64]{1,0:T(8,128)S(1)} %get-tuple-element.26.gram_ref), custom_call_target="tpu_custom_call" | custom-call | tf_op jit(solution)/shard_map/pallas_call | solution.py:27
  (6 shorter events, 0.0 us)
Async XLA Ops:
  7.4 4.4 %copy-start.1 = (f32[64,8]{0,1:T(8,128)S(1)}, f32[64,8]{0,1:T(8,128)}, u32[]{:S(2)}) copy-start(f32[64,8]{0,1:T(8,128)} %param.4) | copy-start | bytes 6148
  7.4 30.8 %all-to-all-start = ((f32[4,16,64,128]{3,2,1,0:T(8,128)}), f32[4,16,64,128]{3,2,1,0:T(8,128)S(1)}, u32[]{:S(2)}, u32[]{:S(2)}) async-start(f32[4,16,64,128]{3,2,1,0:T(8,128)} %shard_map.58), calls=%async_computation | async-start | bytes 4194304 | tf_op jit(solution)/shard_map/all_to_all | solution.py:208
  12.0 6.2 %collective-permute-start = (f32[64,64]{1,0:T(8,128)S(1)}, f32[64,64]{1,0:T(8,128)S(1)}, u32[]{:S(2)}, u32[]{:S(2)}) collective-permute-start(f32[64,64]{1,0:T(8,128)S(1)} %fusion), channel_id=1, source_target_pairs={{0,1},{1,0},{2,3},{3,2},{4,5},{5,4},{6,7},{7,6},{8,9},{9,8},{10,11... | collective-permute-start | bytes 49160 | tf_op jit(solution)/shard_map/ppermute | solution.py:213
  18.2 8.0 %collective-permute-start.1 = (f32[64,64]{1,0:T(8,128)S(1)}, f32[64,64]{1,0:T(8,128)S(1)}, u32[]{:S(2)}, u32[]{:S(2)}) collective-permute-start(f32[64,64]{1,0:T(8,128)S(1)} %add.18), channel_id=1, source_target_pairs={{0,2},{1,3},{2,0},{3,1},{4,6},{5,7},{6,4},{7,5},{8,10},{9,11},{10,... | collective-permute-start | bytes 49160 | tf_op jit(solution)/shard_map/ppermute | solution.py:213
  26.2 11.2 %collective-permute-start.2 = (f32[64,64]{1,0:T(8,128)S(1)}, f32[64,64]{1,0:T(8,128)S(1)}, u32[]{:S(2)}, u32[]{:S(2)}) collective-permute-start(f32[64,64]{1,0:T(8,128)S(1)} %add.19), channel_id=1, source_target_pairs={{0,4},{1,5},{2,6},{3,7},{4,0},{5,1},{6,2},{7,3},{8,12},{9,13},{10,... | collective-permute-start | bytes 49160 | tf_op jit(solution)/shard_map/ppermute | solution.py:213
  37.4 51.2 %copy-start = (f32[64,16]{0,1:T(8,128)S(1)}, f32[64,16]{0,1:T(8,128)}, u32[]{:S(2)}) copy-start(f32[64,16]{0,1:T(8,128)} %param.5) | copy-start | bytes 12292
  39.0 38.0 %all-to-all-start.1 = ((f32[16,64,128]{2,1,0:T(8,128)}), f32[16,64,128]{2,1,0:T(8,128)S(1)}, u32[]{:S(2)}, u32[]{:S(2)}) async-start(f32[16,64,128]{2,1,0:T(8,128)} %get-tuple-element.16), calls=%async_computation.1 | async-start | bytes 1048576 | tf_op jit(solution)/shard_map/all_to_all | solution.py:208
  53.8 17.4 %collective-permute-start.3 = (f32[64,64]{1,0:T(8,128)S(1)}, f32[64,64]{1,0:T(8,128)S(1)}, u32[]{:S(2)}, u32[]{:S(2)}) collective-permute-start(f32[64,64]{1,0:T(8,128)S(1)} %get-tuple-element.17), channel_id=1, source_target_pairs={{0,8},{8,0},{1,9},{9,1},{2,10},{10,2},{3,11},{11,3},{4,12},{12,4},... | collective-permute-start | bytes 49160 | tf_op jit(solution)/shard_map/ppermute | solution.py:213
  71.2 5.8 %collective-permute-start.4 = (f32[64,64]{1,0:T(8,128)S(1)}, f32[64,64]{1,0:T(8,128)S(1)}, u32[]{:S(2)}, u32[]{:S(2)}) collective-permute-start(f32[64,64]{1,0:T(8,128)S(1)} %add.21), channel_id=1, source_target_pairs={{0,16},{16,0},{32,48},{48,32},{1,17},{17,1},{33,49},{49,33},{2,18}... | collective-permute-start | bytes 49160 | tf_op jit(solution)/shard_map/ppermute | solution.py:213
  77.9 24.4 %all-to-all-start.2 = ((f32[16,64,128]{2,1,0:T(8,128)}), f32[16,64,128]{2,1,0:T(8,128)S(1)}, u32[]{:S(2)}, u32[]{:S(2)}) async-start(f32[16,64,128]{2,1,0:T(8,128)} %get-tuple-element.20), calls=%async_computation.2 | async-start | bytes 1048576 | tf_op jit(solution)/shard_map/all_to_all | solution.py:208
  86.1 7.3 %collective-permute-start.5 = (f32[64,64]{1,0:T(8,128)S(1)}, f32[64,64]{1,0:T(8,128)S(1)}, u32[]{:S(2)}, u32[]{:S(2)}) collective-permute-start(f32[64,64]{1,0:T(8,128)S(1)} %get-tuple-element.18), channel_id=1, source_target_pairs={{0,32},{16,48},{32,0},{48,16},{1,33},{17,49},{33,1},{49,17},{2,34}... | collective-permute-start | bytes 49160 | tf_op jit(solution)/shard_map/ppermute | solution.py:213
  157.1 35.3 %all-to-all-start.5 = ((f32[64,16,128]{2,1,0:T(8,128)}), f32[64,16,128]{2,1,0:T(8,128)S(1)}, u32[]{:S(2)}, u32[]{:S(2)}) async-start(f32[64,16,128]{2,1,0:T(8,128)} %get-tuple-element.24), calls=%async_computation.5 | async-start | bytes 1048576 | tf_op jit(solution)/shard_map/all_to_all | solution.py:208

commit v4 on v3

--- a/solution.py
+++ b/solution.py
@@ -33,11 +33,20 @@
     )(*operands)
 
 
-def partial_body(nyhi, nz, kron_ref, x_ref, out_ref):
-    rank, share = kron_ref.shape[0], x_ref.shape[1] // (nyhi * nz)
+def partial_body(nyhi, nz, nights_ref, spans_ref, x_ref, out_ref):
+    rank, nights = nights_ref.shape
+    intervals = spans_ref.shape[1]
+    share = x_ref.shape[1] // (nyhi * nz)
+    kron = jnp.dot(
+        nights_ref[...], onehot(nights, nights * intervals, lambda j, c: c // intervals == j),
+        precision=FULL, preferred_element_type=jnp.float32,
+    ) * jnp.dot(
+        spans_ref[...], onehot(intervals, nights * intervals, lambda k, c: c % intervals == k),
+        precision=FULL, preferred_element_type=jnp.float32,
+    )
     for y in range(nyhi):
         product = jnp.dot(
-            kron_ref[...], x_ref[:, y * nz * share : (y + 1) * nz * share], precision=FULL,
+            kron, x_ref[:, y * nz * share : (y + 1) * nz * share], precision=FULL,
             preferred_element_type=jnp.float32,
         )
         for z in range(nz):
@@ -83,48 +92,43 @@
                 send_ref[k, first + i] = block
 
 
+def onehot(rows, columns, test):
+    return test(
+        lax.broadcasted_iota(jnp.int32, (rows, columns), 0),
+        lax.broadcasted_iota(jnp.int32, (rows, columns), 1),
+    ).astype(jnp.float32)
+
+
 def identity(size):
-    return (
-        lax.broadcasted_iota(jnp.int32, (size, size), 0)
-        == lax.broadcasted_iota(jnp.int32, (size, size), 1)
-    ).astype(jnp.float32)
-
-
-def contract_body(nyhi, nz, x_ref, a_ref, out_ref, total_ref):
+    return onehot(size, size, lambda i, j: i == j)
+
+
+def contract_body(nyhi, nz, x_ref, a_ref, out_ref):
     rank, share = a_ref.shape[1:]
     rows = x_ref.shape[0]
-    step = pl.program_id(0)
-
-    @pl.when(step == 0)
-    def _():
-        total_ref[...] = jnp.zeros_like(total_ref)
-
-    total = total_ref[...]
-    for y in range(nyhi):
-        loadings = jnp.concatenate([a_ref[z * nyhi + y] for z in range(nz)], axis=1)
+    total = jnp.zeros((rows + rank, rank), jnp.float32)
+    for group in range(a_ref.shape[0] // nz):
+        x, y = group // nyhi, group % nyhi
+        loadings = jnp.concatenate(
+            [a_ref[(x * nz + z) * nyhi + y] for z in range(nz)], axis=1
+        )
         left = jnp.concatenate(
-            [x_ref[:, y * nz * share : (y + 1) * nz * share], loadings], axis=0
+            [x_ref[:, group * nz * share : (group + 1) * nz * share], loadings], axis=0
         )
         total += lax.dot_general(
             left, loadings, (((1,), (1,)), ((), ())), precision=FULL,
             preferred_element_type=jnp.float32,
         )
-    total_ref[...] = total
-
-    @pl.when(step == pl.num_programs(0) - 1)
-    def _():
-        half, quarter = rows // 2, rank // 2
-        packed = jnp.concatenate(
-            [
-                jnp.concatenate([total[:half], total[half:rows]], axis=1),
-                jnp.concatenate(
-                    [total[rows : rows + quarter], total[rows + quarter :]], axis=1
-                ),
-            ],
-            axis=0,
-        )
-        for i in range(out_ref.shape[0]):
-            out_ref[i] = packed
+    half, quarter = rows // 2, rank // 2
+    packed = jnp.concatenate(
+        [
+            jnp.concatenate([total[:half], total[half:rows]], axis=1),
+            jnp.concatenate([total[rows : rows + quarter], total[rows + quarter :]], axis=1),
+        ],
+        axis=0,
+    )
+    for i in range(out_ref.shape[0]):
+        out_ref[i] = packed
 
 
 def right_divide(gram, right):
@@ -151,7 +155,9 @@
     return jnp.sum(kept, axis=0, keepdims=True), jnp.sum(kept, axis=1, keepdims=True)
 
 
-def night_body(meters, got_ref, gram_c_ref, spans_t_ref, send_ref, raw_ref, gram_ref, scale_ref):
+def night_body(
+    meters, got_ref, gram_c_ref, spans_t_ref, own_ref, send_ref, raw_ref, gram_ref, columns_ref
+):
     rank = gram_c_ref.shape[0]
     intervals = spans_t_ref.shape[0]
     got = got_ref[0]
@@ -181,7 +187,7 @@
         send_ref[i] = packed
     raw_ref[...] = raw
     gram_ref[...] = gram
-    scale_ref[...] = down
+    columns_ref[...] = own_ref[...] / down
 
 
 def span_body(night_total, got_ref, raw_ref, gram_ref, evenings_ref, spans_ref):
@@ -208,14 +214,11 @@
     return lax.all_to_all(blocks, axis, 0, 0, tiled=True)
 
 
-def paired(total, axis, step):
+def butterfly(total, axis):
     size = lax.axis_size(axis)
-    return total + lax.ppermute(total, axis, [(i, i ^ step) for i in range(size)])
-
-
-def butterfly(total, axis, step=1):
-    while step < lax.axis_size(axis):
-        total = paired(total, axis, step)
+    step = 1
+    while step < size:
+        total += lax.ppermute(total, axis, [(i, i ^ step) for i in range(size)])
         step *= 2
     return total
 
@@ -229,19 +232,19 @@
     copies = lax.axis_size(GRP)
     x2 = readings.reshape(nights * intervals, meters)
     gram_c = jnp.dot(spans, spans.T, precision=FULL)
-    kron = (evenings[:, :, None] * spans[:, None, :]).reshape(rank, nights * intervals)
     places = nyhi * nz
     blocks = pl.pallas_call(
         functools.partial(partial_body, nyhi, nz),
         out_shape=f32(nx, places, rank, share),
         grid=(nx,),
         in_specs=[
-            pl.BlockSpec((rank, nights * intervals), lambda i: (0, 0)),
+            pl.BlockSpec((rank, nights), lambda i: (0, 0)),
+            pl.BlockSpec((rank, intervals), lambda i: (0, 0)),
             pl.BlockSpec((nights * intervals, places * share), lambda i: (0, i)),
         ],
         out_specs=pl.BlockSpec((1, places, rank, share), lambda i: (i, 0, 0, 0)),
         compiler_params=STREAM,
-    )(kron, x2)
+    )(evenings, spans, x2)
 
     square = f32(rank, rank)
     gram_b = jnp.dot(evenings, evenings.T, precision=FULL)
@@ -250,12 +253,11 @@
         join_body, (f32(places, rank, share), square), exchange(blocks, "x"), gram_b
     )
     gram_b = butterfly(gram_b, "yhi")
-    gram_b = paired(gram_b, "x", 1)
     own, send, gram_b = call(
         own_body, (f32(rank, share), f32(places, rank, share), square),
         exchange(joined, ZY), gram_b,
     )
-    gram_b = butterfly(gram_b, "x", 2)
+    gram_b = butterfly(gram_b, "x")
     inverse = call(inverse_body, square, gram_b, gram_c)
     own_raw, send = call(
         apply_body, (f32(rank, share), f32(nx, places, rank, share)),
@@ -263,33 +265,24 @@
     )
     full = exchange(send, "x").reshape(night_devices, rank, share)
 
-    packed_shape = (copies, (nights * intervals + rank) // 2, 2 * rank)
-    packed = pl.pallas_call(
+    packed = call(
         functools.partial(contract_body, nyhi, nz),
-        out_shape=f32(*packed_shape),
-        grid=(nx,),
-        in_specs=[
-            pl.BlockSpec((nights * intervals, places * share), lambda i: (0, i)),
-            pl.BlockSpec((places, rank, share), lambda i: (i, 0, 0)),
-        ],
-        out_specs=pl.BlockSpec(packed_shape, lambda i: (0, 0, 0)),
-        scratch_shapes=[pltpu.VMEM((nights * intervals + rank, rank), jnp.float32)],
-        compiler_params=STREAM,
-    )(x2, full)
-    send, raw, gram_a, scale = call(
+        f32(copies, (nights * intervals + rank) // 2, 2 * rank), x2, full,
+    )
+    send, raw, gram_a, own_columns = call(
         functools.partial(night_body, meters * copies),
         (
             f32(night_devices, nights + intervals // 2, 2 * rank),
-            f32(nights, rank), f32(rank, rank), f32(rank, 1),
+            f32(nights, rank), square, f32(rank, share),
         ),
-        exchange(packed, GRP), gram_c, spans.T,
+        exchange(packed, GRP), gram_c, spans.T, own_raw,
     )
     evenings_out, spans_out = call(
         functools.partial(span_body, nights * night_devices),
         (f32(nights, rank), f32(intervals, rank)),
         exchange(send, NIGHT), raw, gram_a,
     )
-    return own_raw / scale, evenings_out.T, spans_out.T
+    return own_columns, evenings_out.T, spans_out.T
 
 
 def solution(mesh):

time: 200 us -> 197 us (0.985)
  blocking collectives: 39.7 us -> 76.9 us
  waiting for transfers between devices: 49.9 us -> 27.6 us
  starting transfers between devices: 71.8 us -> 56.3 us
  Pallas kernels: 33.9 us -> 31.4 us
  local copies, waits for them, and re-layouts: 0.7 us -> 2.78 us
    all_to_all x2 -> x3, blocking collectives: 39.7 us -> 76.9 us  [exchange(): return lax.all_to_all(blocks, axis, 0, 0, tiled=True)]
    all_to_all x4 -> x3, waiting for transfers between devices: 26.7 us -> 4.48 us  [exchange(): return lax.all_to_all(blocks, axis, 0, 0, tiled=True)]
    all_to_all x4 -> x3, starting transfers between devices: 39.5 us -> 24 us  [exchange(): return lax.all_to_all(blocks, axis, 0, 0, tiled=True)]
    pallas_call x1 -> x0, Pallas kernels: 7.9 us -> none  [on_device(): pl.pallas_call(functools.partial(contract_body, nyhi, nz), out_shape=f32(...]
    pallas_call x6 -> x7, Pallas kernels: 20.6 us -> 25.6 us  [call(): pl.pallas_call(body, out_shape=outs, in_specs=[VMEM] * len(operands), out...]
    unnamed x4 -> x8, local copies, waits for them, and re-layouts: 0.01 us -> 2.78 us
  transfers between devices with their start and end apart: 10 -> 9, of which waited for: 9 -> 8; matrix products, arithmetic and copies ran while one was open for 1% -> 0% of each run, Pallas kernels for 3% -> 3%
where the time goes in v4:
time: 197 us; the launch traced here: 196 us
  blocking collectives  76.9 us (39%)
  starting transfers between devices  56.3 us (29%)
  Pallas kernels  31.4 us (16%)
  waiting for transfers between devices  27.6 us (14%)
  local copies, waits for them, and re-layouts  2.78 us (1%)
    all_to_all x3, blocking collectives, exchange(): return lax.all_to_all(blocks, axis, 0, 0, tiled=True)  76.9 us
    ppermute x6, starting transfers between devices, butterfly(): total += lax.ppermute(total, axis, [(i, i ^ step) for i in range(size)])  32.4 us
    pallas_call x7, Pallas kernels, call(): pl.pallas_call(body, out_shape=outs, in_specs=[VMEM] * len(operands), out...  25.6 us
    all_to_all x3, starting transfers between devices, exchange(): return lax.all_to_all(blocks, axis, 0, 0, tiled=True)  24 us
    ppermute x6, waiting for transfers between devices, butterfly(): total += lax.ppermute(total, axis, [(i, i ^ step) for i in range(size)])  23.1 us
    pallas_call x1, Pallas kernels, on_device(): pl.pallas_call(functools.partial(partial_body, nyhi, nz), out_shape=f32(n...  5.83 us
    all_to_all x3, waiting for transfers between devices, exchange(): return lax.all_to_all(blocks, axis, 0, 0, tiled=True)  4.48 us
  transfers between devices with their start and end apart: 9, of which 8 were waited for; matrix products, arithmetic and copies ran while one was open for 0% of the time, Pallas kernels for 3%

profile of v4, /device:TPU:8, one launch (start us, length us, event | category | flops | bytes accessed | tf_op | source)
XLA Modules:
  0.0 196.3 jit_solution(4136176393726656988)
XLA Ops:
  0.6 1.4 copy.6.nights_ref
  2.0 1.4 copy.7.spans_ref
  3.4 5.8 %shard_map.58 = f32[4,16,64,128]{3,2,1,0:T(8,128)} custom-call(f32[64,8]{1,0:T(8,128)} %copy.6.nights_ref, f32[64,16]{1,0:T(8,128)} %copy.7.spans_ref, f32[128,8192]{1,0:T(8,128)} %bitcast.9), custom_call_target="tpu_custom_call" | custom-call | tf_op jit(solution)/shard_map/pallas_call | solution.py:236
  9.2 0.0 copy-start.2
  9.2 4.4 %all-to-all-start = ((f32[4,16,64,128]{3,2,1,0:T(8,128)}), f32[4,16,64,128]{3,2,1,0:T(8,128)S(1)}, u32[]{:S(2)}, u32[]{:S(2)}) async-start(f32[4,16,64,128]{3,2,1,0:T(8,128)} %shard_map.58), calls=%async_computation | async-start | bytes 4194304 | tf_op jit(solution)/shard_map/all_to_all | solution.py:214
  13.7 0.0 copy-done.2
  13.7 0.2 fusion
  13.9 4.3 %collective-permute-start = (f32[64,64]{1,0:T(8,128)S(1)}, f32[64,64]{1,0:T(8,128)S(1)}, u32[]{:S(2)}, u32[]{:S(2)}) collective-permute-start(f32[64,64]{1,0:T(8,128)S(1)} %fusion), channel_id=1, source_target_pairs={{0,1},{1,0},{2,3},{3,2},{4,5},{5,4},{6,7},{7,6},{8,9},{9,8},{10,11... | collective-permute-start | bytes 49160 | tf_op jit(solution)/shard_map/ppermute | solution.py:221
  18.2 1.9 collective-permute-done
  20.1 6.1 %collective-permute-start.1 = (f32[64,64]{1,0:T(8,128)S(1)}, f32[64,64]{1,0:T(8,128)S(1)}, u32[]{:S(2)}, u32[]{:S(2)}) collective-permute-start(f32[64,64]{1,0:T(8,128)S(1)} %add.18), channel_id=1, source_target_pairs={{0,2},{1,3},{2,0},{3,1},{4,6},{5,7},{6,4},{7,5},{8,10},{9,11},{10,... | collective-permute-start | bytes 49160 | tf_op jit(solution)/shard_map/ppermute | solution.py:221
  26.2 1.9 collective-permute-done.1
  28.0 9.3 %collective-permute-start.2 = (f32[64,64]{1,0:T(8,128)S(1)}, f32[64,64]{1,0:T(8,128)S(1)}, u32[]{:S(2)}, u32[]{:S(2)}) collective-permute-start(f32[64,64]{1,0:T(8,128)S(1)} %add.19), channel_id=1, source_target_pairs={{0,4},{1,5},{2,6},{3,7},{4,0},{5,1},{6,2},{7,3},{8,12},{9,13},{10,... | collective-permute-start | bytes 49160 | tf_op jit(solution)/shard_map/ppermute | solution.py:221
  37.3 1.9 collective-permute-done.2
  39.2 0.0 copy-start.1
  39.2 0.7 all-to-all-done.got_ref
  40.0 0.9 shard_map.59
  40.9 14.8 %all-to-all-start.1 = ((f32[16,64,128]{2,1,0:T(8,128)}), f32[16,64,128]{2,1,0:T(8,128)S(1)}, u32[]{:S(2)}, u32[]{:S(2)}) async-start(f32[16,64,128]{2,1,0:T(8,128)} %get-tuple-element.16), calls=%async_computation.1 | async-start | bytes 1048576 | tf_op jit(solution)/shard_map/all_to_all | solution.py:214
  55.7 7.7 %collective-permute-start.3 = (f32[64,64]{1,0:T(8,128)S(1)}, f32[64,64]{1,0:T(8,128)S(1)}, u32[]{:S(2)}, u32[]{:S(2)}) collective-permute-start(f32[64,64]{1,0:T(8,128)S(1)} %get-tuple-element.17), channel_id=1, source_target_pairs={{0,8},{8,0},{1,9},{9,1},{2,10},{10,2},{3,11},{11,3},{4,12},{12,4},... | collective-permute-start | bytes 49160 | tf_op jit(solution)/shard_map/ppermute | solution.py:221
  63.4 9.6 %collective-permute-done.3 = f32[64,64]{1,0:T(8,128)S(1)} collective-permute-done((f32[64,64]{1,0:T(8,128)S(1)}, f32[64,64]{1,0:T(8,128)S(1)}, u32[]{:S(2)}, u32[]{:S(2)}) %collective-permute-start.3) | collective-permute-done | bytes 16416 | tf_op jit(solution)/shard_map/ppermute | solution.py:221
  73.1 3.7 %all-to-all-done.1.got_ref = f32[16,64,128]{2,1,0:T(8,128)S(1)} async-done(((f32[16,64,128]{2,1,0:T(8,128)}), f32[16,64,128]{2,1,0:T(8,128)S(1)}, u32[]{:S(2)}, u32[]{:S(2)}) %all-to-all-start.1) | async-done | bytes 524320 | tf_op jit(solution)/shard_map/all_to_all | solution.py:214
  76.8 0.9 shard_map.60
  77.7 4.8 %all-to-all-start.2 = ((f32[16,64,128]{2,1,0:T(8,128)}), f32[16,64,128]{2,1,0:T(8,128)S(1)}, u32[]{:S(2)}, u32[]{:S(2)}) async-start(f32[16,64,128]{2,1,0:T(8,128)} %get-tuple-element.20), calls=%async_computation.2 | async-start | bytes 1048576 | tf_op jit(solution)/shard_map/all_to_all | solution.py:214
  82.4 2.5 %collective-permute-start.4 = (f32[64,64]{1,0:T(8,128)S(1)}, f32[64,64]{1,0:T(8,128)S(1)}, u32[]{:S(2)}, u32[]{:S(2)}) collective-permute-start(f32[64,64]{1,0:T(8,128)S(1)} %get-tuple-element.18), channel_id=1, source_target_pairs={{0,16},{16,0},{32,48},{48,32},{1,17},{17,1},{33,49},{49,33},{2,18}... | collective-permute-start | bytes 49160 | tf_op jit(solution)/shard_map/ppermute | solution.py:221
  84.9 3.3 %collective-permute-done.4 = f32[64,64]{1,0:T(8,128)S(1)} collective-permute-done((f32[64,64]{1,0:T(8,128)S(1)}, f32[64,64]{1,0:T(8,128)S(1)}, u32[]{:S(2)}, u32[]{:S(2)}) %collective-permute-start.4) | collective-permute-done | bytes 16416 | tf_op jit(solution)/shard_map/ppermute | solution.py:221
  88.3 2.5 %collective-permute-start.5 = (f32[64,64]{1,0:T(8,128)S(1)}, f32[64,64]{1,0:T(8,128)S(1)}, u32[]{:S(2)}, u32[]{:S(2)}) collective-permute-start(f32[64,64]{1,0:T(8,128)S(1)} %add.22), channel_id=1, source_target_pairs={{0,32},{16,48},{32,0},{48,16},{1,33},{17,49},{33,1},{49,17},{2,34}... | collective-permute-start | bytes 49160 | tf_op jit(solution)/shard_map/ppermute | solution.py:221
  90.8 0.0 copy-done.1
  90.8 0.2 fusion.1.gram_c_ref
  91.1 4.5 %collective-permute-done.5 = f32[64,64]{1,0:T(8,128)S(1)} collective-permute-done((f32[64,64]{1,0:T(8,128)S(1)}, f32[64,64]{1,0:T(8,128)S(1)}, u32[]{:S(2)}, u32[]{:S(2)}) %collective-permute-start.5) | collective-permute-done | bytes 16416 | tf_op jit(solution)/shard_map/ppermute | solution.py:221
  95.6 5.4 %shard_map.61.inverse_ref = f32[64,64]{1,0:T(8,128)S(1)} custom-call(f32[64,64]{1,0:T(8,128)S(1)} %add.23.gram_b_ref, f32[64,64]{1,0:T(8,128)S(1)} %fusion.1.gram_c_ref), custom_call_target="tpu_custom_call" | custom-call | tf_op jit(solution)/shard_map/pallas_call | solution.py:27
  100.9 0.0 all-to-all-done.2.got_ref
  100.9 0.6 shard_map.62
  101.6 0.0 copy-start
  101.6 26.7 %all_to_all.30 = f32[4,16,64,128]{3,2,1,0:T(8,128)S(1)} all-to-all(f32[4,16,64,128]{3,2,1,0:T(8,128)S(1)} %get-tuple-element.21), channel_id=1, replica_groups=mesh['ylo'=4,'core'=2,'x'=4,'yhi'=2,'z'=8] {'x'}, dimensions={0} | all-to-all | bytes 4194304 | tf_op jit(solution)/shard_map/all_to_all | solution.py:214
  128.2 0.0 copy-done
  128.2 5.3 %shard_map.63 = f32[8,96,128]{2,1,0:T(8,128)S(1)} custom-call(f32[128,8192]{1,0:T(8,128)S(1)} %bitcast.10, f32[64,64,128]{2,1,0:T(8,128)S(1)} %bitcast.11), custom_call_target="tpu_custom_call" | custom-call | tf_op jit(solution)/shard_map/pallas_call | solution.py:27
  133.5 13.8 %all_to_all.31.got_ref = f32[8,96,128]{2,1,0:T(8,128)S(1)} all-to-all(f32[8,96,128]{2,1,0:T(8,128)S(1)} %shard_map.63), channel_id=1, replica_groups=mesh['ylo'=4,'core'=2,'x'=4,'yhi'=2,'z'=8] {'ylo','core'}, dimensions={0} | all-to-all | bytes 786432 | tf_op jit(solution)/shard_map/all_to_all | solution.py:214
  147.3 6.2 %shard_map.64 = (f32[64,16,128]{2,1,0:T(8,128)S(1)}, f32[8,64]{1,0:T(8,128)S(1)}, f32[64,64]{1,0:T(8,128)S(1)}, f32[64,128]{1,0:T(8,128)}) custom-call(f32[8,96,128]{2,1,0:T(8,128)S(1)} %all_to_all.31.got_ref, f32[64,64]{1,0:T(8,128)S(1)} %fusion.1.gram_c_ref, f32[16,64]{1,0:T(8,128)S(1)} %bitcast.12, f32[64,128]{1,0:T(8,128)S(1)} %get-tuple-element.22.own_ref), custom_call_target="tpu_custom_call" | custom-call | tf_op jit(solution)/shard_map/pallas_call | solution.py:27
  153.5 36.4 %all_to_all.32.got_ref = f32[64,16,128]{2,1,0:T(8,128)S(1)} all-to-all(f32[64,16,128]{2,1,0:T(8,128)S(1)} %get-tuple-element.24), channel_id=1, replica_groups=mesh['ylo'=4,'core'=2,'x'=4,'yhi'=2,'z'=8] {'x','yhi','z'}, dimensions={0} | all-to-all | bytes 1048576 | tf_op jit(solution)/shard_map/all_to_all | solution.py:214
  189.9 6.4 %shard_map.65 = (f32[8,64]{1,0:T(8,128)}, f32[16,64]{1,0:T(8,128)}) custom-call(f32[64,16,128]{2,1,0:T(8,128)S(1)} %all_to_all.32.got_ref, f32[8,64]{1,0:T(8,128)S(1)} %get-tuple-element.25.raw_ref, f32[64,64]{1,0:T(8,128)S(1)} %get-tuple-element.26.gram_ref), custom_call_target="tpu_custom_call" | custom-call | tf_op jit(solution)/shard_map/pallas_call | solution.py:27
  (6 shorter events, 0.0 us)
Async XLA Ops:
  9.2 4.4 %copy-start.2 = (f32[64,8]{0,1:T(8,128)S(1)}, f32[64,8]{0,1:T(8,128)}, u32[]{:S(2)}) copy-start(f32[64,8]{0,1:T(8,128)} %param.4) | copy-start | bytes 6148
  9.2 30.8 %all-to-all-start = ((f32[4,16,64,128]{3,2,1,0:T(8,128)}), f32[4,16,64,128]{3,2,1,0:T(8,128)S(1)}, u32[]{:S(2)}, u32[]{:S(2)}) async-start(f32[4,16,64,128]{3,2,1,0:T(8,128)} %shard_map.58), calls=%async_computation | async-start | bytes 4194304 | tf_op jit(solution)/shard_map/all_to_all | solution.py:214
  13.9 6.2 %collective-permute-start = (f32[64,64]{1,0:T(8,128)S(1)}, f32[64,64]{1,0:T(8,128)S(1)}, u32[]{:S(2)}, u32[]{:S(2)}) collective-permute-start(f32[64,64]{1,0:T(8,128)S(1)} %fusion), channel_id=1, source_target_pairs={{0,1},{1,0},{2,3},{3,2},{4,5},{5,4},{6,7},{7,6},{8,9},{9,8},{10,11... | collective-permute-start | bytes 49160 | tf_op jit(solution)/shard_map/ppermute | solution.py:221
  20.1 8.0 %collective-permute-start.1 = (f32[64,64]{1,0:T(8,128)S(1)}, f32[64,64]{1,0:T(8,128)S(1)}, u32[]{:S(2)}, u32[]{:S(2)}) collective-permute-start(f32[64,64]{1,0:T(8,128)S(1)} %add.18), channel_id=1, source_target_pairs={{0,2},{1,3},{2,0},{3,1},{4,6},{5,7},{6,4},{7,5},{8,10},{9,11},{10,... | collective-permute-start | bytes 49160 | tf_op jit(solution)/shard_map/ppermute | solution.py:221
  28.0 11.2 %collective-permute-start.2 = (f32[64,64]{1,0:T(8,128)S(1)}, f32[64,64]{1,0:T(8,128)S(1)}, u32[]{:S(2)}, u32[]{:S(2)}) collective-permute-start(f32[64,64]{1,0:T(8,128)S(1)} %add.19), channel_id=1, source_target_pairs={{0,4},{1,5},{2,6},{3,7},{4,0},{5,1},{6,2},{7,3},{8,12},{9,13},{10,... | collective-permute-start | bytes 49160 | tf_op jit(solution)/shard_map/ppermute | solution.py:221
  39.2 51.6 %copy-start.1 = (f32[64,16]{0,1:T(8,128)S(1)}, f32[64,16]{0,1:T(8,128)}, u32[]{:S(2)}) copy-start(f32[64,16]{0,1:T(8,128)} %param.5) | copy-start | bytes 12292
  40.9 35.9 %all-to-all-start.1 = ((f32[16,64,128]{2,1,0:T(8,128)}), f32[16,64,128]{2,1,0:T(8,128)S(1)}, u32[]{:S(2)}, u32[]{:S(2)}) async-start(f32[16,64,128]{2,1,0:T(8,128)} %get-tuple-element.16), calls=%async_computation.1 | async-start | bytes 1048576 | tf_op jit(solution)/shard_map/all_to_all | solution.py:214
  55.7 17.4 %collective-permute-start.3 = (f32[64,64]{1,0:T(8,128)S(1)}, f32[64,64]{1,0:T(8,128)S(1)}, u32[]{:S(2)}, u32[]{:S(2)}) collective-permute-start(f32[64,64]{1,0:T(8,128)S(1)} %get-tuple-element.17), channel_id=1, source_target_pairs={{0,8},{8,0},{1,9},{9,1},{2,10},{10,2},{3,11},{11,3},{4,12},{12,4},... | collective-permute-start | bytes 49160 | tf_op jit(solution)/shard_map/ppermute | solution.py:221
  77.7 23.3 %all-to-all-start.2 = ((f32[16,64,128]{2,1,0:T(8,128)}), f32[16,64,128]{2,1,0:T(8,128)S(1)}, u32[]{:S(2)}, u32[]{:S(2)}) async-start(f32[16,64,128]{2,1,0:T(8,128)} %get-tuple-element.20), calls=%async_computation.2 | async-start | bytes 1048576 | tf_op jit(solution)/shard_map/all_to_all | solution.py:214
  82.4 5.8 %collective-permute-start.4 = (f32[64,64]{1,0:T(8,128)S(1)}, f32[64,64]{1,0:T(8,128)S(1)}, u32[]{:S(2)}, u32[]{:S(2)}) collective-permute-start(f32[64,64]{1,0:T(8,128)S(1)} %get-tuple-element.18), channel_id=1, source_target_pairs={{0,16},{16,0},{32,48},{48,32},{1,17},{17,1},{33,49},{49,33},{2,18}... | collective-permute-start | bytes 49160 | tf_op jit(solution)/shard_map/ppermute | solution.py:221
  88.3 7.3 %collective-permute-start.5 = (f32[64,64]{1,0:T(8,128)S(1)}, f32[64,64]{1,0:T(8,128)S(1)}, u32[]{:S(2)}, u32[]{:S(2)}) collective-permute-start(f32[64,64]{1,0:T(8,128)S(1)} %add.22), channel_id=1, source_target_pairs={{0,32},{16,48},{32,0},{48,16},{1,33},{17,49},{33,1},{49,17},{2,34}... | collective-permute-start | bytes 49160 | tf_op jit(solution)/shard_map/ppermute | solution.py:221
  101.6 26.7 %copy-start = (f32[8,16,8192]{2,1,0:T(8,128)S(1)}, f32[8,16,8192]{2,1,0:T(8,128)}, u32[]{:S(2)}) copy-start(f32[8,16,8192]{2,1,0:T(8,128)} %param.3) | copy-start | bytes 12582916

commit v5 on v4

--- a/solution.py
+++ b/solution.py
@@ -16,6 +16,8 @@
 SPLIT = {"ylo": 4, "core": 2, "x": 4, "yhi": 2, "z": 8}
 VMEM = pl.BlockSpec(memory_space=pltpu.VMEM)
 STREAM = pltpu.CompilerParams(vmem_limit_bytes=60 * 1024 * 1024)
+FAN = pltpu.CompilerParams(vmem_limit_bytes=52 * 1024 * 1024)
+CONTRACT = pltpu.CompilerParams(vmem_limit_bytes=50 * 1024 * 1024)
 PARAMS = pltpu.CompilerParams(vmem_limit_bytes=40 * 1024 * 1024)
 
 
@@ -23,30 +25,39 @@
     return jax.ShapeDtypeStruct(shape, jnp.float32)
 
 
-def call(body, outs, *operands):
+def call(body, outs, *operands, params=PARAMS):
     return pl.pallas_call(
         body,
         out_shape=outs,
         in_specs=[VMEM] * len(operands),
         out_specs=jax.tree.map(lambda _: VMEM, outs),
-        compiler_params=PARAMS,
+        compiler_params=params,
     )(*operands)
 
 
-def partial_body(nyhi, nz, nights_ref, spans_ref, x_ref, out_ref):
-    rank, nights = nights_ref.shape
-    intervals = spans_ref.shape[1]
+def transposed_dot(left, right):
+    return lax.dot_general(
+        left, right, (((0,), (0,)), ((), ())), precision=FULL,
+        preferred_element_type=jnp.float32,
+    )
+
+
+def partial_body(nyhi, nz, nights_ref, spans_ref, x_ref, out_ref, kron_ref):
+    nights, intervals = nights_ref.shape[0], spans_ref.shape[0]
     share = x_ref.shape[1] // (nyhi * nz)
-    kron = jnp.dot(
-        nights_ref[...], onehot(nights, nights * intervals, lambda j, c: c // intervals == j),
-        precision=FULL, preferred_element_type=jnp.float32,
-    ) * jnp.dot(
-        spans_ref[...], onehot(intervals, nights * intervals, lambda k, c: c % intervals == k),
-        precision=FULL, preferred_element_type=jnp.float32,
-    )
+
+    @pl.when(pl.program_id(0) == 0)
+    def _():
+        columns = nights * intervals
+        kron_ref[...] = transposed_dot(
+            nights_ref[...], onehot(nights, columns, lambda j, c: c // intervals == j)
+        ) * transposed_dot(
+            spans_ref[...], onehot(intervals, columns, lambda k, c: c % intervals == k)
+        )
+
     for y in range(nyhi):
         product = jnp.dot(
-            kron, x_ref[:, y * nz * share : (y + 1) * nz * share], precision=FULL,
+            kron_ref[...], x_ref[:, y * nz * share : (y + 1) * nz * share], precision=FULL,
             preferred_element_type=jnp.float32,
         )
         for z in range(nz):
@@ -77,19 +88,10 @@
     gram_out_ref[...] = gram_ref[...]
 
 
-def apply_body(inverse_ref, own_ref, got_ref, own_out_ref, send_ref):
-    dot = functools.partial(jnp.dot, precision=FULL, preferred_element_type=jnp.float32)
-    inverse = inverse_ref[...]
-    own_out_ref[...] = dot(inverse, own_ref[...])
-    step = min(8, got_ref.shape[0])
-    width = got_ref.shape[-1]
-    for first in range(0, got_ref.shape[0], step):
-        products = jnp.concatenate([got_ref[first + i] for i in range(step)], axis=1)
-        loadings = dot(inverse, products)
-        for i in range(step):
-            block = loadings[:, i * width : (i + 1) * width]
-            for k in range(send_ref.shape[0]):
-                send_ref[k, first + i] = block
+def fan_body(got_ref, gram_ref, send_ref, gram_out_ref):
+    for k in range(send_ref.shape[0]):
+        send_ref[k] = got_ref[...]
+    gram_out_ref[...] = gram_ref[...]
 
 
 def onehot(rows, columns, test):
@@ -103,18 +105,31 @@
     return onehot(size, size, lambda i, j: i == j)
 
 
-def contract_body(nyhi, nz, x_ref, a_ref, out_ref):
-    rank, share = a_ref.shape[1:]
+def contract_body(
+    nyhi, nz, inverse_ref, own_ref, x_ref, m_ref, out_ref, own_out_ref, held_ref, sems
+):
+    rank, share = m_ref.shape[1:]
     rows = x_ref.shape[0]
+    copies = [
+        pltpu.make_async_copy(
+            x_ref.at[:, pl.ds(group * nz * share, nz * share)], held_ref.at[group], sems.at[group]
+        )
+        for group in range(held_ref.shape[0])
+    ]
+    for copy in copies:
+        copy.start()
+    dot = functools.partial(jnp.dot, precision=FULL, preferred_element_type=jnp.float32)
+    inverse = inverse_ref[...]
+    own_out_ref[...] = dot(inverse, own_ref[...])
     total = jnp.zeros((rows + rank, rank), jnp.float32)
-    for group in range(a_ref.shape[0] // nz):
+    for group in range(held_ref.shape[0]):
         x, y = group // nyhi, group % nyhi
-        loadings = jnp.concatenate(
-            [a_ref[(x * nz + z) * nyhi + y] for z in range(nz)], axis=1
-        )
-        left = jnp.concatenate(
-            [x_ref[:, group * nz * share : (group + 1) * nz * share], loadings], axis=0
-        )
+        products = jnp.concatenate(
+            [m_ref[(x * nz + z) * nyhi + y] for z in range(nz)], axis=1
+        )
+        loadings = dot(inverse, products)
+        copies[group].wait()
+        left = jnp.concatenate([held_ref[group], loadings], axis=0)
         total += lax.dot_general(
             left, loadings, (((1,), (1,)), ((), ())), precision=FULL,
             preferred_element_type=jnp.float32,
@@ -135,13 +150,24 @@
     size = gram.shape[0]
     work = jnp.concatenate([gram, right], axis=0)
     lane = lax.broadcasted_iota(jnp.int32, (1, size), 1)
-    for p in range(size):
-        at = p % 8
-        row = work[at : at + 1, :]
-        here = lane == p
-        factor = jnp.where(here, -1.0, row) / row[:, p : p + 1]
-        work = jnp.where(here, 0.0, work) - work[:, p : p + 1] * factor
-        if at == 7:
+    for p in range(0, size, 2):
+        at, q = p % 8, p + 1
+        first, second = work[at : at + 1, :], work[at + 1 : at + 2, :]
+        cross = first[:, q : q + 1]
+        invert = 1.0 / first[:, p : p + 1]
+        ratio = cross * invert
+        schur = 1.0 / (second[:, q : q + 1] - cross * ratio)
+        here = (lane == p) | (lane == q)
+        first = jnp.where(here, jnp.where(lane == p, -1.0, 0.0), first)
+        second = jnp.where(here, jnp.where(lane == q, -1.0, 0.0), second)
+        second = (second - ratio * first) * schur
+        first = first * invert - ratio * second
+        work = (
+            jnp.where(here, 0.0, work)
+            - work[:, p : p + 1] * first
+            - work[:, q : q + 1] * second
+        )
+        if at == 6:
             work = work[8:]
     return work
 
@@ -238,13 +264,14 @@
         out_shape=f32(nx, places, rank, share),
         grid=(nx,),
         in_specs=[
-            pl.BlockSpec((rank, nights), lambda i: (0, 0)),
-            pl.BlockSpec((rank, intervals), lambda i: (0, 0)),
+            pl.BlockSpec((nights, rank), lambda i: (0, 0)),
+            pl.BlockSpec((intervals, rank), lambda i: (0, 0)),
             pl.BlockSpec((nights * intervals, places * share), lambda i: (0, i)),
         ],
         out_specs=pl.BlockSpec((1, places, rank, share), lambda i: (i, 0, 0, 0)),
+        scratch_shapes=[pltpu.VMEM((rank, nights * intervals), jnp.float32)],
         compiler_params=STREAM,
-    )(evenings, spans, x2)
+    )(evenings.T, spans.T, x2)
 
     square = f32(rank, rank)
     gram_b = jnp.dot(evenings, evenings.T, precision=FULL)
@@ -252,23 +279,31 @@
     joined, gram_b = call(
         join_body, (f32(places, rank, share), square), exchange(blocks, "x"), gram_b
     )
-    gram_b = butterfly(gram_b, "yhi")
+    gram_b = butterfly(gram_b, "x")
     own, send, gram_b = call(
         own_body, (f32(rank, share), f32(places, rank, share), square),
         exchange(joined, ZY), gram_b,
     )
-    gram_b = butterfly(gram_b, "x")
+    send, gram_b = call(
+        fan_body, (f32(nx, places, rank, share), square), exchange(send, ZY), gram_b,
+        params=FAN,
+    )
+    gram_b = butterfly(gram_b, "yhi")
     inverse = call(inverse_body, square, gram_b, gram_c)
-    own_raw, send = call(
-        apply_body, (f32(rank, share), f32(nx, places, rank, share)),
-        inverse, own, exchange(send, ZY),
-    )
     full = exchange(send, "x").reshape(night_devices, rank, share)
 
-    packed = call(
+    groups = nx * nyhi
+    packed, own_raw = pl.pallas_call(
         functools.partial(contract_body, nyhi, nz),
-        f32(copies, (nights * intervals + rank) // 2, 2 * rank), x2, full,
-    )
+        out_shape=(f32(copies, (nights * intervals + rank) // 2, 2 * rank), f32(rank, share)),
+        in_specs=[VMEM, VMEM, pl.BlockSpec(memory_space=pl.ANY), VMEM],
+        out_specs=(VMEM, VMEM),
+        scratch_shapes=[
+            pltpu.VMEM((groups, nights * intervals, nz * share), jnp.float32),
+            pltpu.SemaphoreType.DMA((groups,)),
+        ],
+        compiler_params=CONTRACT,
+    )(inverse, own, x2, full)
     send, raw, gram_a, own_columns = call(
         functools.partial(night_body, meters * copies),
         (

time: 197 us -> 198 us (level)
  blocking collectives: 76.9 us -> 67.7 us
  waiting for transfers between devices: 27.6 us -> 36.6 us
  Pallas kernels: 31.4 us -> 39.4 us
  starting transfers between devices: 56.3 us -> 51.8 us
  local copies, waits for them, and re-layouts: 2.78 us -> 0.01 us
    all_to_all x3, waiting for transfers between devices: 4.48 us -> 17.6 us  [exchange(): return lax.all_to_all(blocks, axis, 0, 0, tiled=True)]
    pallas_call x0 -> x1, Pallas kernels: none -> 12.8 us  [on_device(): pl.pallas_call(functools.partial(contract_body, nyhi, nz), out_shape=(f32...]
    all_to_all x3, blocking collectives: 76.9 us -> 67.7 us  [exchange(): return lax.all_to_all(blocks, axis, 0, 0, tiled=True)]
    pallas_call x7 -> x6, Pallas kernels: 25.6 us -> 21 us  [call(): pl.pallas_call(body, out_shape=outs, in_specs=[VMEM] * len(operands), out...]
    ppermute x6, waiting for transfers between devices: 23.1 us -> 19 us  [butterfly(): total += lax.ppermute(total, axis, [(i, i ^ step) for i in range(size)])]
    ppermute x6, starting transfers between devices: 32.4 us -> 28.8 us  [butterfly(): total += lax.ppermute(total, axis, [(i, i ^ step) for i in range(size)])]
    unnamed x8 -> x4, local copies, waits for them, and re-layouts: 2.78 us -> 0.01 us
  transfers between devices with their start and end apart: 9 -> 9, of which waited for: 8 -> 9; matrix products, arithmetic and copies ran while one was open for 0% -> 0% of each run, Pallas kernels for 3% -> 3%
where the time goes in v5:
time: 198 us; the launch traced here: 197 us
  blocking collectives  67.7 us (34%)
  starting transfers between devices  51.8 us (26%)
  Pallas kernels  39.4 us (20%)
  waiting for transfers between devices  36.6 us (18%)
    all_to_all x3, blocking collectives, exchange(): return lax.all_to_all(blocks, axis, 0, 0, tiled=True)  67.7 us
    ppermute x6, starting transfers between devices, butterfly(): total += lax.ppermute(total, axis, [(i, i ^ step) for i in range(size)])  28.8 us
    all_to_all x3, starting transfers between devices, exchange(): return lax.all_to_all(blocks, axis, 0, 0, tiled=True)  22.9 us
    pallas_call x6, Pallas kernels, call(): pl.pallas_call(body, out_shape=outs, in_specs=[VMEM] * len(operands), out...  21 us
    ppermute x6, waiting for transfers between devices, butterfly(): total += lax.ppermute(total, axis, [(i, i ^ step) for i in range(size)])  19 us
    all_to_all x3, waiting for transfers between devices, exchange(): return lax.all_to_all(blocks, axis, 0, 0, tiled=True)  17.6 us
    pallas_call x1, Pallas kernels, on_device(): pl.pallas_call(functools.partial(contract_body, nyhi, nz), out_shape=(f32...  12.8 us
    pallas_call x1, Pallas kernels, on_device(): pl.pallas_call(functools.partial(partial_body, nyhi, nz), out_shape=f32(n...  5.63 us
  transfers between devices with their start and end apart: 9, of which 9 were waited for; matrix products, arithmetic and copies ran while one was open for 0% of the time, Pallas kernels for 3%

profile of v5, /device:TPU:8, one launch (start us, length us, event | category | flops | bytes accessed | tf_op | source)
XLA Modules:
  0.0 196.7 jit_solution(9317497400263636402)
XLA Ops:
  0.6 5.6 %shard_map.58 = f32[4,16,64,128]{3,2,1,0:T(8,128)} custom-call(f32[8,64]{1,0:T(8,128)} %bitcast.15, f32[16,64]{1,0:T(8,128)} %bitcast.11, f32[128,8192]{1,0:T(8,128)} %bitcast.13), custom_call_target="tpu_custom_call" | custom-call | tf_op jit(solution)/shard_map/pallas_call | solution.py:262
  6.3 0.0 copy-start.1
  6.3 4.4 %all-to-all-start = ((f32[4,16,64,128]{3,2,1,0:T(8,128)}), f32[4,16,64,128]{3,2,1,0:T(8,128)S(1)}, u32[]{:S(2)}, u32[]{:S(2)}) async-start(f32[4,16,64,128]{3,2,1,0:T(8,128)} %shard_map.58), calls=%async_computation | async-start | bytes 4194304 | tf_op jit(solution)/shard_map/all_to_all | solution.py:240
  10.7 0.0 copy-done.1
  10.7 0.2 fusion
  10.9 4.3 %collective-permute-start = (f32[64,64]{1,0:T(8,128)S(1)}, f32[64,64]{1,0:T(8,128)S(1)}, u32[]{:S(2)}, u32[]{:S(2)}) collective-permute-start(f32[64,64]{1,0:T(8,128)S(1)} %fusion), channel_id=1, source_target_pairs={{0,1},{1,0},{2,3},{3,2},{4,5},{5,4},{6,7},{7,6},{8,9},{9,8},{10,11... | collective-permute-start | bytes 49160 | tf_op jit(solution)/shard_map/ppermute | solution.py:247
  15.2 1.9 collective-permute-done
  17.1 6.1 %collective-permute-start.1 = (f32[64,64]{1,0:T(8,128)S(1)}, f32[64,64]{1,0:T(8,128)S(1)}, u32[]{:S(2)}, u32[]{:S(2)}) collective-permute-start(f32[64,64]{1,0:T(8,128)S(1)} %add.18), channel_id=1, source_target_pairs={{0,2},{1,3},{2,0},{3,1},{4,6},{5,7},{6,4},{7,5},{8,10},{9,11},{10,... | collective-permute-start | bytes 49160 | tf_op jit(solution)/shard_map/ppermute | solution.py:247
  23.2 1.9 collective-permute-done.1
  25.1 9.3 %collective-permute-start.2 = (f32[64,64]{1,0:T(8,128)S(1)}, f32[64,64]{1,0:T(8,128)S(1)}, u32[]{:S(2)}, u32[]{:S(2)}) collective-permute-start(f32[64,64]{1,0:T(8,128)S(1)} %add.19), channel_id=1, source_target_pairs={{0,4},{1,5},{2,6},{3,7},{4,0},{5,1},{6,2},{7,3},{8,12},{9,13},{10,... | collective-permute-start | bytes 49160 | tf_op jit(solution)/shard_map/ppermute | solution.py:247
  34.4 1.9 collective-permute-done.2
  36.3 0.7 all-to-all-done.got_ref
  37.0 0.9 shard_map.59
  37.9 14.8 %all-to-all-start.1 = ((f32[16,64,128]{2,1,0:T(8,128)}), f32[16,64,128]{2,1,0:T(8,128)S(1)}, u32[]{:S(2)}, u32[]{:S(2)}) async-start(f32[16,64,128]{2,1,0:T(8,128)} %get-tuple-element.18), calls=%async_computation.1 | async-start | bytes 1048576 | tf_op jit(solution)/shard_map/all_to_all | solution.py:240
  52.7 2.5 %collective-permute-start.3 = (f32[64,64]{1,0:T(8,128)S(1)}, f32[64,64]{1,0:T(8,128)S(1)}, u32[]{:S(2)}, u32[]{:S(2)}) collective-permute-start(f32[64,64]{1,0:T(8,128)S(1)} %get-tuple-element.19), channel_id=1, source_target_pairs={{0,16},{16,0},{32,48},{48,32},{1,17},{17,1},{33,49},{49,33},{2,18}... | collective-permute-start | bytes 49160 | tf_op jit(solution)/shard_map/ppermute | solution.py:247
  55.2 3.3 %collective-permute-done.3 = f32[64,64]{1,0:T(8,128)S(1)} collective-permute-done((f32[64,64]{1,0:T(8,128)S(1)}, f32[64,64]{1,0:T(8,128)S(1)}, u32[]{:S(2)}, u32[]{:S(2)}) %collective-permute-start.3) | collective-permute-done | bytes 16416 | tf_op jit(solution)/shard_map/ppermute | solution.py:247
  58.5 2.5 %collective-permute-start.4 = (f32[64,64]{1,0:T(8,128)S(1)}, f32[64,64]{1,0:T(8,128)S(1)}, u32[]{:S(2)}, u32[]{:S(2)}) collective-permute-start(f32[64,64]{1,0:T(8,128)S(1)} %add.21), channel_id=1, source_target_pairs={{0,32},{16,48},{32,0},{48,16},{1,33},{17,49},{33,1},{49,17},{2,34}... | collective-permute-start | bytes 49160 | tf_op jit(solution)/shard_map/ppermute | solution.py:247
  61.0 4.8 %collective-permute-done.4 = f32[64,64]{1,0:T(8,128)S(1)} collective-permute-done((f32[64,64]{1,0:T(8,128)S(1)}, f32[64,64]{1,0:T(8,128)S(1)}, u32[]{:S(2)}, u32[]{:S(2)}) %collective-permute-start.4) | collective-permute-done | bytes 16416 | tf_op jit(solution)/shard_map/ppermute | solution.py:247
  65.8 7.8 %all-to-all-done.1.got_ref = f32[16,64,128]{2,1,0:T(8,128)S(1)} async-done(((f32[16,64,128]{2,1,0:T(8,128)}), f32[16,64,128]{2,1,0:T(8,128)S(1)}, u32[]{:S(2)}, u32[]{:S(2)}) %all-to-all-start.1) | async-done | bytes 524320 | tf_op jit(solution)/shard_map/all_to_all | solution.py:240
  73.6 0.1 shard_map.60
  73.7 23.6 %all_to_all.30.got_ref = f32[16,64,128]{2,1,0:T(8,128)S(1)} all-to-all(f32[16,64,128]{2,1,0:T(8,128)S(1)} %get-tuple-element.20), channel_id=1, replica_groups=mesh['ylo'=4,'core'=2,'x'=4,'yhi'=2,'z'=8] {'z','yhi'}, dimensions={0} | all-to-all | bytes 1048576 | tf_op jit(solution)/shard_map/all_to_all | solution.py:240
  97.3 1.5 shard_map.61
  98.8 0.0 copy-start
  98.8 3.7 %all-to-all-start.3 = ((f32[4,16,64,128]{3,2,1,0:T(8,128)}), f32[4,16,64,128]{3,2,1,0:T(8,128)S(1)}, u32[]{:S(2)}, u32[]{:S(2)}) async-start(f32[4,16,64,128]{3,2,1,0:T(8,128)} %get-tuple-element.24), calls=%async_computation.3 | async-start | bytes 4194304 | tf_op jit(solution)/shard_map/all_to_all | solution.py:240
  102.5 4.2 %collective-permute-start.5 = (f32[64,64]{1,0:T(8,128)S(1)}, f32[64,64]{1,0:T(8,128)S(1)}, u32[]{:S(2)}, u32[]{:S(2)}) collective-permute-start(f32[64,64]{1,0:T(8,128)S(1)} %get-tuple-element.22), channel_id=1, source_target_pairs={{0,8},{8,0},{1,9},{9,1},{2,10},{10,2},{3,11},{11,3},{4,12},{12,4},... | collective-permute-start | bytes 49160 | tf_op jit(solution)/shard_map/ppermute | solution.py:247
  106.7 0.0 copy-done
  106.8 0.2 fusion.1.gram_c_ref
  107.0 5.3 %collective-permute-done.5 = f32[64,64]{1,0:T(8,128)S(1)} collective-permute-done((f32[64,64]{1,0:T(8,128)S(1)}, f32[64,64]{1,0:T(8,128)S(1)}, u32[]{:S(2)}, u32[]{:S(2)}) %collective-permute-start.5) | collective-permute-done | bytes 16416 | tf_op jit(solution)/shard_map/ppermute | solution.py:247
  112.3 5.8 %shard_map.62.inverse_ref = f32[64,64]{1,0:T(8,128)S(1)} custom-call(f32[64,64]{1,0:T(8,128)S(1)} %add.23.gram_b_ref, f32[64,64]{1,0:T(8,128)S(1)} %fusion.1.gram_c_ref), custom_call_target="tpu_custom_call" | custom-call | tf_op jit(solution)/shard_map/pallas_call | solution.py:29
  118.0 9.1 %all-to-all-done.3 = f32[4,16,64,128]{3,2,1,0:T(8,128)S(1)} async-done(((f32[4,16,64,128]{3,2,1,0:T(8,128)}), f32[4,16,64,128]{3,2,1,0:T(8,128)S(1)}, u32[]{:S(2)}, u32[]{:S(2)}) %all-to-all-start.3) | async-done | bytes 2097184 | tf_op jit(solution)/shard_map/all_to_all | solution.py:240
  127.1 12.8 %shard_map.63 = (f32[8,96,128]{2,1,0:T(8,128)S(1)}, f32[64,128]{1,0:T(8,128)S(1)}) custom-call(f32[64,64]{1,0:T(8,128)S(1)} %shard_map.62.inverse_ref, f32[64,128]{1,0:T(8,128)S(1)} %get-tuple-element.23.own_ref, f32[128,8192]{1,0:T(8,128)} %bitcast.14, f32[64,64,128]{2,1,0:T(8,128)S(1)} %bitcast.10), custom_call_target="tpu_custom_call" | custom-call | tf_op jit(solution)/shard_map/pallas_call | solution.py:296
  139.9 13.8 %all_to_all.31.got_ref = f32[8,96,128]{2,1,0:T(8,128)S(1)} all-to-all(f32[8,96,128]{2,1,0:T(8,128)S(1)} %get-tuple-element.25), channel_id=1, replica_groups=mesh['ylo'=4,'core'=2,'x'=4,'yhi'=2,'z'=8] {'ylo','core'}, dimensions={0} | all-to-all | bytes 786432 | tf_op jit(solution)/shard_map/all_to_all | solution.py:240
  153.7 6.2 %shard_map.64 = (f32[64,16,128]{2,1,0:T(8,128)S(1)}, f32[8,64]{1,0:T(8,128)S(1)}, f32[64,64]{1,0:T(8,128)S(1)}, f32[64,128]{1,0:T(8,128)}) custom-call(f32[8,96,128]{2,1,0:T(8,128)S(1)} %all_to_all.31.got_ref, f32[64,64]{1,0:T(8,128)S(1)} %fusion.1.gram_c_ref, f32[16,64]{1,0:T(8,128)S(1)} %bitcast.12, f32[64,128]{1,0:T(8,128)S(1)} %get-tuple-element.26.own_ref), custom_call_target="tpu_custom_call" | custom-call | tf_op jit(solution)/shard_map/pallas_call | solution.py:29
  159.9 30.2 %all_to_all.32.got_ref = f32[64,16,128]{2,1,0:T(8,128)S(1)} all-to-all(f32[64,16,128]{2,1,0:T(8,128)S(1)} %get-tuple-element.28), channel_id=1, replica_groups=mesh['ylo'=4,'core'=2,'x'=4,'yhi'=2,'z'=8] {'x','yhi','z'}, dimensions={0} | all-to-all | bytes 1048576 | tf_op jit(solution)/shard_map/all_to_all | solution.py:240
  190.1 6.6 %shard_map.65 = (f32[8,64]{1,0:T(8,128)}, f32[16,64]{1,0:T(8,128)}) custom-call(f32[64,16,128]{2,1,0:T(8,128)S(1)} %all_to_all.32.got_ref, f32[8,64]{1,0:T(8,128)S(1)} %get-tuple-element.29.raw_ref, f32[64,64]{1,0:T(8,128)S(1)} %get-tuple-element.30.gram_ref), custom_call_target="tpu_custom_call" | custom-call | tf_op jit(solution)/shard_map/pallas_call | solution.py:29
  (6 shorter events, 0.0 us)
Async XLA Ops:
  6.3 4.4 %copy-start.1 = (f32[64,8]{0,1:T(8,128)S(1)}, f32[64,8]{0,1:T(8,128)}, u32[]{:S(2)}) copy-start(f32[64,8]{0,1:T(8,128)} %param.4) | copy-start | bytes 6148
  6.3 30.8 %all-to-all-start = ((f32[4,16,64,128]{3,2,1,0:T(8,128)}), f32[4,16,64,128]{3,2,1,0:T(8,128)S(1)}, u32[]{:S(2)}, u32[]{:S(2)}) async-start(f32[4,16,64,128]{3,2,1,0:T(8,128)} %shard_map.58), calls=%async_computation | async-start | bytes 4194304 | tf_op jit(solution)/shard_map/all_to_all | solution.py:240
  10.9 6.2 %collective-permute-start = (f32[64,64]{1,0:T(8,128)S(1)}, f32[64,64]{1,0:T(8,128)S(1)}, u32[]{:S(2)}, u32[]{:S(2)}) collective-permute-start(f32[64,64]{1,0:T(8,128)S(1)} %fusion), channel_id=1, source_target_pairs={{0,1},{1,0},{2,3},{3,2},{4,5},{5,4},{6,7},{7,6},{8,9},{9,8},{10,11... | collective-permute-start | bytes 49160 | tf_op jit(solution)/shard_map/ppermute | solution.py:247
  17.1 8.0 %collective-permute-start.1 = (f32[64,64]{1,0:T(8,128)S(1)}, f32[64,64]{1,0:T(8,128)S(1)}, u32[]{:S(2)}, u32[]{:S(2)}) collective-permute-start(f32[64,64]{1,0:T(8,128)S(1)} %add.18), channel_id=1, source_target_pairs={{0,2},{1,3},{2,0},{3,1},{4,6},{5,7},{6,4},{7,5},{8,10},{9,11},{10,... | collective-permute-start | bytes 49160 | tf_op jit(solution)/shard_map/ppermute | solution.py:247
  25.1 11.2 %collective-permute-start.2 = (f32[64,64]{1,0:T(8,128)S(1)}, f32[64,64]{1,0:T(8,128)S(1)}, u32[]{:S(2)}, u32[]{:S(2)}) collective-permute-start(f32[64,64]{1,0:T(8,128)S(1)} %add.19), channel_id=1, source_target_pairs={{0,4},{1,5},{2,6},{3,7},{4,0},{5,1},{6,2},{7,3},{8,12},{9,13},{10,... | collective-permute-start | bytes 49160 | tf_op jit(solution)/shard_map/ppermute | solution.py:247
  37.9 35.7 %all-to-all-start.1 = ((f32[16,64,128]{2,1,0:T(8,128)}), f32[16,64,128]{2,1,0:T(8,128)S(1)}, u32[]{:S(2)}, u32[]{:S(2)}) async-start(f32[16,64,128]{2,1,0:T(8,128)} %get-tuple-element.18), calls=%async_computation.1 | async-start | bytes 1048576 | tf_op jit(solution)/shard_map/all_to_all | solution.py:240
  52.7 5.8 %collective-permute-start.3 = (f32[64,64]{1,0:T(8,128)S(1)}, f32[64,64]{1,0:T(8,128)S(1)}, u32[]{:S(2)}, u32[]{:S(2)}) collective-permute-start(f32[64,64]{1,0:T(8,128)S(1)} %get-tuple-element.19), channel_id=1, source_target_pairs={{0,16},{16,0},{32,48},{48,32},{1,17},{17,1},{33,49},{49,33},{2,18}... | collective-permute-start | bytes 49160 | tf_op jit(solution)/shard_map/ppermute | solution.py:247
  58.5 7.3 %collective-permute-start.4 = (f32[64,64]{1,0:T(8,128)S(1)}, f32[64,64]{1,0:T(8,128)S(1)}, u32[]{:S(2)}, u32[]{:S(2)}) collective-permute-start(f32[64,64]{1,0:T(8,128)S(1)} %add.21), channel_id=1, source_target_pairs={{0,32},{16,48},{32,0},{48,16},{1,33},{17,49},{33,1},{49,17},{2,34}... | collective-permute-start | bytes 49160 | tf_op jit(solution)/shard_map/ppermute | solution.py:247
  98.8 8.0 %copy-start = (f32[64,16]{0,1:T(8,128)S(1)}, f32[64,16]{0,1:T(8,128)}, u32[]{:S(2)}) copy-start(f32[64,16]{0,1:T(8,128)} %param.5) | copy-start | bytes 12292
  98.8 28.3 %all-to-all-start.3 = ((f32[4,16,64,128]{3,2,1,0:T(8,128)}), f32[4,16,64,128]{3,2,1,0:T(8,128)S(1)}, u32[]{:S(2)}, u32[]{:S(2)}) async-start(f32[4,16,64,128]{3,2,1,0:T(8,128)} %get-tuple-element.24), calls=%async_computation.3 | async-start | bytes 4194304 | tf_op jit(solution)/shard_map/all_to_all | solution.py:240
  102.5 9.7 %collective-permute-start.5 = (f32[64,64]{1,0:T(8,128)S(1)}, f32[64,64]{1,0:T(8,128)S(1)}, u32[]{:S(2)}, u32[]{:S(2)}) collective-permute-start(f32[64,64]{1,0:T(8,128)S(1)} %get-tuple-element.22), channel_id=1, source_target_pairs={{0,8},{8,0},{1,9},{9,1},{2,10},{10,2},{3,11},{11,3},{4,12},{12,4},... | collective-permute-start | bytes 49160 | tf_op jit(solution)/shard_map/ppermute | solution.py:247

commit v6 on v5

--- a/solution.py
+++ b/solution.py
@@ -35,6 +35,11 @@
     )(*operands)
 
 
+def split(values):
+    high = values.astype(jnp.bfloat16)
+    return high, (values - high.astype(jnp.float32)).astype(jnp.bfloat16)
+
+
 def transposed_dot(left, right):
     return lax.dot_general(
         left, right, (((0,), (0,)), ((), ())), precision=FULL,
@@ -55,11 +60,21 @@
             spans_ref[...], onehot(intervals, columns, lambda k, c: c % intervals == k)
         )
 
+    high, low = split(kron_ref[...])
+    rank = kron_ref.shape[0]
+    left = jnp.concatenate(
+        [
+            jnp.concatenate([high, high], axis=1),
+            jnp.concatenate([low, jnp.zeros_like(low)], axis=1),
+        ],
+        axis=0,
+    )
     for y in range(nyhi):
-        product = jnp.dot(
-            kron_ref[...], x_ref[:, y * nz * share : (y + 1) * nz * share], precision=FULL,
-            preferred_element_type=jnp.float32,
-        )
+        right = jnp.concatenate(
+            split(x_ref[:, y * nz * share : (y + 1) * nz * share]), axis=0
+        )
+        product = jnp.dot(left, right, preferred_element_type=jnp.float32)
+        product = product[:rank] + product[rank:]
         for z in range(nz):
             out_ref[0, z * nyhi + y] = product[:, z * share : (z + 1) * share]
 
@@ -118,22 +133,34 @@
     ]
     for copy in copies:
         copy.start()
-    dot = functools.partial(jnp.dot, precision=FULL, preferred_element_type=jnp.float32)
     inverse = inverse_ref[...]
-    own_out_ref[...] = dot(inverse, own_ref[...])
-    total = jnp.zeros((rows + rank, rank), jnp.float32)
+    own_out_ref[...] = jnp.dot(
+        inverse, own_ref[...], precision=FULL, preferred_element_type=jnp.float32
+    )
+    high, low = split(inverse)
+    solver = jnp.concatenate([high, high, low], axis=1)
+    loadings = []
     for group in range(held_ref.shape[0]):
         x, y = group // nyhi, group % nyhi
-        products = jnp.concatenate(
-            [m_ref[(x * nz + z) * nyhi + y] for z in range(nz)], axis=1
-        )
-        loadings = dot(inverse, products)
+        high, low = split(
+            jnp.concatenate([m_ref[(x * nz + z) * nyhi + y] for z in range(nz)], axis=1)
+        )
+        factor = jnp.dot(
+            solver, jnp.concatenate([high, low, high], axis=0),
+            preferred_element_type=jnp.float32,
+        )
+        loadings.append(split(factor))
+    total = jnp.zeros((2 * (rows + rank), 2 * rank), jnp.float32)
+    for group, (high, low) in enumerate(loadings):
         copies[group].wait()
-        left = jnp.concatenate([held_ref[group], loadings], axis=0)
+        x_high, x_low = split(held_ref[group])
         total += lax.dot_general(
-            left, loadings, (((1,), (1,)), ((), ())), precision=FULL,
-            preferred_element_type=jnp.float32,
-        )
+            jnp.concatenate([x_high, high, x_low, low], axis=0),
+            jnp.concatenate([high, low], axis=0),
+            (((1,), (1,)), ((), ())), preferred_element_type=jnp.float32,
+        )
+    total = total[:, :rank] + total[:, rank:]
+    total = total[: rows + rank] + total[rows + rank :]
     half, quarter = rows // 2, rank // 2
     packed = jnp.concatenate(
         [
@@ -150,24 +177,13 @@
     size = gram.shape[0]
     work = jnp.concatenate([gram, right], axis=0)
     lane = lax.broadcasted_iota(jnp.int32, (1, size), 1)
-    for p in range(0, size, 2):
-        at, q = p % 8, p + 1
-        first, second = work[at : at + 1, :], work[at + 1 : at + 2, :]
-        cross = first[:, q : q + 1]
-        invert = 1.0 / first[:, p : p + 1]
-        ratio = cross * invert
-        schur = 1.0 / (second[:, q : q + 1] - cross * ratio)
-        here = (lane == p) | (lane == q)
-        first = jnp.where(here, jnp.where(lane == p, -1.0, 0.0), first)
-        second = jnp.where(here, jnp.where(lane == q, -1.0, 0.0), second)
-        second = (second - ratio * first) * schur
-        first = first * invert - ratio * second
-        work = (
-            jnp.where(here, 0.0, work)
-            - work[:, p : p + 1] * first
-            - work[:, q : q + 1] * second
-        )
-        if at == 6:
+    for p in range(size):
+        at = p % 8
+        row = work[at : at + 1, :]
+        here = lane == p
+        factor = jnp.where(here, -1.0, row) / row[:, p : p + 1]
+        work = jnp.where(here, 0.0, work) - work[:, p : p + 1] * factor
+        if at == 7:
             work = work[8:]
     return work
 

time: 198 us -> 189 us (0.955)
  Pallas kernels: 39.4 us -> 31.1 us
    pallas_call x1, Pallas kernels: 12.8 us -> 5.59 us  [on_device(): pl.pallas_call(functools.partial(contract_body, nyhi, nz), out_shape=(f32...]
where the time goes in v6:
time: 189 us; the launch traced here: 188 us
  blocking collectives  67.3 us (36%)
  starting transfers between devices  51.8 us (27%)
  waiting for transfers between devices  36.9 us (20%)
  Pallas kernels  31.1 us (16%)
    all_to_all x3, blocking collectives, exchange(): return lax.all_to_all(blocks, axis, 0, 0, tiled=True)  67.3 us
    ppermute x6, starting transfers between devices, butterfly(): total += lax.ppermute(total, axis, [(i, i ^ step) for i in range(size)])  28.9 us
    all_to_all x3, starting transfers between devices, exchange(): return lax.all_to_all(blocks, axis, 0, 0, tiled=True)  22.9 us
    pallas_call x6, Pallas kernels, call(): pl.pallas_call(body, out_shape=outs, in_specs=[VMEM] * len(operands), out...  20.4 us
    ppermute x6, waiting for transfers between devices, butterfly(): total += lax.ppermute(total, axis, [(i, i ^ step) for i in range(size)])  19 us
    all_to_all x3, waiting for transfers between devices, exchange(): return lax.all_to_all(blocks, axis, 0, 0, tiled=True)  18 us
    pallas_call x1, Pallas kernels, on_device(): pl.pallas_call(functools.partial(contract_body, nyhi, nz), out_shape=(f32...  5.59 us
    pallas_call x1, Pallas kernels, on_device(): pl.pallas_call(functools.partial(partial_body, nyhi, nz), out_shape=f32(n...  5.07 us
  transfers between devices with their start and end apart: 9, of which 9 were waited for; matrix products, arithmetic and copies ran while one was open for 0% of the time, Pallas kernels for 3%

profile of v6, /device:TPU:8, one launch (start us, length us, event | category | flops | bytes accessed | tf_op | source)
XLA Modules:
  0.0 188.3 jit_solution(7152269919673449371)
XLA Ops:
  0.6 5.1 %shard_map.58 = f32[4,16,64,128]{3,2,1,0:T(8,128)} custom-call(f32[8,64]{1,0:T(8,128)} %bitcast.15, f32[16,64]{1,0:T(8,128)} %bitcast.11, f32[128,8192]{1,0:T(8,128)} %bitcast.13), custom_call_target="tpu_custom_call" | custom-call | tf_op jit(solution)/shard_map/pallas_call | solution.py:278
  5.7 0.0 copy-start.1
  5.7 4.4 %all-to-all-start = ((f32[4,16,64,128]{3,2,1,0:T(8,128)}), f32[4,16,64,128]{3,2,1,0:T(8,128)S(1)}, u32[]{:S(2)}, u32[]{:S(2)}) async-start(f32[4,16,64,128]{3,2,1,0:T(8,128)} %shard_map.58), calls=%async_computation | async-start | bytes 4194304 | tf_op jit(solution)/shard_map/all_to_all | solution.py:256
  10.1 0.0 copy-done.1
  10.1 0.2 fusion
  10.4 4.3 %collective-permute-start = (f32[64,64]{1,0:T(8,128)S(1)}, f32[64,64]{1,0:T(8,128)S(1)}, u32[]{:S(2)}, u32[]{:S(2)}) collective-permute-start(f32[64,64]{1,0:T(8,128)S(1)} %fusion), channel_id=1, source_target_pairs={{0,1},{1,0},{2,3},{3,2},{4,5},{5,4},{6,7},{7,6},{8,9},{9,8},{10,11... | collective-permute-start | bytes 49160 | tf_op jit(solution)/shard_map/ppermute | solution.py:263
  14.7 1.9 collective-permute-done
  16.5 6.1 %collective-permute-start.1 = (f32[64,64]{1,0:T(8,128)S(1)}, f32[64,64]{1,0:T(8,128)S(1)}, u32[]{:S(2)}, u32[]{:S(2)}) collective-permute-start(f32[64,64]{1,0:T(8,128)S(1)} %add.18), channel_id=1, source_target_pairs={{0,2},{1,3},{2,0},{3,1},{4,6},{5,7},{6,4},{7,5},{8,10},{9,11},{10,... | collective-permute-start | bytes 49160 | tf_op jit(solution)/shard_map/ppermute | solution.py:263
  22.6 1.9 collective-permute-done.1
  24.5 9.3 %collective-permute-start.2 = (f32[64,64]{1,0:T(8,128)S(1)}, f32[64,64]{1,0:T(8,128)S(1)}, u32[]{:S(2)}, u32[]{:S(2)}) collective-permute-start(f32[64,64]{1,0:T(8,128)S(1)} %add.19), channel_id=1, source_target_pairs={{0,4},{1,5},{2,6},{3,7},{4,0},{5,1},{6,2},{7,3},{8,12},{9,13},{10,... | collective-permute-start | bytes 49160 | tf_op jit(solution)/shard_map/ppermute | solution.py:263
  33.8 1.9 %collective-permute-done.2 = f32[64,64]{1,0:T(8,128)S(1)} collective-permute-done((f32[64,64]{1,0:T(8,128)S(1)}, f32[64,64]{1,0:T(8,128)S(1)}, u32[]{:S(2)}, u32[]{:S(2)}) %collective-permute-start.2) | collective-permute-done | bytes 16416 | tf_op jit(solution)/shard_map/ppermute | solution.py:263
  35.7 0.7 all-to-all-done.got_ref
  36.5 0.9 shard_map.59
  37.4 14.8 %all-to-all-start.1 = ((f32[16,64,128]{2,1,0:T(8,128)}), f32[16,64,128]{2,1,0:T(8,128)S(1)}, u32[]{:S(2)}, u32[]{:S(2)}) async-start(f32[16,64,128]{2,1,0:T(8,128)} %get-tuple-element.18), calls=%async_computation.1 | async-start | bytes 1048576 | tf_op jit(solution)/shard_map/all_to_all | solution.py:256
  52.1 2.5 %collective-permute-start.3 = (f32[64,64]{1,0:T(8,128)S(1)}, f32[64,64]{1,0:T(8,128)S(1)}, u32[]{:S(2)}, u32[]{:S(2)}) collective-permute-start(f32[64,64]{1,0:T(8,128)S(1)} %get-tuple-element.19), channel_id=1, source_target_pairs={{0,16},{16,0},{32,48},{48,32},{1,17},{17,1},{33,49},{49,33},{2,18}... | collective-permute-start | bytes 49160 | tf_op jit(solution)/shard_map/ppermute | solution.py:263
  54.6 3.3 %collective-permute-done.3 = f32[64,64]{1,0:T(8,128)S(1)} collective-permute-done((f32[64,64]{1,0:T(8,128)S(1)}, f32[64,64]{1,0:T(8,128)S(1)}, u32[]{:S(2)}, u32[]{:S(2)}) %collective-permute-start.3) | collective-permute-done | bytes 16416 | tf_op jit(solution)/shard_map/ppermute | solution.py:263
  58.0 2.5 %collective-permute-start.4 = (f32[64,64]{1,0:T(8,128)S(1)}, f32[64,64]{1,0:T(8,128)S(1)}, u32[]{:S(2)}, u32[]{:S(2)}) collective-permute-start(f32[64,64]{1,0:T(8,128)S(1)} %add.21), channel_id=1, source_target_pairs={{0,32},{16,48},{32,0},{48,16},{1,33},{17,49},{33,1},{49,17},{2,34}... | collective-permute-start | bytes 49160 | tf_op jit(solution)/shard_map/ppermute | solution.py:263
  60.5 4.8 %collective-permute-done.4 = f32[64,64]{1,0:T(8,128)S(1)} collective-permute-done((f32[64,64]{1,0:T(8,128)S(1)}, f32[64,64]{1,0:T(8,128)S(1)}, u32[]{:S(2)}, u32[]{:S(2)}) %collective-permute-start.4) | collective-permute-done | bytes 16416 | tf_op jit(solution)/shard_map/ppermute | solution.py:263
  65.3 7.7 %all-to-all-done.1.got_ref = f32[16,64,128]{2,1,0:T(8,128)S(1)} async-done(((f32[16,64,128]{2,1,0:T(8,128)}), f32[16,64,128]{2,1,0:T(8,128)S(1)}, u32[]{:S(2)}, u32[]{:S(2)}) %all-to-all-start.1) | async-done | bytes 524320 | tf_op jit(solution)/shard_map/all_to_all | solution.py:256
  73.0 0.1 shard_map.60
  73.1 23.7 %all_to_all.30.got_ref = f32[16,64,128]{2,1,0:T(8,128)S(1)} all-to-all(f32[16,64,128]{2,1,0:T(8,128)S(1)} %get-tuple-element.20), channel_id=1, replica_groups=mesh['ylo'=4,'core'=2,'x'=4,'yhi'=2,'z'=8] {'z','yhi'}, dimensions={0} | all-to-all | bytes 1048576 | tf_op jit(solution)/shard_map/all_to_all | solution.py:256
  96.8 1.5 shard_map.61
  98.2 0.0 copy-start
  98.2 3.7 %all-to-all-start.3 = ((f32[4,16,64,128]{3,2,1,0:T(8,128)}), f32[4,16,64,128]{3,2,1,0:T(8,128)S(1)}, u32[]{:S(2)}, u32[]{:S(2)}) async-start(f32[4,16,64,128]{3,2,1,0:T(8,128)} %get-tuple-element.24), calls=%async_computation.3 | async-start | bytes 4194304 | tf_op jit(solution)/shard_map/all_to_all | solution.py:256
  102.0 4.2 %collective-permute-start.5 = (f32[64,64]{1,0:T(8,128)S(1)}, f32[64,64]{1,0:T(8,128)S(1)}, u32[]{:S(2)}, u32[]{:S(2)}) collective-permute-start(f32[64,64]{1,0:T(8,128)S(1)} %get-tuple-element.22), channel_id=1, source_target_pairs={{0,8},{8,0},{1,9},{9,1},{2,10},{10,2},{3,11},{11,3},{4,12},{12,4},... | collective-permute-start | bytes 49160 | tf_op jit(solution)/shard_map/ppermute | solution.py:263
  106.2 0.0 copy-done
  106.3 0.2 fusion.1.gram_c_ref
  106.5 5.2 %collective-permute-done.5 = f32[64,64]{1,0:T(8,128)S(1)} collective-permute-done((f32[64,64]{1,0:T(8,128)S(1)}, f32[64,64]{1,0:T(8,128)S(1)}, u32[]{:S(2)}, u32[]{:S(2)}) %collective-permute-start.5) | collective-permute-done | bytes 16416 | tf_op jit(solution)/shard_map/ppermute | solution.py:263
  111.7 5.4 %shard_map.62.inverse_ref = f32[64,64]{1,0:T(8,128)S(1)} custom-call(f32[64,64]{1,0:T(8,128)S(1)} %add.23.gram_b_ref, f32[64,64]{1,0:T(8,128)S(1)} %fusion.1.gram_c_ref), custom_call_target="tpu_custom_call" | custom-call | tf_op jit(solution)/shard_map/pallas_call | solution.py:29
  117.1 9.5 %all-to-all-done.3 = f32[4,16,64,128]{3,2,1,0:T(8,128)S(1)} async-done(((f32[4,16,64,128]{3,2,1,0:T(8,128)}), f32[4,16,64,128]{3,2,1,0:T(8,128)S(1)}, u32[]{:S(2)}, u32[]{:S(2)}) %all-to-all-start.3) | async-done | bytes 2097184 | tf_op jit(solution)/shard_map/all_to_all | solution.py:256
  126.6 5.6 %shard_map.63 = (f32[8,96,128]{2,1,0:T(8,128)S(1)}, f32[64,128]{1,0:T(8,128)S(1)}) custom-call(f32[64,64]{1,0:T(8,128)S(1)} %shard_map.62.inverse_ref, f32[64,128]{1,0:T(8,128)S(1)} %get-tuple-element.23.own_ref, f32[128,8192]{1,0:T(8,128)} %bitcast.14, f32[64,64,128]{2,1,0:T(8,128)S(1)} %bitcast.10), custom_call_target="tpu_custom_call" | custom-call | tf_op jit(solution)/shard_map/pallas_call | solution.py:312
  132.2 13.8 %all_to_all.31.got_ref = f32[8,96,128]{2,1,0:T(8,128)S(1)} all-to-all(f32[8,96,128]{2,1,0:T(8,128)S(1)} %get-tuple-element.25), channel_id=1, replica_groups=mesh['ylo'=4,'core'=2,'x'=4,'yhi'=2,'z'=8] {'ylo','core'}, dimensions={0} | all-to-all | bytes 786432 | tf_op jit(solution)/shard_map/all_to_all | solution.py:256
  146.0 6.2 %shard_map.64 = (f32[64,16,128]{2,1,0:T(8,128)S(1)}, f32[8,64]{1,0:T(8,128)S(1)}, f32[64,64]{1,0:T(8,128)S(1)}, f32[64,128]{1,0:T(8,128)}) custom-call(f32[8,96,128]{2,1,0:T(8,128)S(1)} %all_to_all.31.got_ref, f32[64,64]{1,0:T(8,128)S(1)} %fusion.1.gram_c_ref, f32[16,64]{1,0:T(8,128)S(1)} %bitcast.12, f32[64,128]{1,0:T(8,128)S(1)} %get-tuple-element.26.own_ref), custom_call_target="tpu_custom_call" | custom-call | tf_op jit(solution)/shard_map/pallas_call | solution.py:29
  152.2 29.7 %all_to_all.32.got_ref = f32[64,16,128]{2,1,0:T(8,128)S(1)} all-to-all(f32[64,16,128]{2,1,0:T(8,128)S(1)} %get-tuple-element.28), channel_id=1, replica_groups=mesh['ylo'=4,'core'=2,'x'=4,'yhi'=2,'z'=8] {'x','yhi','z'}, dimensions={0} | all-to-all | bytes 1048576 | tf_op jit(solution)/shard_map/all_to_all | solution.py:256
  181.9 6.4 %shard_map.65 = (f32[8,64]{1,0:T(8,128)}, f32[16,64]{1,0:T(8,128)}) custom-call(f32[64,16,128]{2,1,0:T(8,128)S(1)} %all_to_all.32.got_ref, f32[8,64]{1,0:T(8,128)S(1)} %get-tuple-element.29.raw_ref, f32[64,64]{1,0:T(8,128)S(1)} %get-tuple-element.30.gram_ref), custom_call_target="tpu_custom_call" | custom-call | tf_op jit(solution)/shard_map/pallas_call | solution.py:29
  (6 shorter events, 0.0 us)
Async XLA Ops:
  5.7 4.4 %copy-start.1 = (f32[64,8]{0,1:T(8,128)S(1)}, f32[64,8]{0,1:T(8,128)}, u32[]{:S(2)}) copy-start(f32[64,8]{0,1:T(8,128)} %param.4) | copy-start | bytes 6148
  5.7 30.8 %all-to-all-start = ((f32[4,16,64,128]{3,2,1,0:T(8,128)}), f32[4,16,64,128]{3,2,1,0:T(8,128)S(1)}, u32[]{:S(2)}, u32[]{:S(2)}) async-start(f32[4,16,64,128]{3,2,1,0:T(8,128)} %shard_map.58), calls=%async_computation | async-start | bytes 4194304 | tf_op jit(solution)/shard_map/all_to_all | solution.py:256
  10.4 6.2 %collective-permute-start = (f32[64,64]{1,0:T(8,128)S(1)}, f32[64,64]{1,0:T(8,128)S(1)}, u32[]{:S(2)}, u32[]{:S(2)}) collective-permute-start(f32[64,64]{1,0:T(8,128)S(1)} %fusion), channel_id=1, source_target_pairs={{0,1},{1,0},{2,3},{3,2},{4,5},{5,4},{6,7},{7,6},{8,9},{9,8},{10,11... | collective-permute-start | bytes 49160 | tf_op jit(solution)/shard_map/ppermute | solution.py:263
  16.5 8.0 %collective-permute-start.1 = (f32[64,64]{1,0:T(8,128)S(1)}, f32[64,64]{1,0:T(8,128)S(1)}, u32[]{:S(2)}, u32[]{:S(2)}) collective-permute-start(f32[64,64]{1,0:T(8,128)S(1)} %add.18), channel_id=1, source_target_pairs={{0,2},{1,3},{2,0},{3,1},{4,6},{5,7},{6,4},{7,5},{8,10},{9,11},{10,... | collective-permute-start | bytes 49160 | tf_op jit(solution)/shard_map/ppermute | solution.py:263
  24.5 11.2 %collective-permute-start.2 = (f32[64,64]{1,0:T(8,128)S(1)}, f32[64,64]{1,0:T(8,128)S(1)}, u32[]{:S(2)}, u32[]{:S(2)}) collective-permute-start(f32[64,64]{1,0:T(8,128)S(1)} %add.19), channel_id=1, source_target_pairs={{0,4},{1,5},{2,6},{3,7},{4,0},{5,1},{6,2},{7,3},{8,12},{9,13},{10,... | collective-permute-start | bytes 49160 | tf_op jit(solution)/shard_map/ppermute | solution.py:263
  37.4 35.6 %all-to-all-start.1 = ((f32[16,64,128]{2,1,0:T(8,128)}), f32[16,64,128]{2,1,0:T(8,128)S(1)}, u32[]{:S(2)}, u32[]{:S(2)}) async-start(f32[16,64,128]{2,1,0:T(8,128)} %get-tuple-element.18), calls=%async_computation.1 | async-start | bytes 1048576 | tf_op jit(solution)/shard_map/all_to_all | solution.py:256
  52.1 5.8 %collective-permute-start.3 = (f32[64,64]{1,0:T(8,128)S(1)}, f32[64,64]{1,0:T(8,128)S(1)}, u32[]{:S(2)}, u32[]{:S(2)}) collective-permute-start(f32[64,64]{1,0:T(8,128)S(1)} %get-tuple-element.19), channel_id=1, source_target_pairs={{0,16},{16,0},{32,48},{48,32},{1,17},{17,1},{33,49},{49,33},{2,18}... | collective-permute-start | bytes 49160 | tf_op jit(solution)/shard_map/ppermute | solution.py:263
  58.0 7.3 %collective-permute-start.4 = (f32[64,64]{1,0:T(8,128)S(1)}, f32[64,64]{1,0:T(8,128)S(1)}, u32[]{:S(2)}, u32[]{:S(2)}) collective-permute-start(f32[64,64]{1,0:T(8,128)S(1)} %add.21), channel_id=1, source_target_pairs={{0,32},{16,48},{32,0},{48,16},{1,33},{17,49},{33,1},{49,17},{2,34}... | collective-permute-start | bytes 49160 | tf_op jit(solution)/shard_map/ppermute | solution.py:263
  98.2 8.0 %copy-start = (f32[64,16]{0,1:T(8,128)S(1)}, f32[64,16]{0,1:T(8,128)}, u32[]{:S(2)}) copy-start(f32[64,16]{0,1:T(8,128)} %param.5) | copy-start | bytes 12292
  98.2 28.3 %all-to-all-start.3 = ((f32[4,16,64,128]{3,2,1,0:T(8,128)}), f32[4,16,64,128]{3,2,1,0:T(8,128)S(1)}, u32[]{:S(2)}, u32[]{:S(2)}) async-start(f32[4,16,64,128]{3,2,1,0:T(8,128)} %get-tuple-element.24), calls=%async_computation.3 | async-start | bytes 4194304 | tf_op jit(solution)/shard_map/all_to_all | solution.py:256
  102.0 9.7 %collective-permute-start.5 = (f32[64,64]{1,0:T(8,128)S(1)}, f32[64,64]{1,0:T(8,128)S(1)}, u32[]{:S(2)}, u32[]{:S(2)}) collective-permute-start(f32[64,64]{1,0:T(8,128)S(1)} %get-tuple-element.22), channel_id=1, source_target_pairs={{0,8},{8,0},{1,9},{9,1},{2,10},{10,2},{3,11},{11,3},{4,12},{12,4},... | collective-permute-start | bytes 49160 | tf_op jit(solution)/shard_map/ppermute | solution.py:263

commit v7 on v6

--- a/solution.py
+++ b/solution.py
@@ -47,21 +47,28 @@
     )
 
 
-def partial_body(nyhi, nz, nights_ref, spans_ref, x_ref, out_ref, kron_ref):
-    nights, intervals = nights_ref.shape[0], spans_ref.shape[0]
-    share = x_ref.shape[1] // (nyhi * nz)
-
-    @pl.when(pl.program_id(0) == 0)
-    def _():
-        columns = nights * intervals
-        kron_ref[...] = transposed_dot(
-            nights_ref[...], onehot(nights, columns, lambda j, c: c // intervals == j)
-        ) * transposed_dot(
-            spans_ref[...], onehot(intervals, columns, lambda k, c: c % intervals == k)
-        )
-
-    high, low = split(kron_ref[...])
-    rank = kron_ref.shape[0]
+def partial_body(
+    nyhi, nz, nights_ref, spans_ref, x_ref, out_ref, held_ref, made_ref, in_sems, out_sems
+):
+    nights, rank = nights_ref.shape
+    intervals = spans_ref.shape[0]
+    share = out_ref.shape[-1]
+    groups, width = held_ref.shape[0], nz * share
+    arrivals = [
+        pltpu.make_async_copy(
+            x_ref.at[:, pl.ds(group * width, width)], held_ref.at[group], in_sems.at[group]
+        )
+        for group in range(groups)
+    ]
+    for copy in arrivals:
+        copy.start()
+    columns = nights * intervals
+    kron = transposed_dot(
+        nights_ref[...], onehot(nights, columns, lambda j, c: c // intervals == j)
+    ) * transposed_dot(
+        spans_ref[...], onehot(intervals, columns, lambda k, c: c % intervals == k)
+    )
+    high, low = split(kron)
     left = jnp.concatenate(
         [
             jnp.concatenate([high, high], axis=1),
@@ -69,14 +76,21 @@
         ],
         axis=0,
     )
-    for y in range(nyhi):
-        right = jnp.concatenate(
-            split(x_ref[:, y * nz * share : (y + 1) * nz * share]), axis=0
-        )
+    departures = []
+    for group in range(groups):
+        x, y = group // nyhi, group % nyhi
+        arrivals[group].wait()
+        right = jnp.concatenate(split(held_ref[group]), axis=0)
         product = jnp.dot(left, right, preferred_element_type=jnp.float32)
         product = product[:rank] + product[rank:]
         for z in range(nz):
-            out_ref[0, z * nyhi + y] = product[:, z * share : (z + 1) * share]
+            made_ref[x, z * nyhi + y] = product[:, z * share : (z + 1) * share]
+        if y == nyhi - 1:
+            copy = pltpu.make_async_copy(made_ref.at[x], out_ref.at[x], out_sems.at[x])
+            copy.start()
+            departures.append(copy)
+    for copy in departures:
+        copy.wait()
 
 
 def inverse_body(gram_b_ref, gram_c_ref, out_ref):
@@ -174,17 +188,39 @@
 
 
 def right_divide(gram, right):
-    size = gram.shape[0]
+    size, block = gram.shape[0], 8
     work = jnp.concatenate([gram, right], axis=0)
     lane = lax.broadcasted_iota(jnp.int32, (1, size), 1)
-    for p in range(size):
-        at = p % 8
-        row = work[at : at + 1, :]
-        here = lane == p
-        factor = jnp.where(here, -1.0, row) / row[:, p : p + 1]
-        work = jnp.where(here, 0.0, work) - work[:, p : p + 1] * factor
-        if at == 7:
-            work = work[8:]
+    for p in range(0, size, block):
+        rows = [work[i : i + 1, :] for i in range(block)]
+        d = {
+            (i, j): jnp.broadcast_to(rows[i][:, p + j : p + j + 1], (1, size))
+            for i in range(block)
+            for j in range(i, block)
+        }
+        here = (lane >= p) & (lane < p + block)
+        y = [
+            jnp.where(here, jnp.where(lane == p + i, -1.0, 0.0), rows[i])
+            for i in range(block)
+        ]
+        inverse, low = [], {}
+        for i in range(block):
+            inverse.append(1.0 / d[i, i])
+            for j in range(i + 1, block):
+                low[j, i] = d[i, j] * inverse[i]
+            for j in range(i + 1, block):
+                for k in range(j, block):
+                    d[j, k] -= low[j, i] * d[i, k]
+                y[j] -= low[j, i] * y[i]
+        factors = [None] * block
+        for i in reversed(range(block)):
+            factors[i] = y[i] * inverse[i]
+            for j in range(i + 1, block):
+                factors[i] -= low[j, i] * factors[j]
+        rest = work[block:]
+        work = jnp.where(here, 0.0, rest)
+        for i in range(block):
+            work -= rest[:, p + i : p + i + 1] * factors[i]
     return work
 
 
@@ -275,17 +311,20 @@
     x2 = readings.reshape(nights * intervals, meters)
     gram_c = jnp.dot(spans, spans.T, precision=FULL)
     places = nyhi * nz
+    groups = nx * nyhi
+    anywhere = pl.BlockSpec(memory_space=pl.ANY)
+    held = pltpu.VMEM((groups, nights * intervals, nz * share), jnp.float32)
     blocks = pl.pallas_call(
         functools.partial(partial_body, nyhi, nz),
         out_shape=f32(nx, places, rank, share),
-        grid=(nx,),
-        in_specs=[
-            pl.BlockSpec((nights, rank), lambda i: (0, 0)),
-            pl.BlockSpec((intervals, rank), lambda i: (0, 0)),
-            pl.BlockSpec((nights * intervals, places * share), lambda i: (0, i)),
+        in_specs=[VMEM, VMEM, anywhere],
+        out_specs=anywhere,
+        scratch_shapes=[
+            held,
+            pltpu.VMEM((nx, places, rank, share), jnp.float32),
+            pltpu.SemaphoreType.DMA((groups,)),
+            pltpu.SemaphoreType.DMA((nx,)),
         ],
-        out_specs=pl.BlockSpec((1, places, rank, share), lambda i: (i, 0, 0, 0)),
-        scratch_shapes=[pltpu.VMEM((rank, nights * intervals), jnp.float32)],
         compiler_params=STREAM,
     )(evenings.T, spans.T, x2)
 
@@ -308,16 +347,12 @@
     inverse = call(inverse_body, square, gram_b, gram_c)
     full = exchange(send, "x").reshape(night_devices, rank, share)
 
-    groups = nx * nyhi
     packed, own_raw = pl.pallas_call(
         functools.partial(contract_body, nyhi, nz),
         out_shape=(f32(copies, (nights * intervals + rank) // 2, 2 * rank), f32(rank, share)),
-        in_specs=[VMEM, VMEM, pl.BlockSpec(memory_space=pl.ANY), VMEM],
+        in_specs=[VMEM, VMEM, anywhere, VMEM],
         out_specs=(VMEM, VMEM),
-        scratch_shapes=[
-            pltpu.VMEM((groups, nights * intervals, nz * share), jnp.float32),
-            pltpu.SemaphoreType.DMA((groups,)),
-        ],
+        scratch_shapes=[held, pltpu.SemaphoreType.DMA((groups,))],
         compiler_params=CONTRACT,
     )(inverse, own, x2, full)
     send, raw, gram_a, own_columns = call(

time: 189 us -> 183 us (0.968)
  Pallas kernels: 31.1 us -> 20.7 us
  waiting for transfers between devices: 36.9 us -> 40.8 us
    pallas_call x6, Pallas kernels: 20.4 us -> 10.5 us  [call(): pl.pallas_call(body, out_shape=outs, in_specs=[VMEM] * len(operands), out...]
    all_to_all x3, waiting for transfers between devices: 18 us -> 21.7 us  [exchange(): return lax.all_to_all(blocks, axis, 0, 0, tiled=True)]
  transfers between devices with their start and end apart: 9 -> 9, of which waited for: 9 -> 9; matrix products, arithmetic and copies ran while one was open for 0% -> 0% of each run, Pallas kernels for 3% -> 1%
where the time goes in v7:
time: 183 us; the launch traced here: 182 us
  blocking collectives  67.4 us (37%)
  starting transfers between devices  51.6 us (28%)
  waiting for transfers between devices  40.8 us (22%)
  Pallas kernels  20.7 us (11%)
    all_to_all x3, blocking collectives, exchange(): return lax.all_to_all(blocks, axis, 0, 0, tiled=True)  67.4 us
    ppermute x6, starting transfers between devices, butterfly(): total += lax.ppermute(total, axis, [(i, i ^ step) for i in range(size)])  28.7 us
    all_to_all x3, starting transfers between devices, exchange(): return lax.all_to_all(blocks, axis, 0, 0, tiled=True)  22.8 us
    all_to_all x3, waiting for transfers between devices, exchange(): return lax.all_to_all(blocks, axis, 0, 0, tiled=True)  21.7 us
    ppermute x6, waiting for transfers between devices, butterfly(): total += lax.ppermute(total, axis, [(i, i ^ step) for i in range(size)])  19.1 us
    pallas_call x6, Pallas kernels, call(): pl.pallas_call(body, out_shape=outs, in_specs=[VMEM] * len(operands), out...  10.5 us
    pallas_call x1, Pallas kernels, on_device(): pl.pallas_call(functools.partial(contract_body, nyhi, nz), out_shape=(f32...  5.59 us
    pallas_call x1, Pallas kernels, on_device(): pl.pallas_call(functools.partial(partial_body, nyhi, nz), out_shape=f32(n...  4.59 us
  transfers between devices with their start and end apart: 9, of which 9 were waited for; matrix products, arithmetic and copies ran while one was open for 0% of the time, Pallas kernels for 1%

profile of v7, /device:TPU:8, one launch (start us, length us, event | category | flops | bytes accessed | tf_op | source)
XLA Modules:
  0.0 181.8 jit_solution(12414312419564281387)
XLA Ops:
  0.6 4.6 %shard_map.58 = f32[4,16,64,128]{3,2,1,0:T(8,128)} custom-call(f32[8,64]{1,0:T(8,128)} %bitcast.15, f32[16,64]{1,0:T(8,128)} %bitcast.11, f32[128,8192]{1,0:T(8,128)} %bitcast.13), custom_call_target="tpu_custom_call" | custom-call | tf_op jit(solution)/shard_map/pallas_call | solution.py:317
  5.2 0.0 copy-start.1
  5.2 4.3 %all-to-all-start = ((f32[4,16,64,128]{3,2,1,0:T(8,128)}), f32[4,16,64,128]{3,2,1,0:T(8,128)S(1)}, u32[]{:S(2)}, u32[]{:S(2)}) async-start(f32[4,16,64,128]{3,2,1,0:T(8,128)} %shard_map.58), calls=%async_computation | async-start | bytes 4194304 | tf_op jit(solution)/shard_map/all_to_all | solution.py:292
  9.5 0.0 copy-done.1
  9.6 0.2 fusion
  9.8 4.3 %collective-permute-start = (f32[64,64]{1,0:T(8,128)S(1)}, f32[64,64]{1,0:T(8,128)S(1)}, u32[]{:S(2)}, u32[]{:S(2)}) collective-permute-start(f32[64,64]{1,0:T(8,128)S(1)} %fusion), channel_id=1, source_target_pairs={{0,1},{1,0},{2,3},{3,2},{4,5},{5,4},{6,7},{7,6},{8,9},{9,8},{10,11... | collective-permute-start | bytes 49160 | tf_op jit(solution)/shard_map/ppermute | solution.py:299
  14.1 1.9 %collective-permute-done = f32[64,64]{1,0:T(8,128)S(1)} collective-permute-done((f32[64,64]{1,0:T(8,128)S(1)}, f32[64,64]{1,0:T(8,128)S(1)}, u32[]{:S(2)}, u32[]{:S(2)}) %collective-permute-start) | collective-permute-done | bytes 16416 | tf_op jit(solution)/shard_map/ppermute | solution.py:299
  16.0 6.1 %collective-permute-start.1 = (f32[64,64]{1,0:T(8,128)S(1)}, f32[64,64]{1,0:T(8,128)S(1)}, u32[]{:S(2)}, u32[]{:S(2)}) collective-permute-start(f32[64,64]{1,0:T(8,128)S(1)} %add.18), channel_id=1, source_target_pairs={{0,2},{1,3},{2,0},{3,1},{4,6},{5,7},{6,4},{7,5},{8,10},{9,11},{10,... | collective-permute-start | bytes 49160 | tf_op jit(solution)/shard_map/ppermute | solution.py:299
  22.0 1.9 %collective-permute-done.1 = f32[64,64]{1,0:T(8,128)S(1)} collective-permute-done((f32[64,64]{1,0:T(8,128)S(1)}, f32[64,64]{1,0:T(8,128)S(1)}, u32[]{:S(2)}, u32[]{:S(2)}) %collective-permute-start.1) | collective-permute-done | bytes 16416 | tf_op jit(solution)/shard_map/ppermute | solution.py:299
  23.9 9.3 %collective-permute-start.2 = (f32[64,64]{1,0:T(8,128)S(1)}, f32[64,64]{1,0:T(8,128)S(1)}, u32[]{:S(2)}, u32[]{:S(2)}) collective-permute-start(f32[64,64]{1,0:T(8,128)S(1)} %add.19), channel_id=1, source_target_pairs={{0,4},{1,5},{2,6},{3,7},{4,0},{5,1},{6,2},{7,3},{8,12},{9,13},{10,... | collective-permute-start | bytes 49160 | tf_op jit(solution)/shard_map/ppermute | solution.py:299
  33.2 1.9 %collective-permute-done.2 = f32[64,64]{1,0:T(8,128)S(1)} collective-permute-done((f32[64,64]{1,0:T(8,128)S(1)}, f32[64,64]{1,0:T(8,128)S(1)}, u32[]{:S(2)}, u32[]{:S(2)}) %collective-permute-start.2) | collective-permute-done | bytes 16416 | tf_op jit(solution)/shard_map/ppermute | solution.py:299
  35.1 0.7 all-to-all-done.got_ref
  35.9 0.9 shard_map.59
  36.8 14.8 %all-to-all-start.1 = ((f32[16,64,128]{2,1,0:T(8,128)}), f32[16,64,128]{2,1,0:T(8,128)S(1)}, u32[]{:S(2)}, u32[]{:S(2)}) async-start(f32[16,64,128]{2,1,0:T(8,128)} %get-tuple-element.18), calls=%async_computation.1 | async-start | bytes 1048576 | tf_op jit(solution)/shard_map/all_to_all | solution.py:292
  51.6 2.5 %collective-permute-start.3 = (f32[64,64]{1,0:T(8,128)S(1)}, f32[64,64]{1,0:T(8,128)S(1)}, u32[]{:S(2)}, u32[]{:S(2)}) collective-permute-start(f32[64,64]{1,0:T(8,128)S(1)} %get-tuple-element.19), channel_id=1, source_target_pairs={{0,16},{16,0},{32,48},{48,32},{1,17},{17,1},{33,49},{49,33},{2,18}... | collective-permute-start | bytes 49160 | tf_op jit(solution)/shard_map/ppermute | solution.py:299
  54.1 3.3 %collective-permute-done.3 = f32[64,64]{1,0:T(8,128)S(1)} collective-permute-done((f32[64,64]{1,0:T(8,128)S(1)}, f32[64,64]{1,0:T(8,128)S(1)}, u32[]{:S(2)}, u32[]{:S(2)}) %collective-permute-start.3) | collective-permute-done | bytes 16416 | tf_op jit(solution)/shard_map/ppermute | solution.py:299
  57.4 2.5 %collective-permute-start.4 = (f32[64,64]{1,0:T(8,128)S(1)}, f32[64,64]{1,0:T(8,128)S(1)}, u32[]{:S(2)}, u32[]{:S(2)}) collective-permute-start(f32[64,64]{1,0:T(8,128)S(1)} %add.21), channel_id=1, source_target_pairs={{0,32},{16,48},{32,0},{48,16},{1,33},{17,49},{33,1},{49,17},{2,34}... | collective-permute-start | bytes 49160 | tf_op jit(solution)/shard_map/ppermute | solution.py:299
  59.9 4.8 %collective-permute-done.4 = f32[64,64]{1,0:T(8,128)S(1)} collective-permute-done((f32[64,64]{1,0:T(8,128)S(1)}, f32[64,64]{1,0:T(8,128)S(1)}, u32[]{:S(2)}, u32[]{:S(2)}) %collective-permute-start.4) | collective-permute-done | bytes 16416 | tf_op jit(solution)/shard_map/ppermute | solution.py:299
  64.7 7.8 %all-to-all-done.1.got_ref = f32[16,64,128]{2,1,0:T(8,128)S(1)} async-done(((f32[16,64,128]{2,1,0:T(8,128)}), f32[16,64,128]{2,1,0:T(8,128)S(1)}, u32[]{:S(2)}, u32[]{:S(2)}) %all-to-all-start.1) | async-done | bytes 524320 | tf_op jit(solution)/shard_map/all_to_all | solution.py:292
  72.5 0.1 shard_map.60
  72.6 23.6 %all_to_all.30.got_ref = f32[16,64,128]{2,1,0:T(8,128)S(1)} all-to-all(f32[16,64,128]{2,1,0:T(8,128)S(1)} %get-tuple-element.20), channel_id=1, replica_groups=mesh['ylo'=4,'core'=2,'x'=4,'yhi'=2,'z'=8] {'z','yhi'}, dimensions={0} | all-to-all | bytes 1048576 | tf_op jit(solution)/shard_map/all_to_all | solution.py:292
  96.2 1.5 shard_map.61
  97.6 0.0 copy-start
  97.6 3.7 %all-to-all-start.3 = ((f32[4,16,64,128]{3,2,1,0:T(8,128)}), f32[4,16,64,128]{3,2,1,0:T(8,128)S(1)}, u32[]{:S(2)}, u32[]{:S(2)}) async-start(f32[4,16,64,128]{3,2,1,0:T(8,128)} %get-tuple-element.24), calls=%async_computation.3 | async-start | bytes 4194304 | tf_op jit(solution)/shard_map/all_to_all | solution.py:292
  101.4 4.1 %collective-permute-start.5 = (f32[64,64]{1,0:T(8,128)S(1)}, f32[64,64]{1,0:T(8,128)S(1)}, u32[]{:S(2)}, u32[]{:S(2)}) collective-permute-start(f32[64,64]{1,0:T(8,128)S(1)} %get-tuple-element.22), channel_id=1, source_target_pairs={{0,8},{8,0},{1,9},{9,1},{2,10},{10,2},{3,11},{11,3},{4,12},{12,4},... | collective-permute-start | bytes 49160 | tf_op jit(solution)/shard_map/ppermute | solution.py:299
  105.5 0.0 copy-done
  105.5 0.2 fusion.1.gram_c_ref
  105.7 5.3 %collective-permute-done.5 = f32[64,64]{1,0:T(8,128)S(1)} collective-permute-done((f32[64,64]{1,0:T(8,128)S(1)}, f32[64,64]{1,0:T(8,128)S(1)}, u32[]{:S(2)}, u32[]{:S(2)}) %collective-permute-start.5) | collective-permute-done | bytes 16416 | tf_op jit(solution)/shard_map/ppermute | solution.py:299
  111.1 1.7 shard_map.62.inverse_ref
  112.8 13.2 %all-to-all-done.3 = f32[4,16,64,128]{3,2,1,0:T(8,128)S(1)} async-done(((f32[4,16,64,128]{3,2,1,0:T(8,128)}), f32[4,16,64,128]{3,2,1,0:T(8,128)S(1)}, u32[]{:S(2)}, u32[]{:S(2)}) %all-to-all-start.3) | async-done | bytes 2097184 | tf_op jit(solution)/shard_map/all_to_all | solution.py:292
  125.9 5.6 %shard_map.63 = (f32[8,96,128]{2,1,0:T(8,128)S(1)}, f32[64,128]{1,0:T(8,128)S(1)}) custom-call(f32[64,64]{1,0:T(8,128)S(1)} %shard_map.62.inverse_ref, f32[64,128]{1,0:T(8,128)S(1)} %get-tuple-element.23.own_ref, f32[128,8192]{1,0:T(8,128)} %bitcast.14, f32[64,64,128]{2,1,0:T(8,128)S(1)} %bitcast.10), custom_call_target="tpu_custom_call" | custom-call | tf_op jit(solution)/shard_map/pallas_call | solution.py:350
  131.5 13.8 %all_to_all.31.got_ref = f32[8,96,128]{2,1,0:T(8,128)S(1)} all-to-all(f32[8,96,128]{2,1,0:T(8,128)S(1)} %get-tuple-element.25), channel_id=1, replica_groups=mesh['ylo'=4,'core'=2,'x'=4,'yhi'=2,'z'=8] {'ylo','core'}, dimensions={0} | all-to-all | bytes 786432 | tf_op jit(solution)/shard_map/all_to_all | solution.py:292
  145.4 3.0 %shard_map.64 = (f32[64,16,128]{2,1,0:T(8,128)S(1)}, f32[8,64]{1,0:T(8,128)S(1)}, f32[64,64]{1,0:T(8,128)S(1)}, f32[64,128]{1,0:T(8,128)}) custom-call(f32[8,96,128]{2,1,0:T(8,128)S(1)} %all_to_all.31.got_ref, f32[64,64]{1,0:T(8,128)S(1)} %fusion.1.gram_c_ref, f32[16,64]{1,0:T(8,128)S(1)} %bitcast.12, f32[64,128]{1,0:T(8,128)S(1)} %get-tuple-element.26.own_ref), custom_call_target="tpu_custom_call" | custom-call | tf_op jit(solution)/shard_map/pallas_call | solution.py:29
  148.4 30.0 %all_to_all.32.got_ref = f32[64,16,128]{2,1,0:T(8,128)S(1)} all-to-all(f32[64,16,128]{2,1,0:T(8,128)S(1)} %get-tuple-element.28), channel_id=1, replica_groups=mesh['ylo'=4,'core'=2,'x'=4,'yhi'=2,'z'=8] {'x','yhi','z'}, dimensions={0} | all-to-all | bytes 1048576 | tf_op jit(solution)/shard_map/all_to_all | solution.py:292
  178.4 3.4 %shard_map.65 = (f32[8,64]{1,0:T(8,128)}, f32[16,64]{1,0:T(8,128)}) custom-call(f32[64,16,128]{2,1,0:T(8,128)S(1)} %all_to_all.32.got_ref, f32[8,64]{1,0:T(8,128)S(1)} %get-tuple-element.29.raw_ref, f32[64,64]{1,0:T(8,128)S(1)} %get-tuple-element.30.gram_ref), custom_call_target="tpu_custom_call" | custom-call | tf_op jit(solution)/shard_map/pallas_call | solution.py:29
  (6 shorter events, 0.0 us)
Async XLA Ops:
  5.2 4.3 %copy-start.1 = (f32[64,8]{0,1:T(8,128)S(1)}, f32[64,8]{0,1:T(8,128)}, u32[]{:S(2)}) copy-start(f32[64,8]{0,1:T(8,128)} %param.4) | copy-start | bytes 6148
  5.2 30.6 %all-to-all-start = ((f32[4,16,64,128]{3,2,1,0:T(8,128)}), f32[4,16,64,128]{3,2,1,0:T(8,128)S(1)}, u32[]{:S(2)}, u32[]{:S(2)}) async-start(f32[4,16,64,128]{3,2,1,0:T(8,128)} %shard_map.58), calls=%async_computation | async-start | bytes 4194304 | tf_op jit(solution)/shard_map/all_to_all | solution.py:292
  9.8 6.2 %collective-permute-start = (f32[64,64]{1,0:T(8,128)S(1)}, f32[64,64]{1,0:T(8,128)S(1)}, u32[]{:S(2)}, u32[]{:S(2)}) collective-permute-start(f32[64,64]{1,0:T(8,128)S(1)} %fusion), channel_id=1, source_target_pairs={{0,1},{1,0},{2,3},{3,2},{4,5},{5,4},{6,7},{7,6},{8,9},{9,8},{10,11... | collective-permute-start | bytes 49160 | tf_op jit(solution)/shard_map/ppermute | solution.py:299
  16.0 8.0 %collective-permute-start.1 = (f32[64,64]{1,0:T(8,128)S(1)}, f32[64,64]{1,0:T(8,128)S(1)}, u32[]{:S(2)}, u32[]{:S(2)}) collective-permute-start(f32[64,64]{1,0:T(8,128)S(1)} %add.18), channel_id=1, source_target_pairs={{0,2},{1,3},{2,0},{3,1},{4,6},{5,7},{6,4},{7,5},{8,10},{9,11},{10,... | collective-permute-start | bytes 49160 | tf_op jit(solution)/shard_map/ppermute | solution.py:299
  23.9 11.2 %collective-permute-start.2 = (f32[64,64]{1,0:T(8,128)S(1)}, f32[64,64]{1,0:T(8,128)S(1)}, u32[]{:S(2)}, u32[]{:S(2)}) collective-permute-start(f32[64,64]{1,0:T(8,128)S(1)} %add.19), channel_id=1, source_target_pairs={{0,4},{1,5},{2,6},{3,7},{4,0},{5,1},{6,2},{7,3},{8,12},{9,13},{10,... | collective-permute-start | bytes 49160 | tf_op jit(solution)/shard_map/ppermute | solution.py:299
  36.8 35.7 %all-to-all-start.1 = ((f32[16,64,128]{2,1,0:T(8,128)}), f32[16,64,128]{2,1,0:T(8,128)S(1)}, u32[]{:S(2)}, u32[]{:S(2)}) async-start(f32[16,64,128]{2,1,0:T(8,128)} %get-tuple-element.18), calls=%async_computation.1 | async-start | bytes 1048576 | tf_op jit(solution)/shard_map/all_to_all | solution.py:292
  51.6 5.8 %collective-permute-start.3 = (f32[64,64]{1,0:T(8,128)S(1)}, f32[64,64]{1,0:T(8,128)S(1)}, u32[]{:S(2)}, u32[]{:S(2)}) collective-permute-start(f32[64,64]{1,0:T(8,128)S(1)} %get-tuple-element.19), channel_id=1, source_target_pairs={{0,16},{16,0},{32,48},{48,32},{1,17},{17,1},{33,49},{49,33},{2,18}... | collective-permute-start | bytes 49160 | tf_op jit(solution)/shard_map/ppermute | solution.py:299
  57.4 7.3 %collective-permute-start.4 = (f32[64,64]{1,0:T(8,128)S(1)}, f32[64,64]{1,0:T(8,128)S(1)}, u32[]{:S(2)}, u32[]{:S(2)}) collective-permute-start(f32[64,64]{1,0:T(8,128)S(1)} %add.21), channel_id=1, source_target_pairs={{0,32},{16,48},{32,0},{48,16},{1,33},{17,49},{33,1},{49,17},{2,34}... | collective-permute-start | bytes 49160 | tf_op jit(solution)/shard_map/ppermute | solution.py:299
  97.6 7.9 %copy-start = (f32[64,16]{0,1:T(8,128)S(1)}, f32[64,16]{0,1:T(8,128)}, u32[]{:S(2)}) copy-start(f32[64,16]{0,1:T(8,128)} %param.5) | copy-start | bytes 12292
  97.6 28.3 %all-to-all-start.3 = ((f32[4,16,64,128]{3,2,1,0:T(8,128)}), f32[4,16,64,128]{3,2,1,0:T(8,128)S(1)}, u32[]{:S(2)}, u32[]{:S(2)}) async-start(f32[4,16,64,128]{3,2,1,0:T(8,128)} %get-tuple-element.24), calls=%async_computation.3 | async-start | bytes 4194304 | tf_op jit(solution)/shard_map/all_to_all | solution.py:292
  101.4 9.7 %collective-permute-start.5 = (f32[64,64]{1,0:T(8,128)S(1)}, f32[64,64]{1,0:T(8,128)S(1)}, u32[]{:S(2)}, u32[]{:S(2)}) collective-permute-start(f32[64,64]{1,0:T(8,128)S(1)} %get-tuple-element.22), channel_id=1, source_target_pairs={{0,8},{8,0},{1,9},{9,1},{2,10},{10,2},{3,11},{11,3},{4,12},{12,4},... | collective-permute-start | bytes 49160 | tf_op jit(solution)/shard_map/ppermute | solution.py:299

commit v8 on v7

--- a/solution.py
+++ b/solution.py
@@ -16,7 +16,6 @@
 SPLIT = {"ylo": 4, "core": 2, "x": 4, "yhi": 2, "z": 8}
 VMEM = pl.BlockSpec(memory_space=pltpu.VMEM)
 STREAM = pltpu.CompilerParams(vmem_limit_bytes=60 * 1024 * 1024)
-FAN = pltpu.CompilerParams(vmem_limit_bytes=52 * 1024 * 1024)
 CONTRACT = pltpu.CompilerParams(vmem_limit_bytes=50 * 1024 * 1024)
 PARAMS = pltpu.CompilerParams(vmem_limit_bytes=40 * 1024 * 1024)
 
@@ -117,10 +116,11 @@
     gram_out_ref[...] = gram_ref[...]
 
 
-def fan_body(got_ref, gram_ref, send_ref, gram_out_ref):
-    for k in range(send_ref.shape[0]):
-        send_ref[k] = got_ref[...]
-    gram_out_ref[...] = gram_ref[...]
+def relay_body(left_ref, right_ref, inverse_ref, first_ref, second_ref, inverse_out_ref):
+    half = first_ref.shape[0]
+    first_ref[...] = left_ref[:half]
+    second_ref[...] = right_ref[half:]
+    inverse_out_ref[...] = inverse_ref[...]
 
 
 def onehot(rows, columns, test):
@@ -134,36 +134,36 @@
     return onehot(size, size, lambda i, j: i == j)
 
 
-def contract_body(
-    nyhi, nz, inverse_ref, own_ref, x_ref, m_ref, out_ref, own_out_ref, held_ref, sems
-):
-    rank, share = m_ref.shape[1:]
-    rows = x_ref.shape[0]
-    copies = [
-        pltpu.make_async_copy(
-            x_ref.at[:, pl.ds(group * nz * share, nz * share)], held_ref.at[group], sems.at[group]
-        )
-        for group in range(held_ref.shape[0])
-    ]
+def contracted_blocks(nyhi, nz, place_ref, inverse, x_ref, chunks, held_ref, sems):
+    nx = place_ref[1]
+    rank, share = chunks[0][1][0].shape
+    rows, width = held_ref.shape[1:]
+    copies = []
+    for distance, _ in chunks:
+        x = lax.rem(place_ref[0] + distance, nx)
+        for y in range(nyhi):
+            start = pl.multiple_of((x * nyhi + y) * width, width)
+            at = len(copies)
+            copies.append(
+                pltpu.make_async_copy(
+                    x_ref.at[:, pl.ds(start, width)], held_ref.at[at], sems.at[at]
+                )
+            )
     for copy in copies:
         copy.start()
-    inverse = inverse_ref[...]
-    own_out_ref[...] = jnp.dot(
-        inverse, own_ref[...], precision=FULL, preferred_element_type=jnp.float32
-    )
     high, low = split(inverse)
     solver = jnp.concatenate([high, high, low], axis=1)
     loadings = []
-    for group in range(held_ref.shape[0]):
-        x, y = group // nyhi, group % nyhi
-        high, low = split(
-            jnp.concatenate([m_ref[(x * nz + z) * nyhi + y] for z in range(nz)], axis=1)
-        )
-        factor = jnp.dot(
-            solver, jnp.concatenate([high, low, high], axis=0),
-            preferred_element_type=jnp.float32,
-        )
-        loadings.append(split(factor))
+    for _, blocks in chunks:
+        for y in range(nyhi):
+            high, low = split(
+                jnp.concatenate([blocks[z * nyhi + y] for z in range(nz)], axis=1)
+            )
+            factor = jnp.dot(
+                solver, jnp.concatenate([high, low, high], axis=0),
+                preferred_element_type=jnp.float32,
+            )
+            loadings.append(split(factor))
     total = jnp.zeros((2 * (rows + rank), 2 * rank), jnp.float32)
     for group, (high, low) in enumerate(loadings):
         copies[group].wait()
@@ -174,7 +174,37 @@
             (((1,), (1,)), ((), ())), preferred_element_type=jnp.float32,
         )
     total = total[:, :rank] + total[:, rank:]
-    total = total[: rows + rank] + total[rows + rank :]
+    return total[: rows + rank] + total[rows + rank :]
+
+
+def near_body(
+    nyhi, nz, nx, place_ref, inverse_ref, x_ref, own_ref, left_ref, right_ref, total_ref,
+    held_ref, sems,
+):
+    places = own_ref.shape[0]
+    chunks = [
+        (distance, [ref[i] for i in range(places)])
+        for distance, ref in ((0, own_ref), (nx - 1, left_ref), (1, right_ref))
+    ]
+    total_ref[...] = contracted_blocks(
+        nyhi, nz, place_ref, inverse_ref[...], x_ref, chunks, held_ref, sems
+    )
+
+
+def far_body(
+    nyhi, nz, place_ref, inverse_ref, own_ref, x_ref, first_ref, second_ref, near_ref,
+    out_ref, own_out_ref, held_ref, sems,
+):
+    inverse = inverse_ref[...]
+    rank = inverse.shape[0]
+    own_out_ref[...] = jnp.dot(
+        inverse, own_ref[...], precision=FULL, preferred_element_type=jnp.float32
+    )
+    blocks = [ref[i] for ref in (first_ref, second_ref) for i in range(ref.shape[0])]
+    total = near_ref[...] + contracted_blocks(
+        nyhi, nz, place_ref, inverse, x_ref, [(2, blocks)], held_ref, sems
+    )
+    rows = total.shape[0] - rank
     half, quarter = rows // 2, rank // 2
     packed = jnp.concatenate(
         [
@@ -339,22 +369,43 @@
         own_body, (f32(rank, share), f32(places, rank, share), square),
         exchange(joined, ZY), gram_b,
     )
-    send, gram_b = call(
-        fan_body, (f32(nx, places, rank, share), square), exchange(send, ZY), gram_b,
-        params=FAN,
-    )
+    chunk = exchange(send, ZY)
     gram_b = butterfly(gram_b, "yhi")
     inverse = call(inverse_body, square, gram_b, gram_c)
-    full = exchange(send, "x").reshape(night_devices, rank, share)
-
+
+    up = [(i, (i + 1) % nx) for i in range(nx)]
+    down = [(i, (i - 1) % nx) for i in range(nx)]
+    left = lax.ppermute(chunk, "x", up)
+    right = lax.ppermute(chunk, "x", down)
+    part = f32(places // 2, rank, share)
+    first, second, inverse = call(relay_body, (part, part, square), left, right, inverse)
+    first = lax.ppermute(first, "x", up)
+    second = lax.ppermute(second, "x", down)
+    place = jnp.stack([lax.axis_index("x"), jnp.int32(nx)]).astype(jnp.int32)
+    smem = pl.BlockSpec(memory_space=pltpu.SMEM)
+
+    def parts(groups):
+        return [
+            pltpu.VMEM((groups, nights * intervals, nz * share), jnp.float32),
+            pltpu.SemaphoreType.DMA((groups,)),
+        ]
+
+    near = pl.pallas_call(
+        functools.partial(near_body, nyhi, nz, nx),
+        out_shape=f32(nights * intervals + rank, rank),
+        in_specs=[smem, VMEM, anywhere, VMEM, VMEM, VMEM],
+        out_specs=VMEM,
+        scratch_shapes=parts(3 * nyhi),
+        compiler_params=CONTRACT,
+    )(place, inverse, x2, chunk, left, right)
     packed, own_raw = pl.pallas_call(
-        functools.partial(contract_body, nyhi, nz),
+        functools.partial(far_body, nyhi, nz),
         out_shape=(f32(copies, (nights * intervals + rank) // 2, 2 * rank), f32(rank, share)),
-        in_specs=[VMEM, VMEM, anywhere, VMEM],
+        in_specs=[smem, VMEM, VMEM, anywhere, VMEM, VMEM, VMEM],
         out_specs=(VMEM, VMEM),
-        scratch_shapes=[held, pltpu.SemaphoreType.DMA((groups,))],
+        scratch_shapes=parts(nyhi),
         compiler_params=CONTRACT,
-    )(inverse, own, x2, full)
+    )(place, inverse, own, x2, first, second, near)
     send, raw, gram_a, own_columns = call(
         functools.partial(night_body, meters * copies),
         (

time: 183 us -> 181 us (0.989)
  waiting for transfers between devices: 40.8 us -> 27.7 us
  starting transfers between devices: 51.6 us -> 61.9 us
    ppermute x0 -> x4, starting transfers between devices: none -> 14.1 us  [the longest x1 5.13 us: on_device(): second = lax.ppermute(second, 'x', down)]
    all_to_all x3 -> x2, waiting for transfers between devices: 21.7 us -> 8.55 us  [exchange(): return lax.all_to_all(blocks, axis, 0, 0, tiled=True)]
    all_to_all x3 -> x2, starting transfers between devices: 22.8 us -> 19.1 us  [exchange(): return lax.all_to_all(blocks, axis, 0, 0, tiled=True)]
    pallas_call x1 -> x2, Pallas kernels: 5.59 us -> 7.79 us  [the longest x1 5.13 us: on_device(): pl.pallas_call(functools.partial(near_body, nyhi, nz, nx), out_shape=f32(...]
  transfers between devices with their start and end apart: 9 -> 12, of which waited for: 9 -> 8; matrix products, arithmetic and copies ran while one was open for 0% -> 0% of each run, Pallas kernels for 1% -> 4%
where the time goes in v8:
time: 181 us
  blocking collectives  68.2 us (38%)
  starting transfers between devices  61.9 us (34%)
  waiting for transfers between devices  27.7 us (15%)
  Pallas kernels  21.5 us (12%)
    all_to_all x3, blocking collectives, exchange(): return lax.all_to_all(blocks, axis, 0, 0, tiled=True)  68.2 us
    ppermute x6, starting transfers between devices, butterfly(): total += lax.ppermute(total, axis, [(i, i ^ step) for i in range(size)])  28.7 us
    ppermute x6, waiting for transfers between devices, butterfly(): total += lax.ppermute(total, axis, [(i, i ^ step) for i in range(size)])  19.1 us
    all_to_all x2, starting transfers between devices, exchange(): return lax.all_to_all(blocks, axis, 0, 0, tiled=True)  19.1 us
    pallas_call x6, Pallas kernels, call(): pl.pallas_call(body, out_shape=outs, in_specs=[VMEM] * len(operands), out...  9.11 us
    all_to_all x2, waiting for transfers between devices, exchange(): return lax.all_to_all(blocks, axis, 0, 0, tiled=True)  8.55 us
    ppermute x1, starting transfers between devices, on_device(): second = lax.ppermute(second, 'x', down)  5.13 us
    pallas_call x1, Pallas kernels, on_device(): pl.pallas_call(functools.partial(near_body, nyhi, nz, nx), out_shape=f32(...  5.13 us
  transfers between devices with their start and end apart: 12, of which 8 were waited for; matrix products, arithmetic and copies ran while one was open for 0% of the time, Pallas kernels for 4%

profile of v8, /device:TPU:8, one launch (start us, length us, event | category | flops | bytes accessed | tf_op | source)
XLA Modules:
  0.0 180.7 jit_solution(7995186529765205471)
XLA Ops:
  0.6 4.6 %shard_map.58 = f32[4,16,64,128]{3,2,1,0:T(8,128)} custom-call(f32[8,64]{1,0:T(8,128)} %bitcast.15, f32[16,64]{1,0:T(8,128)} %bitcast.10, f32[128,8192]{1,0:T(8,128)} %bitcast.12), custom_call_target="tpu_custom_call" | custom-call | tf_op jit(solution)/shard_map/pallas_call | solution.py:347
  5.2 0.0 copy-start.1
  5.2 4.3 %all-to-all-start = ((f32[4,16,64,128]{3,2,1,0:T(8,128)}), f32[4,16,64,128]{3,2,1,0:T(8,128)S(1)}, u32[]{:S(2)}, u32[]{:S(2)}) async-start(f32[4,16,64,128]{3,2,1,0:T(8,128)} %shard_map.58), calls=%async_computation | async-start | bytes 4194304 | tf_op jit(solution)/shard_map/all_to_all | solution.py:322
  9.5 0.0 copy-done.1
  9.5 0.2 fusion
  9.8 4.3 %collective-permute-start = (f32[64,64]{1,0:T(8,128)S(1)}, f32[64,64]{1,0:T(8,128)S(1)}, u32[]{:S(2)}, u32[]{:S(2)}) collective-permute-start(f32[64,64]{1,0:T(8,128)S(1)} %fusion), channel_id=1, source_target_pairs={{0,1},{1,0},{2,3},{3,2},{4,5},{5,4},{6,7},{7,6},{8,9},{9,8},{10,11... | collective-permute-start | bytes 49160 | tf_op jit(solution)/shard_map/ppermute | solution.py:329
  14.1 1.9 %collective-permute-done = f32[64,64]{1,0:T(8,128)S(1)} collective-permute-done((f32[64,64]{1,0:T(8,128)S(1)}, f32[64,64]{1,0:T(8,128)S(1)}, u32[]{:S(2)}, u32[]{:S(2)}) %collective-permute-start) | collective-permute-done | bytes 16416 | tf_op jit(solution)/shard_map/ppermute | solution.py:329
  16.0 6.1 %collective-permute-start.1 = (f32[64,64]{1,0:T(8,128)S(1)}, f32[64,64]{1,0:T(8,128)S(1)}, u32[]{:S(2)}, u32[]{:S(2)}) collective-permute-start(f32[64,64]{1,0:T(8,128)S(1)} %add.18), channel_id=1, source_target_pairs={{0,2},{1,3},{2,0},{3,1},{4,6},{5,7},{6,4},{7,5},{8,10},{9,11},{10,... | collective-permute-start | bytes 49160 | tf_op jit(solution)/shard_map/ppermute | solution.py:329
  22.0 1.9 %collective-permute-done.1 = f32[64,64]{1,0:T(8,128)S(1)} collective-permute-done((f32[64,64]{1,0:T(8,128)S(1)}, f32[64,64]{1,0:T(8,128)S(1)}, u32[]{:S(2)}, u32[]{:S(2)}) %collective-permute-start.1) | collective-permute-done | bytes 16416 | tf_op jit(solution)/shard_map/ppermute | solution.py:329
  23.9 9.3 %collective-permute-start.2 = (f32[64,64]{1,0:T(8,128)S(1)}, f32[64,64]{1,0:T(8,128)S(1)}, u32[]{:S(2)}, u32[]{:S(2)}) collective-permute-start(f32[64,64]{1,0:T(8,128)S(1)} %add.19), channel_id=1, source_target_pairs={{0,4},{1,5},{2,6},{3,7},{4,0},{5,1},{6,2},{7,3},{8,12},{9,13},{10,... | collective-permute-start | bytes 49160 | tf_op jit(solution)/shard_map/ppermute | solution.py:329
  33.2 1.9 %collective-permute-done.2 = f32[64,64]{1,0:T(8,128)S(1)} collective-permute-done((f32[64,64]{1,0:T(8,128)S(1)}, f32[64,64]{1,0:T(8,128)S(1)}, u32[]{:S(2)}, u32[]{:S(2)}) %collective-permute-start.2) | collective-permute-done | bytes 16416 | tf_op jit(solution)/shard_map/ppermute | solution.py:329
  35.1 0.0 copy-start
  35.1 0.7 all-to-all-done.got_ref
  35.9 0.9 shard_map.59
  36.8 14.8 %all-to-all-start.1 = ((f32[16,64,128]{2,1,0:T(8,128)}), f32[16,64,128]{2,1,0:T(8,128)S(1)}, u32[]{:S(2)}, u32[]{:S(2)}) async-start(f32[16,64,128]{2,1,0:T(8,128)} %get-tuple-element.19), calls=%async_computation.1 | async-start | bytes 1048576 | tf_op jit(solution)/shard_map/all_to_all | solution.py:322
  51.6 2.5 %collective-permute-start.3 = (f32[64,64]{1,0:T(8,128)S(1)}, f32[64,64]{1,0:T(8,128)S(1)}, u32[]{:S(2)}, u32[]{:S(2)}) collective-permute-start(f32[64,64]{1,0:T(8,128)S(1)} %get-tuple-element.20), channel_id=1, source_target_pairs={{0,16},{16,0},{32,48},{48,32},{1,17},{17,1},{33,49},{49,33},{2,18}... | collective-permute-start | bytes 49160 | tf_op jit(solution)/shard_map/ppermute | solution.py:329
  54.0 3.3 %collective-permute-done.3 = f32[64,64]{1,0:T(8,128)S(1)} collective-permute-done((f32[64,64]{1,0:T(8,128)S(1)}, f32[64,64]{1,0:T(8,128)S(1)}, u32[]{:S(2)}, u32[]{:S(2)}) %collective-permute-start.3) | collective-permute-done | bytes 16416 | tf_op jit(solution)/shard_map/ppermute | solution.py:329
  57.4 2.5 %collective-permute-start.4 = (f32[64,64]{1,0:T(8,128)S(1)}, f32[64,64]{1,0:T(8,128)S(1)}, u32[]{:S(2)}, u32[]{:S(2)}) collective-permute-start(f32[64,64]{1,0:T(8,128)S(1)} %add.21), channel_id=1, source_target_pairs={{0,32},{16,48},{32,0},{48,16},{1,33},{17,49},{33,1},{49,17},{2,34}... | collective-permute-start | bytes 49160 | tf_op jit(solution)/shard_map/ppermute | solution.py:329
  59.9 4.8 %collective-permute-done.4 = f32[64,64]{1,0:T(8,128)S(1)} collective-permute-done((f32[64,64]{1,0:T(8,128)S(1)}, f32[64,64]{1,0:T(8,128)S(1)}, u32[]{:S(2)}, u32[]{:S(2)}) %collective-permute-start.4) | collective-permute-done | bytes 16416 | tf_op jit(solution)/shard_map/ppermute | solution.py:329
  64.7 7.8 %all-to-all-done.1.got_ref = f32[16,64,128]{2,1,0:T(8,128)S(1)} async-done(((f32[16,64,128]{2,1,0:T(8,128)}), f32[16,64,128]{2,1,0:T(8,128)S(1)}, u32[]{:S(2)}, u32[]{:S(2)}) %all-to-all-start.1) | async-done | bytes 524320 | tf_op jit(solution)/shard_map/all_to_all | solution.py:322
  72.5 0.1 shard_map.60
  72.6 23.6 %all_to_all.25.own_ref = f32[16,64,128]{2,1,0:T(8,128)S(1)} all-to-all(f32[16,64,128]{2,1,0:T(8,128)S(1)} %get-tuple-element.21), channel_id=1, replica_groups=mesh['ylo'=4,'core'=2,'x'=4,'yhi'=2,'z'=8] {'z','yhi'}, dimensions={0} | all-to-all | bytes 1048576 | tf_op jit(solution)/shard_map/all_to_all | solution.py:322
  96.1 2.5 %collective-permute-start.5 = (f32[16,64,128]{2,1,0:T(8,128)S(1)}, f32[16,64,128]{2,1,0:T(8,128)S(1)}, u32[]{:S(2)}, u32[]{:S(2)}) collective-permute-start(f32[16,64,128]{2,1,0:T(8,128)S(1)} %all_to_all.25.own_ref), channel_id=1, source_target_pairs={{0,16},{16,32},{32,48},{48,0},{1,17},{17,33},{33,49},{49,1},{2,18}... | collective-permute-start | bytes 1572872 | tf_op jit(solution)/shard_map/ppermute | solution.py:378
  98.6 4.6 %collective-permute-start.6 = (f32[16,64,128]{2,1,0:T(8,128)S(1)}, f32[16,64,128]{2,1,0:T(8,128)S(1)}, u32[]{:S(2)}, u32[]{:S(2)}) collective-permute-start(f32[16,64,128]{2,1,0:T(8,128)S(1)} %all_to_all.25.own_ref), channel_id=1, source_target_pairs={{0,48},{16,0},{32,16},{48,32},{1,49},{17,1},{33,17},{49,33},{2,50}... | collective-permute-start | bytes 1572872 | tf_op jit(solution)/shard_map/ppermute | solution.py:379
  103.2 4.1 %collective-permute-start.7 = (f32[64,64]{1,0:T(8,128)S(1)}, f32[64,64]{1,0:T(8,128)S(1)}, u32[]{:S(2)}, u32[]{:S(2)}) collective-permute-start(f32[64,64]{1,0:T(8,128)S(1)} %get-tuple-element.22), channel_id=1, source_target_pairs={{0,8},{8,0},{1,9},{9,1},{2,10},{10,2},{3,11},{11,3},{4,12},{12,4},... | collective-permute-start | bytes 49160 | tf_op jit(solution)/shard_map/ppermute | solution.py:329
  107.3 0.0 copy-done
  107.3 0.2 fusion.1.gram_c_ref
  107.6 5.4 %collective-permute-done.7 = f32[64,64]{1,0:T(8,128)S(1)} collective-permute-done((f32[64,64]{1,0:T(8,128)S(1)}, f32[64,64]{1,0:T(8,128)S(1)}, u32[]{:S(2)}, u32[]{:S(2)}) %collective-permute-start.7) | collective-permute-done | bytes 16416 | tf_op jit(solution)/shard_map/ppermute | solution.py:329
  112.9 1.7 shard_map.61.inverse_ref
  114.6 0.0 collective-permute-done.5.left_ref
  114.6 0.0 collective-permute-done.6.right_ref
  114.7 1.9 %collective-permute-start.8 = (f32[8,64,128]{2,1,0:T(8,128)S(1)}, f32[8,64,128]{2,1,0:T(8,128)S(1)}, u32[]{:S(2)}, u32[]{:S(2)}) collective-permute-start(f32[8,64,128]{2,1,0:T(8,128)S(1)} %get-tuple-element.25), channel_id=1, source_target_pairs={{0,16},{16,32},{32,48},{48,0},{1,17},{17,33},{33,49},{49,1},{2,18}... | collective-permute-start | bytes 786440 | tf_op jit(solution)/shard_map/ppermute | solution.py:382
  116.6 5.1 %collective-permute-start.9 = (f32[8,64,128]{2,1,0:T(8,128)S(1)}, f32[8,64,128]{2,1,0:T(8,128)S(1)}, u32[]{:S(2)}, u32[]{:S(2)}) collective-permute-start(f32[8,64,128]{2,1,0:T(8,128)S(1)} %get-tuple-element.26), channel_id=1, source_target_pairs={{0,48},{16,0},{32,16},{48,32},{1,49},{17,1},{33,17},{49,33},{2,50}... | collective-permute-start | bytes 786440 | tf_op jit(solution)/shard_map/ppermute | solution.py:383
  121.7 0.1 pad_add_fusion.place_ref
  121.8 5.1 %shard_map.63.near_ref = f32[192,64]{1,0:T(8,128)S(1)} custom-call(s32[2]{0:T(128)S(1)} %pad_add_fusion.place_ref, f32[64,64]{1,0:T(8,128)S(1)} %get-tuple-element.23.inverse_ref, f32[128,8192]{1,0:T(8,128)} %bitcast.13, f32[16,64,128]{2,1,0:T(8,128)S(1)} %all_to_all.25.own_ref, f32[16,64,128]{2,1,0:T(8,128)S(1)} %collective-permute-done.5.left_ref, ...), custom_call_target="tpu_custom_call" | custom-call | tf_op jit(solution)/shard_map/pallas_call | solution.py:393
  126.9 0.0 collective-permute-done.8.first_ref
  127.0 0.0 collective-permute-done.9.second_ref
  127.0 2.7 %shard_map.64 = (f32[8,96,128]{2,1,0:T(8,128)S(1)}, f32[64,128]{1,0:T(8,128)S(1)}) custom-call(s32[2]{0:T(128)S(1)} %pad_add_fusion.place_ref, f32[64,64]{1,0:T(8,128)S(1)} %get-tuple-element.23.inverse_ref, f32[64,128]{1,0:T(8,128)S(1)} %get-tuple-element.24.own_ref, f32[128,8192]{1,0:T(8,128)} %bitcast.14, ...), custom_call_target="tpu_custom_call" | custom-call | tf_op jit(solution)/shard_map/pallas_call | solution.py:401
  129.6 13.8 %all_to_all.26.got_ref = f32[8,96,128]{2,1,0:T(8,128)S(1)} all-to-all(f32[8,96,128]{2,1,0:T(8,128)S(1)} %get-tuple-element.27), channel_id=1, replica_groups=mesh['ylo'=4,'core'=2,'x'=4,'yhi'=2,'z'=8] {'ylo','core'}, dimensions={0} | all-to-all | bytes 786432 | tf_op jit(solution)/shard_map/all_to_all | solution.py:322
  143.5 3.0 %shard_map.65 = (f32[64,16,128]{2,1,0:T(8,128)S(1)}, f32[8,64]{1,0:T(8,128)S(1)}, f32[64,64]{1,0:T(8,128)S(1)}, f32[64,128]{1,0:T(8,128)}) custom-call(f32[8,96,128]{2,1,0:T(8,128)S(1)} %all_to_all.26.got_ref, f32[64,64]{1,0:T(8,128)S(1)} %fusion.1.gram_c_ref, f32[16,64]{1,0:T(8,128)S(1)} %bitcast.11, f32[64,128]{1,0:T(8,128)S(1)} %get-tuple-element.28.own_ref), custom_call_target="tpu_custom_call" | custom-call | tf_op jit(solution)/shard_map/pallas_call | solution.py:28
  146.5 30.8 %all_to_all.27.got_ref = f32[64,16,128]{2,1,0:T(8,128)S(1)} all-to-all(f32[64,16,128]{2,1,0:T(8,128)S(1)} %get-tuple-element.30), channel_id=1, replica_groups=mesh['ylo'=4,'core'=2,'x'=4,'yhi'=2,'z'=8] {'x','yhi','z'}, dimensions={0} | all-to-all | bytes 1048576 | tf_op jit(solution)/shard_map/all_to_all | solution.py:322
  177.3 3.4 %shard_map.66 = (f32[8,64]{1,0:T(8,128)}, f32[16,64]{1,0:T(8,128)}) custom-call(f32[64,16,128]{2,1,0:T(8,128)S(1)} %all_to_all.27.got_ref, f32[8,64]{1,0:T(8,128)S(1)} %get-tuple-element.31.raw_ref, f32[64,64]{1,0:T(8,128)S(1)} %get-tuple-element.32.gram_ref), custom_call_target="tpu_custom_call" | custom-call | tf_op jit(solution)/shard_map/pallas_call | solution.py:28
  (7 shorter events, 0.1 us)
Async XLA Ops:
  5.2 4.3 %copy-start.1 = (f32[64,8]{0,1:T(8,128)S(1)}, f32[64,8]{0,1:T(8,128)}, u32[]{:S(2)}) copy-start(f32[64,8]{0,1:T(8,128)} %param.4) | copy-start | bytes 6148
  5.2 30.6 %all-to-all-start = ((f32[4,16,64,128]{3,2,1,0:T(8,128)}), f32[4,16,64,128]{3,2,1,0:T(8,128)S(1)}, u32[]{:S(2)}, u32[]{:S(2)}) async-start(f32[4,16,64,128]{3,2,1,0:T(8,128)} %shard_map.58), calls=%async_computation | async-start | bytes 4194304 | tf_op jit(solution)/shard_map/all_to_all | solution.py:322
  9.8 6.2 %collective-permute-start = (f32[64,64]{1,0:T(8,128)S(1)}, f32[64,64]{1,0:T(8,128)S(1)}, u32[]{:S(2)}, u32[]{:S(2)}) collective-permute-start(f32[64,64]{1,0:T(8,128)S(1)} %fusion), channel_id=1, source_target_pairs={{0,1},{1,0},{2,3},{3,2},{4,5},{5,4},{6,7},{7,6},{8,9},{9,8},{10,11... | collective-permute-start | bytes 49160 | tf_op jit(solution)/shard_map/ppermute | solution.py:329
  16.0 8.0 %collective-permute-start.1 = (f32[64,64]{1,0:T(8,128)S(1)}, f32[64,64]{1,0:T(8,128)S(1)}, u32[]{:S(2)}, u32[]{:S(2)}) collective-permute-start(f32[64,64]{1,0:T(8,128)S(1)} %add.18), channel_id=1, source_target_pairs={{0,2},{1,3},{2,0},{3,1},{4,6},{5,7},{6,4},{7,5},{8,10},{9,11},{10,... | collective-permute-start | bytes 49160 | tf_op jit(solution)/shard_map/ppermute | solution.py:329
  23.9 11.2 %collective-permute-start.2 = (f32[64,64]{1,0:T(8,128)S(1)}, f32[64,64]{1,0:T(8,128)S(1)}, u32[]{:S(2)}, u32[]{:S(2)}) collective-permute-start(f32[64,64]{1,0:T(8,128)S(1)} %add.19), channel_id=1, source_target_pairs={{0,4},{1,5},{2,6},{3,7},{4,0},{5,1},{6,2},{7,3},{8,12},{9,13},{10,... | collective-permute-start | bytes 49160 | tf_op jit(solution)/shard_map/ppermute | solution.py:329
  35.1 72.2 %copy-start = (f32[64,16]{0,1:T(8,128)S(1)}, f32[64,16]{0,1:T(8,128)}, u32[]{:S(2)}) copy-start(f32[64,16]{0,1:T(8,128)} %param.5) | copy-start | bytes 12292
  36.8 35.7 %all-to-all-start.1 = ((f32[16,64,128]{2,1,0:T(8,128)}), f32[16,64,128]{2,1,0:T(8,128)S(1)}, u32[]{:S(2)}, u32[]{:S(2)}) async-start(f32[16,64,128]{2,1,0:T(8,128)} %get-tuple-element.19), calls=%async_computation.1 | async-start | bytes 1048576 | tf_op jit(solution)/shard_map/all_to_all | solution.py:322
  51.6 5.8 %collective-permute-start.3 = (f32[64,64]{1,0:T(8,128)S(1)}, f32[64,64]{1,0:T(8,128)S(1)}, u32[]{:S(2)}, u32[]{:S(2)}) collective-permute-start(f32[64,64]{1,0:T(8,128)S(1)} %get-tuple-element.20), channel_id=1, source_target_pairs={{0,16},{16,0},{32,48},{48,32},{1,17},{17,1},{33,49},{49,33},{2,18}... | collective-permute-start | bytes 49160 | tf_op jit(solution)/shard_map/ppermute | solution.py:329
  57.4 7.3 %collective-permute-start.4 = (f32[64,64]{1,0:T(8,128)S(1)}, f32[64,64]{1,0:T(8,128)S(1)}, u32[]{:S(2)}, u32[]{:S(2)}) collective-permute-start(f32[64,64]{1,0:T(8,128)S(1)} %add.21), channel_id=1, source_target_pairs={{0,32},{16,48},{32,0},{48,16},{1,33},{17,49},{33,1},{49,17},{2,34}... | collective-permute-start | bytes 49160 | tf_op jit(solution)/shard_map/ppermute | solution.py:329
  96.1 18.4 %collective-permute-start.5 = (f32[16,64,128]{2,1,0:T(8,128)S(1)}, f32[16,64,128]{2,1,0:T(8,128)S(1)}, u32[]{:S(2)}, u32[]{:S(2)}) collective-permute-start(f32[16,64,128]{2,1,0:T(8,128)S(1)} %all_to_all.25.own_ref), channel_id=1, source_target_pairs={{0,16},{16,32},{32,48},{48,0},{1,17},{17,33},{33,49},{49,1},{2,18}... | collective-permute-start | bytes 1572872 | tf_op jit(solution)/shard_map/ppermute | solution.py:378
  98.6 16.0 %collective-permute-start.6 = (f32[16,64,128]{2,1,0:T(8,128)S(1)}, f32[16,64,128]{2,1,0:T(8,128)S(1)}, u32[]{:S(2)}, u32[]{:S(2)}) collective-permute-start(f32[16,64,128]{2,1,0:T(8,128)S(1)} %all_to_all.25.own_ref), channel_id=1, source_target_pairs={{0,48},{16,0},{32,16},{48,32},{1,49},{17,1},{33,17},{49,33},{2,50}... | collective-permute-start | bytes 1572872 | tf_op jit(solution)/shard_map/ppermute | solution.py:379
  103.2 9.7 %collective-permute-start.7 = (f32[64,64]{1,0:T(8,128)S(1)}, f32[64,64]{1,0:T(8,128)S(1)}, u32[]{:S(2)}, u32[]{:S(2)}) collective-permute-start(f32[64,64]{1,0:T(8,128)S(1)} %get-tuple-element.22), channel_id=1, source_target_pairs={{0,8},{8,0},{1,9},{9,1},{2,10},{10,2},{3,11},{11,3},{4,12},{12,4},... | collective-permute-start | bytes 49160 | tf_op jit(solution)/shard_map/ppermute | solution.py:329
  114.7 12.3 %collective-permute-start.8 = (f32[8,64,128]{2,1,0:T(8,128)S(1)}, f32[8,64,128]{2,1,0:T(8,128)S(1)}, u32[]{:S(2)}, u32[]{:S(2)}) collective-permute-start(f32[8,64,128]{2,1,0:T(8,128)S(1)} %get-tuple-element.25), channel_id=1, source_target_pairs={{0,16},{16,32},{32,48},{48,0},{1,17},{17,33},{33,49},{49,1},{2,18}... | collective-permute-start | bytes 786440 | tf_op jit(solution)/shard_map/ppermute | solution.py:382
  116.6 10.4 %collective-permute-start.9 = (f32[8,64,128]{2,1,0:T(8,128)S(1)}, f32[8,64,128]{2,1,0:T(8,128)S(1)}, u32[]{:S(2)}, u32[]{:S(2)}) collective-permute-start(f32[8,64,128]{2,1,0:T(8,128)S(1)} %get-tuple-element.26), channel_id=1, source_target_pairs={{0,48},{16,0},{32,16},{48,32},{1,49},{17,1},{33,17},{49,33},{2,50}... | collective-permute-start | bytes 786440 | tf_op jit(solution)/shard_map/ppermute | solution.py:383

commit v9 on v8

--- a/solution.py
+++ b/solution.py
@@ -178,9 +178,12 @@
 
 
 def near_body(
-    nyhi, nz, nx, place_ref, inverse_ref, x_ref, own_ref, left_ref, right_ref, total_ref,
-    held_ref, sems,
+    nyhi, nz, nx, place_ref, inverse_ref, mine_ref, x_ref, own_ref, left_ref, right_ref,
+    total_ref, own_out_ref, held_ref, sems,
 ):
+    own_out_ref[...] = jnp.dot(
+        inverse_ref[...], mine_ref[...], precision=FULL, preferred_element_type=jnp.float32
+    )
     places = own_ref.shape[0]
     chunks = [
         (distance, [ref[i] for i in range(places)])
@@ -192,14 +195,11 @@
 
 
 def far_body(
-    nyhi, nz, place_ref, inverse_ref, own_ref, x_ref, first_ref, second_ref, near_ref,
-    out_ref, own_out_ref, held_ref, sems,
+    nyhi, nz, place_ref, inverse_ref, x_ref, first_ref, second_ref, near_ref, out_ref,
+    held_ref, sems,
 ):
     inverse = inverse_ref[...]
     rank = inverse.shape[0]
-    own_out_ref[...] = jnp.dot(
-        inverse, own_ref[...], precision=FULL, preferred_element_type=jnp.float32
-    )
     blocks = [ref[i] for ref in (first_ref, second_ref) for i in range(ref.shape[0])]
     total = near_ref[...] + contracted_blocks(
         nyhi, nz, place_ref, inverse, x_ref, [(2, blocks)], held_ref, sems
@@ -390,22 +390,22 @@
             pltpu.SemaphoreType.DMA((groups,)),
         ]
 
-    near = pl.pallas_call(
+    near, own_raw = pl.pallas_call(
         functools.partial(near_body, nyhi, nz, nx),
-        out_shape=f32(nights * intervals + rank, rank),
+        out_shape=(f32(nights * intervals + rank, rank), f32(rank, share)),
+        in_specs=[smem, VMEM, VMEM, anywhere, VMEM, VMEM, VMEM],
+        out_specs=(VMEM, VMEM),
+        scratch_shapes=parts(3 * nyhi),
+        compiler_params=CONTRACT,
+    )(place, inverse, own, x2, chunk, left, right)
+    packed = pl.pallas_call(
+        functools.partial(far_body, nyhi, nz),
+        out_shape=f32(copies, (nights * intervals + rank) // 2, 2 * rank),
         in_specs=[smem, VMEM, anywhere, VMEM, VMEM, VMEM],
         out_specs=VMEM,
-        scratch_shapes=parts(3 * nyhi),
-        compiler_params=CONTRACT,
-    )(place, inverse, x2, chunk, left, right)
-    packed, own_raw = pl.pallas_call(
-        functools.partial(far_body, nyhi, nz),
-        out_shape=(f32(copies, (nights * intervals + rank) // 2, 2 * rank), f32(rank, share)),
-        in_specs=[smem, VMEM, VMEM, anywhere, VMEM, VMEM, VMEM],
-        out_specs=(VMEM, VMEM),
         scratch_shapes=parts(nyhi),
         compiler_params=CONTRACT,
-    )(place, inverse, own, x2, first, second, near)
+    )(place, inverse, x2, first, second, near)
     send, raw, gram_a, own_columns = call(
         functools.partial(night_body, meters * copies),
         (

time: 181 us -> 181 us (level)
  no operation moved by 1% of the time
where the time goes in v9:
time: 181 us
  blocking collectives  68.3 us (38%)
  starting transfers between devices  61.9 us (34%)
  waiting for transfers between devices  27.7 us (15%)
  Pallas kernels  21.4 us (12%)
    all_to_all x3, blocking collectives, exchange(): return lax.all_to_all(blocks, axis, 0, 0, tiled=True)  68.3 us
    ppermute x6, starting transfers between devices, butterfly(): total += lax.ppermute(total, axis, [(i, i ^ step) for i in range(size)])  28.7 us
    ppermute x6, waiting for transfers between devices, butterfly(): total += lax.ppermute(total, axis, [(i, i ^ step) for i in range(size)])  19.1 us
    all_to_all x2, starting transfers between devices, exchange(): return lax.all_to_all(blocks, axis, 0, 0, tiled=True)  19.1 us
    pallas_call x6, Pallas kernels, call(): pl.pallas_call(body, out_shape=outs, in_specs=[VMEM] * len(operands), out...  9.11 us
    all_to_all x2, waiting for transfers between devices, exchange(): return lax.all_to_all(blocks, axis, 0, 0, tiled=True)  8.55 us
    ppermute x1, starting transfers between devices, on_device(): second = lax.ppermute(second, 'x', down)  5.13 us
    pallas_call x1, Pallas kernels, on_device(): pl.pallas_call(functools.partial(near_body, nyhi, nz, nx), out_shape=(f32...  5.06 us
  transfers between devices with their start and end apart: 12, of which 8 were waited for; matrix products, arithmetic and copies ran while one was open for 0% of the time, Pallas kernels for 4%

profile of v9, /device:TPU:8, one launch (start us, length us, event | category | flops | bytes accessed | tf_op | source)
XLA Modules:
  0.0 180.7 jit_solution(2101572893678521123)
XLA Ops:
  0.6 4.6 %shard_map.58 = f32[4,16,64,128]{3,2,1,0:T(8,128)} custom-call(f32[8,64]{1,0:T(8,128)} %bitcast.15, f32[16,64]{1,0:T(8,128)} %bitcast.10, f32[128,8192]{1,0:T(8,128)} %bitcast.12), custom_call_target="tpu_custom_call" | custom-call | tf_op jit(solution)/shard_map/pallas_call | solution.py:347
  5.2 0.0 copy-start.1
  5.2 4.3 %all-to-all-start = ((f32[4,16,64,128]{3,2,1,0:T(8,128)}), f32[4,16,64,128]{3,2,1,0:T(8,128)S(1)}, u32[]{:S(2)}, u32[]{:S(2)}) async-start(f32[4,16,64,128]{3,2,1,0:T(8,128)} %shard_map.58), calls=%async_computation | async-start | bytes 4194304 | tf_op jit(solution)/shard_map/all_to_all | solution.py:322
  9.5 0.0 copy-done.1
  9.5 0.2 fusion
  9.8 4.3 %collective-permute-start = (f32[64,64]{1,0:T(8,128)S(1)}, f32[64,64]{1,0:T(8,128)S(1)}, u32[]{:S(2)}, u32[]{:S(2)}) collective-permute-start(f32[64,64]{1,0:T(8,128)S(1)} %fusion), channel_id=1, source_target_pairs={{0,1},{1,0},{2,3},{3,2},{4,5},{5,4},{6,7},{7,6},{8,9},{9,8},{10,11... | collective-permute-start | bytes 49160 | tf_op jit(solution)/shard_map/ppermute | solution.py:329
  14.1 1.9 %collective-permute-done = f32[64,64]{1,0:T(8,128)S(1)} collective-permute-done((f32[64,64]{1,0:T(8,128)S(1)}, f32[64,64]{1,0:T(8,128)S(1)}, u32[]{:S(2)}, u32[]{:S(2)}) %collective-permute-start) | collective-permute-done | bytes 16416 | tf_op jit(solution)/shard_map/ppermute | solution.py:329
  16.0 6.1 %collective-permute-start.1 = (f32[64,64]{1,0:T(8,128)S(1)}, f32[64,64]{1,0:T(8,128)S(1)}, u32[]{:S(2)}, u32[]{:S(2)}) collective-permute-start(f32[64,64]{1,0:T(8,128)S(1)} %add.18), channel_id=1, source_target_pairs={{0,2},{1,3},{2,0},{3,1},{4,6},{5,7},{6,4},{7,5},{8,10},{9,11},{10,... | collective-permute-start | bytes 49160 | tf_op jit(solution)/shard_map/ppermute | solution.py:329
  22.0 1.9 %collective-permute-done.1 = f32[64,64]{1,0:T(8,128)S(1)} collective-permute-done((f32[64,64]{1,0:T(8,128)S(1)}, f32[64,64]{1,0:T(8,128)S(1)}, u32[]{:S(2)}, u32[]{:S(2)}) %collective-permute-start.1) | collective-permute-done | bytes 16416 | tf_op jit(solution)/shard_map/ppermute | solution.py:329
  23.9 9.3 %collective-permute-start.2 = (f32[64,64]{1,0:T(8,128)S(1)}, f32[64,64]{1,0:T(8,128)S(1)}, u32[]{:S(2)}, u32[]{:S(2)}) collective-permute-start(f32[64,64]{1,0:T(8,128)S(1)} %add.19), channel_id=1, source_target_pairs={{0,4},{1,5},{2,6},{3,7},{4,0},{5,1},{6,2},{7,3},{8,12},{9,13},{10,... | collective-permute-start | bytes 49160 | tf_op jit(solution)/shard_map/ppermute | solution.py:329
  33.2 1.9 %collective-permute-done.2 = f32[64,64]{1,0:T(8,128)S(1)} collective-permute-done((f32[64,64]{1,0:T(8,128)S(1)}, f32[64,64]{1,0:T(8,128)S(1)}, u32[]{:S(2)}, u32[]{:S(2)}) %collective-permute-start.2) | collective-permute-done | bytes 16416 | tf_op jit(solution)/shard_map/ppermute | solution.py:329
  35.1 0.0 copy-start
  35.1 0.7 all-to-all-done.got_ref
  35.9 0.9 shard_map.59
  36.8 14.8 %all-to-all-start.1 = ((f32[16,64,128]{2,1,0:T(8,128)}), f32[16,64,128]{2,1,0:T(8,128)S(1)}, u32[]{:S(2)}, u32[]{:S(2)}) async-start(f32[16,64,128]{2,1,0:T(8,128)} %get-tuple-element.19), calls=%async_computation.1 | async-start | bytes 1048576 | tf_op jit(solution)/shard_map/all_to_all | solution.py:322
  51.6 2.5 %collective-permute-start.3 = (f32[64,64]{1,0:T(8,128)S(1)}, f32[64,64]{1,0:T(8,128)S(1)}, u32[]{:S(2)}, u32[]{:S(2)}) collective-permute-start(f32[64,64]{1,0:T(8,128)S(1)} %get-tuple-element.20), channel_id=1, source_target_pairs={{0,16},{16,0},{32,48},{48,32},{1,17},{17,1},{33,49},{49,33},{2,18}... | collective-permute-start | bytes 49160 | tf_op jit(solution)/shard_map/ppermute | solution.py:329
  54.0 3.3 %collective-permute-done.3 = f32[64,64]{1,0:T(8,128)S(1)} collective-permute-done((f32[64,64]{1,0:T(8,128)S(1)}, f32[64,64]{1,0:T(8,128)S(1)}, u32[]{:S(2)}, u32[]{:S(2)}) %collective-permute-start.3) | collective-permute-done | bytes 16416 | tf_op jit(solution)/shard_map/ppermute | solution.py:329
  57.4 2.5 %collective-permute-start.4 = (f32[64,64]{1,0:T(8,128)S(1)}, f32[64,64]{1,0:T(8,128)S(1)}, u32[]{:S(2)}, u32[]{:S(2)}) collective-permute-start(f32[64,64]{1,0:T(8,128)S(1)} %add.21), channel_id=1, source_target_pairs={{0,32},{16,48},{32,0},{48,16},{1,33},{17,49},{33,1},{49,17},{2,34}... | collective-permute-start | bytes 49160 | tf_op jit(solution)/shard_map/ppermute | solution.py:329
  59.9 4.8 %collective-permute-done.4 = f32[64,64]{1,0:T(8,128)S(1)} collective-permute-done((f32[64,64]{1,0:T(8,128)S(1)}, f32[64,64]{1,0:T(8,128)S(1)}, u32[]{:S(2)}, u32[]{:S(2)}) %collective-permute-start.4) | collective-permute-done | bytes 16416 | tf_op jit(solution)/shard_map/ppermute | solution.py:329
  64.7 7.8 %all-to-all-done.1.got_ref = f32[16,64,128]{2,1,0:T(8,128)S(1)} async-done(((f32[16,64,128]{2,1,0:T(8,128)}), f32[16,64,128]{2,1,0:T(8,128)S(1)}, u32[]{:S(2)}, u32[]{:S(2)}) %all-to-all-start.1) | async-done | bytes 524320 | tf_op jit(solution)/shard_map/all_to_all | solution.py:322
  72.5 0.1 shard_map.60
  72.6 23.6 %all_to_all.25.own_ref = f32[16,64,128]{2,1,0:T(8,128)S(1)} all-to-all(f32[16,64,128]{2,1,0:T(8,128)S(1)} %get-tuple-element.21), channel_id=1, replica_groups=mesh['ylo'=4,'core'=2,'x'=4,'yhi'=2,'z'=8] {'z','yhi'}, dimensions={0} | all-to-all | bytes 1048576 | tf_op jit(solution)/shard_map/all_to_all | solution.py:322
  96.1 2.5 %collective-permute-start.5 = (f32[16,64,128]{2,1,0:T(8,128)S(1)}, f32[16,64,128]{2,1,0:T(8,128)S(1)}, u32[]{:S(2)}, u32[]{:S(2)}) collective-permute-start(f32[16,64,128]{2,1,0:T(8,128)S(1)} %all_to_all.25.own_ref), channel_id=1, source_target_pairs={{0,16},{16,32},{32,48},{48,0},{1,17},{17,33},{33,49},{49,1},{2,18}... | collective-permute-start | bytes 1572872 | tf_op jit(solution)/shard_map/ppermute | solution.py:378
  98.6 4.6 %collective-permute-start.6 = (f32[16,64,128]{2,1,0:T(8,128)S(1)}, f32[16,64,128]{2,1,0:T(8,128)S(1)}, u32[]{:S(2)}, u32[]{:S(2)}) collective-permute-start(f32[16,64,128]{2,1,0:T(8,128)S(1)} %all_to_all.25.own_ref), channel_id=1, source_target_pairs={{0,48},{16,0},{32,16},{48,32},{1,49},{17,1},{33,17},{49,33},{2,50}... | collective-permute-start | bytes 1572872 | tf_op jit(solution)/shard_map/ppermute | solution.py:379
  103.2 4.1 %collective-permute-start.7 = (f32[64,64]{1,0:T(8,128)S(1)}, f32[64,64]{1,0:T(8,128)S(1)}, u32[]{:S(2)}, u32[]{:S(2)}) collective-permute-start(f32[64,64]{1,0:T(8,128)S(1)} %get-tuple-element.22), channel_id=1, source_target_pairs={{0,8},{8,0},{1,9},{9,1},{2,10},{10,2},{3,11},{11,3},{4,12},{12,4},... | collective-permute-start | bytes 49160 | tf_op jit(solution)/shard_map/ppermute | solution.py:329
  107.3 0.0 copy-done
  107.3 0.2 fusion.1.gram_c_ref
  107.6 5.4 %collective-permute-done.7 = f32[64,64]{1,0:T(8,128)S(1)} collective-permute-done((f32[64,64]{1,0:T(8,128)S(1)}, f32[64,64]{1,0:T(8,128)S(1)}, u32[]{:S(2)}, u32[]{:S(2)}) %collective-permute-start.7) | collective-permute-done | bytes 16416 | tf_op jit(solution)/shard_map/ppermute | solution.py:329
  112.9 1.7 shard_map.61.inverse_ref
  114.6 0.0 collective-permute-done.5.left_ref
  114.6 0.0 collective-permute-done.6.right_ref
  114.7 1.9 %collective-permute-start.8 = (f32[8,64,128]{2,1,0:T(8,128)S(1)}, f32[8,64,128]{2,1,0:T(8,128)S(1)}, u32[]{:S(2)}, u32[]{:S(2)}) collective-permute-start(f32[8,64,128]{2,1,0:T(8,128)S(1)} %get-tuple-element.24), channel_id=1, source_target_pairs={{0,16},{16,32},{32,48},{48,0},{1,17},{17,33},{33,49},{49,1},{2,18}... | collective-permute-start | bytes 786440 | tf_op jit(solution)/shard_map/ppermute | solution.py:382
  116.6 5.1 %collective-permute-start.9 = (f32[8,64,128]{2,1,0:T(8,128)S(1)}, f32[8,64,128]{2,1,0:T(8,128)S(1)}, u32[]{:S(2)}, u32[]{:S(2)}) collective-permute-start(f32[8,64,128]{2,1,0:T(8,128)S(1)} %get-tuple-element.25), channel_id=1, source_target_pairs={{0,48},{16,0},{32,16},{48,32},{1,49},{17,1},{33,17},{49,33},{2,50}... | collective-permute-start | bytes 786440 | tf_op jit(solution)/shard_map/ppermute | solution.py:383
  121.7 0.1 pad_add_fusion.place_ref
  121.8 5.1 %shard_map.63 = (f32[192,64]{1,0:T(8,128)S(1)}, f32[64,128]{1,0:T(8,128)S(1)}) custom-call(s32[2]{0:T(128)S(1)} %pad_add_fusion.place_ref, f32[64,64]{1,0:T(8,128)S(1)} %get-tuple-element.23.inverse_ref, f32[64,128]{1,0:T(8,128)S(1)} %get-tuple-element.26.mine_ref, f32[128,8192]{1,0:T(8,128)} %bitcast.13, f32[16,64,128]{2,1,0:T(8,128)S(1)} %all_to_all.25.own_ref, ...), custom_call_target="tpu_custom_call" | custom-call | tf_op jit(solution)/shard_map/pallas_call | solution.py:393
  126.9 0.0 collective-permute-done.8.first_ref
  126.9 0.0 collective-permute-done.9.second_ref
  126.9 2.6 %shard_map.64 = f32[8,96,128]{2,1,0:T(8,128)S(1)} custom-call(s32[2]{0:T(128)S(1)} %pad_add_fusion.place_ref, f32[64,64]{1,0:T(8,128)S(1)} %get-tuple-element.23.inverse_ref, f32[128,8192]{1,0:T(8,128)} %bitcast.14, f32[8,64,128]{2,1,0:T(8,128)S(1)} %collective-permute-done.8.first_ref, f32[8,64,128]{2,1,0:T(8,128)S(1)} %collective-permute-done.9.second_ref, ...), custom_call_target="tpu_custom_call" | custom-call | tf_op jit(solution)/shard_map/pallas_call | solution.py:401
  129.5 13.8 %all_to_all.26.got_ref = f32[8,96,128]{2,1,0:T(8,128)S(1)} all-to-all(f32[8,96,128]{2,1,0:T(8,128)S(1)} %shard_map.64), channel_id=1, replica_groups=mesh['ylo'=4,'core'=2,'x'=4,'yhi'=2,'z'=8] {'ylo','core'}, dimensions={0} | all-to-all | bytes 786432 | tf_op jit(solution)/shard_map/all_to_all | solution.py:322
  143.4 3.0 %shard_map.65 = (f32[64,16,128]{2,1,0:T(8,128)S(1)}, f32[8,64]{1,0:T(8,128)S(1)}, f32[64,64]{1,0:T(8,128)S(1)}, f32[64,128]{1,0:T(8,128)}) custom-call(f32[8,96,128]{2,1,0:T(8,128)S(1)} %all_to_all.26.got_ref, f32[64,64]{1,0:T(8,128)S(1)} %fusion.1.gram_c_ref, f32[16,64]{1,0:T(8,128)S(1)} %bitcast.11, f32[64,128]{1,0:T(8,128)S(1)} %get-tuple-element.28.own_ref), custom_call_target="tpu_custom_call" | custom-call | tf_op jit(solution)/shard_map/pallas_call | solution.py:28
  146.4 30.9 %all_to_all.27.got_ref = f32[64,16,128]{2,1,0:T(8,128)S(1)} all-to-all(f32[64,16,128]{2,1,0:T(8,128)S(1)} %get-tuple-element.30), channel_id=1, replica_groups=mesh['ylo'=4,'core'=2,'x'=4,'yhi'=2,'z'=8] {'x','yhi','z'}, dimensions={0} | all-to-all | bytes 1048576 | tf_op jit(solution)/shard_map/all_to_all | solution.py:322
  177.3 3.4 %shard_map.66 = (f32[8,64]{1,0:T(8,128)}, f32[16,64]{1,0:T(8,128)}) custom-call(f32[64,16,128]{2,1,0:T(8,128)S(1)} %all_to_all.27.got_ref, f32[8,64]{1,0:T(8,128)S(1)} %get-tuple-element.31.raw_ref, f32[64,64]{1,0:T(8,128)S(1)} %get-tuple-element.32.gram_ref), custom_call_target="tpu_custom_call" | custom-call | tf_op jit(solution)/shard_map/pallas_call | solution.py:28
  (7 shorter events, 0.1 us)
Async XLA Ops:
  5.2 4.3 %copy-start.1 = (f32[64,8]{0,1:T(8,128)S(1)}, f32[64,8]{0,1:T(8,128)}, u32[]{:S(2)}) copy-start(f32[64,8]{0,1:T(8,128)} %param.4) | copy-start | bytes 6148
  5.2 30.6 %all-to-all-start = ((f32[4,16,64,128]{3,2,1,0:T(8,128)}), f32[4,16,64,128]{3,2,1,0:T(8,128)S(1)}, u32[]{:S(2)}, u32[]{:S(2)}) async-start(f32[4,16,64,128]{3,2,1,0:T(8,128)} %shard_map.58), calls=%async_computation | async-start | bytes 4194304 | tf_op jit(solution)/shard_map/all_to_all | solution.py:322
  9.8 6.2 %collective-permute-start = (f32[64,64]{1,0:T(8,128)S(1)}, f32[64,64]{1,0:T(8,128)S(1)}, u32[]{:S(2)}, u32[]{:S(2)}) collective-permute-start(f32[64,64]{1,0:T(8,128)S(1)} %fusion), channel_id=1, source_target_pairs={{0,1},{1,0},{2,3},{3,2},{4,5},{5,4},{6,7},{7,6},{8,9},{9,8},{10,11... | collective-permute-start | bytes 49160 | tf_op jit(solution)/shard_map/ppermute | solution.py:329
  16.0 8.0 %collective-permute-start.1 = (f32[64,64]{1,0:T(8,128)S(1)}, f32[64,64]{1,0:T(8,128)S(1)}, u32[]{:S(2)}, u32[]{:S(2)}) collective-permute-start(f32[64,64]{1,0:T(8,128)S(1)} %add.18), channel_id=1, source_target_pairs={{0,2},{1,3},{2,0},{3,1},{4,6},{5,7},{6,4},{7,5},{8,10},{9,11},{10,... | collective-permute-start | bytes 49160 | tf_op jit(solution)/shard_map/ppermute | solution.py:329
  23.9 11.2 %collective-permute-start.2 = (f32[64,64]{1,0:T(8,128)S(1)}, f32[64,64]{1,0:T(8,128)S(1)}, u32[]{:S(2)}, u32[]{:S(2)}) collective-permute-start(f32[64,64]{1,0:T(8,128)S(1)} %add.19), channel_id=1, source_target_pairs={{0,4},{1,5},{2,6},{3,7},{4,0},{5,1},{6,2},{7,3},{8,12},{9,13},{10,... | collective-permute-start | bytes 49160 | tf_op jit(solution)/shard_map/ppermute | solution.py:329
  35.1 72.2 %copy-start = (f32[64,16]{0,1:T(8,128)S(1)}, f32[64,16]{0,1:T(8,128)}, u32[]{:S(2)}) copy-start(f32[64,16]{0,1:T(8,128)} %param.5) | copy-start | bytes 12292
  36.8 35.7 %all-to-all-start.1 = ((f32[16,64,128]{2,1,0:T(8,128)}), f32[16,64,128]{2,1,0:T(8,128)S(1)}, u32[]{:S(2)}, u32[]{:S(2)}) async-start(f32[16,64,128]{2,1,0:T(8,128)} %get-tuple-element.19), calls=%async_computation.1 | async-start | bytes 1048576 | tf_op jit(solution)/shard_map/all_to_all | solution.py:322
  51.6 5.8 %collective-permute-start.3 = (f32[64,64]{1,0:T(8,128)S(1)}, f32[64,64]{1,0:T(8,128)S(1)}, u32[]{:S(2)}, u32[]{:S(2)}) collective-permute-start(f32[64,64]{1,0:T(8,128)S(1)} %get-tuple-element.20), channel_id=1, source_target_pairs={{0,16},{16,0},{32,48},{48,32},{1,17},{17,1},{33,49},{49,33},{2,18}... | collective-permute-start | bytes 49160 | tf_op jit(solution)/shard_map/ppermute | solution.py:329
  57.4 7.3 %collective-permute-start.4 = (f32[64,64]{1,0:T(8,128)S(1)}, f32[64,64]{1,0:T(8,128)S(1)}, u32[]{:S(2)}, u32[]{:S(2)}) collective-permute-start(f32[64,64]{1,0:T(8,128)S(1)} %add.21), channel_id=1, source_target_pairs={{0,32},{16,48},{32,0},{48,16},{1,33},{17,49},{33,1},{49,17},{2,34}... | collective-permute-start | bytes 49160 | tf_op jit(solution)/shard_map/ppermute | solution.py:329
  96.1 18.4 %collective-permute-start.5 = (f32[16,64,128]{2,1,0:T(8,128)S(1)}, f32[16,64,128]{2,1,0:T(8,128)S(1)}, u32[]{:S(2)}, u32[]{:S(2)}) collective-permute-start(f32[16,64,128]{2,1,0:T(8,128)S(1)} %all_to_all.25.own_ref), channel_id=1, source_target_pairs={{0,16},{16,32},{32,48},{48,0},{1,17},{17,33},{33,49},{49,1},{2,18}... | collective-permute-start | bytes 1572872 | tf_op jit(solution)/shard_map/ppermute | solution.py:378
  98.6 16.0 %collective-permute-start.6 = (f32[16,64,128]{2,1,0:T(8,128)S(1)}, f32[16,64,128]{2,1,0:T(8,128)S(1)}, u32[]{:S(2)}, u32[]{:S(2)}) collective-permute-start(f32[16,64,128]{2,1,0:T(8,128)S(1)} %all_to_all.25.own_ref), channel_id=1, source_target_pairs={{0,48},{16,0},{32,16},{48,32},{1,49},{17,1},{33,17},{49,33},{2,50}... | collective-permute-start | bytes 1572872 | tf_op jit(solution)/shard_map/ppermute | solution.py:379
  103.2 9.7 %collective-permute-start.7 = (f32[64,64]{1,0:T(8,128)S(1)}, f32[64,64]{1,0:T(8,128)S(1)}, u32[]{:S(2)}, u32[]{:S(2)}) collective-permute-start(f32[64,64]{1,0:T(8,128)S(1)} %get-tuple-element.22), channel_id=1, source_target_pairs={{0,8},{8,0},{1,9},{9,1},{2,10},{10,2},{3,11},{11,3},{4,12},{12,4},... | collective-permute-start | bytes 49160 | tf_op jit(solution)/shard_map/ppermute | solution.py:329
  114.7 12.2 %collective-permute-start.8 = (f32[8,64,128]{2,1,0:T(8,128)S(1)}, f32[8,64,128]{2,1,0:T(8,128)S(1)}, u32[]{:S(2)}, u32[]{:S(2)}) collective-permute-start(f32[8,64,128]{2,1,0:T(8,128)S(1)} %get-tuple-element.24), channel_id=1, source_target_pairs={{0,16},{16,32},{32,48},{48,0},{1,17},{17,33},{33,49},{49,1},{2,18}... | collective-permute-start | bytes 786440 | tf_op jit(solution)/shard_map/ppermute | solution.py:382
  116.6 10.3 %collective-permute-start.9 = (f32[8,64,128]{2,1,0:T(8,128)S(1)}, f32[8,64,128]{2,1,0:T(8,128)S(1)}, u32[]{:S(2)}, u32[]{:S(2)}) collective-permute-start(f32[8,64,128]{2,1,0:T(8,128)S(1)} %get-tuple-element.25), channel_id=1, source_target_pairs={{0,48},{16,0},{32,16},{48,32},{1,49},{17,1},{33,17},{49,33},{2,50}... | collective-permute-start | bytes 786440 | tf_op jit(solution)/shard_map/ppermute | solution.py:383
